TPU v7x, 32 devices: a whole 2x2x4 slice. The times are simulated.
32 devices in a mesh: frame: 8 (over z, x), head: 4 (over y, core).
Axes of the slice: x: 2, y: 2, z: 4, core: 2. Of those that a mesh axis runs over, the one named last changes fastest.
Arguments:
- latents: bfloat16 [64, 64, 1152], P('frame', None, 'head'), may hold values from -6 to 6
- fresh: bfloat16 [2, 64, 1152], P(None, None, 'head'), may hold values from -6 to 6
- noise_level: int32 [64], P('frame'), may hold values from 0 to 63
- window_mask: int32 [64, 17], P('frame'), may hold values from 0 to 1, as said below
- mod_table: float32 [64, 6, 1152], replicated, may hold values from -3 to 3
- keep_coef: float32 [64], replicated, may hold values from 0.3 to 1
- layer_coef: float32 [64], replicated, may hold values from 0.2 to 1
- w_qkv: bfloat16 [3, 1152, 1152], P(None, None, 'head')
- w_out: bfloat16 [1152, 1152], P('head'), may hold values from -0.1875 to 0.1875
- w_fc1: bfloat16 [1152, 4608], P(None, 'head'), may hold values from -0.1875 to 0.1875
- w_fc2: bfloat16 [4608, 1152], P('head'), may hold values from -0.09375 to 0.09375
Outputs:
- queue_out: bfloat16 [64, 64, 1152], P('frame', None, 'head')
Inputs may be any that keep to these rules, and one draw needn't show every extreme that they name: `window_mask`: column 8 (offset zero) is 1 in every row.
All inputs are finite; a program needn't handle non-finite values.
Results may differ from a plain program's by a relative error of at most 0.029.
Values may be sent and summed in bfloat16 or wider, within the bound.
No kernel may reach another device: no remote copies, remote signals or barrier semaphores. Data moves between devices by JAX's collectives and lax.ppermute only.
A program may use at most 64 MiB of HBM per device.

v0:
```python
import math

import jax
import jax.numpy as jnp
from jax import lax
from jax.sharding import PartitionSpec as P

HD = 72
W = 8


epsilon = 1e-06


def padded_2(array, sides, width):
    for axis, dim in sides:
        size, length = (lax.axis_size(axis), array.shape[dim])
        up = [(i, (i + 1) % size) for i in range(size - 1)]
        down = [(j, i) for i, j in up]
        last = lax.slice_in_dim(array, length - width, length, axis=dim)
        first = lax.slice_in_dim(array, 0, width, axis=dim)
        before = lax.ppermute(last, axis, up)
        after = lax.ppermute(first, axis, down)
        array = jnp.concatenate([before, array, after], axis=dim)
    return array


def shifted(value, axis, steps):
    count = lax.axis_size(axis)
    first, last = (max(0, -steps), min(count, count - steps))
    return lax.ppermute(value, axis, [(source, source + steps) for source in range(first, last)])


def modulate(values, shift_row, scale_row):
    center = values - jnp.mean(values, axis=-1, keepdims=True)
    spread_sq = jnp.mean(center * center, axis=-1, keepdims=True)
    return center * lax.rsqrt(spread_sq + epsilon) * (1.0 + scale_row) + shift_row


def window_attention(queries, padded, allowed):
    frame_count, token_count, feature_width = queries.shape
    head_count = feature_width // HD
    span = padded.shape[1]
    query_heads = queries.reshape(frame_count, token_count, head_count, HD)
    key_heads = padded[0].reshape(span, token_count, head_count, HD)
    value_heads = padded[1].reshape(span, token_count, head_count, HD)
    scaling = 1.0 / math.sqrt(HD)
    scores = (
        jnp.einsum("fphd,gphd->phfg", query_heads, key_heads, preferred_element_type=jnp.float32)
        * scaling
    )
    distance = (
        jnp.arange(span, dtype=jnp.int32)[None, :]
        - jnp.arange(frame_count, dtype=jnp.int32)[:, None]
    )
    offsets = jnp.arange(2 * W + 1, dtype=jnp.int32)
    band = jnp.any((distance[:, :, None] == offsets[None, None, :]) & allowed[:, None, :], axis=-1)
    open_mask = band[None, None, :, :]
    scores = jnp.where(open_mask, scores, -1e30)
    top_score = jnp.max(scores, axis=-1, keepdims=True)
    weights = jnp.where(open_mask, jnp.exp(scores - top_score), 0.0)
    probabilities = (weights / jnp.sum(weights, axis=-1, keepdims=True)).astype(jnp.bfloat16)
    mixed = jnp.einsum(
        "phfg,gphd->fphd", probabilities, value_heads, preferred_element_type=jnp.float32
    )
    return mixed.reshape(frame_count, token_count, feature_width).astype(jnp.bfloat16)


def attention_part(rows_bf, modulation, allowed, w_qkv, w_out):
    normed = modulate(
        rows_bf.astype(jnp.float32), modulation[:, None, 0], modulation[:, None, 1]
    ).astype(jnp.bfloat16)
    projected = jnp.einsum(
        "fpd,tde->tfpe", normed, w_qkv, preferred_element_type=jnp.float32
    ).astype(jnp.bfloat16)
    padded = padded_2(projected[1:], (("frame", 1),), W)
    attended = window_attention(projected[0], padded, allowed)
    return jnp.dot(attended, w_out, preferred_element_type=jnp.float32)


def feed_part(after_bf, modulation, w_fc1, w_fc2):
    normed_two = modulate(
        after_bf.astype(jnp.float32), modulation[:, None, 3], modulation[:, None, 4]
    ).astype(jnp.bfloat16)
    hidden = jax.nn.gelu(
        jnp.dot(normed_two, w_fc1, preferred_element_type=jnp.float32), approximate=True
    ).astype(jnp.bfloat16)
    return jnp.dot(hidden, w_fc2, preferred_element_type=jnp.float32)


def on_device(
    latents,
    fresh,
    noise_level,
    window_mask,
    mod_table,
    keep_coef,
    layer_coef,
    w_qkv,
    w_out,
    w_fc1,
    w_fc2,
):
    frames_here = latents.shape[0]
    share_width = latents.shape[2]
    level_count = mod_table.shape[0]
    head_index = lax.axis_index("head")
    frame_index = lax.axis_index("frame")
    total_frames = frames_here * lax.axis_size("frame")
    one_hot = (noise_level[:, None] == jnp.arange(level_count, dtype=jnp.int32)[None, :]).astype(
        jnp.float32
    )
    modulation = jnp.dot(
        one_hot, mod_table.reshape(level_count, -1), precision=lax.Precision.HIGHEST
    ).reshape(frames_here, 6, mod_table.shape[2])
    coef_pair = jnp.dot(
        one_hot, jnp.stack([keep_coef, layer_coef], 1), precision=lax.Precision.HIGHEST
    )
    keep_here = coef_pair[:, 0][:, None, None]
    layer_here = coef_pair[:, 1][:, None, None]
    positions = (
        frame_index * frames_here
        + jnp.arange(frames_here, dtype=jnp.int32)[:, None]
        + jnp.arange(2 * W + 1, dtype=jnp.int32)[None, :]
        - W
    )
    allowed = (window_mask == 1) & (positions >= 0) & (positions < total_frames)
    at_start = frame_index == 0
    current, fresh_rows = (
        lax.all_gather(latents, "head", axis=2, tiled=True),
        lax.all_gather(fresh, "head", axis=2, tiled=True),
    )
    for step_idx in range(2):
        incoming = shifted(current[-1:], "frame", 1)
        incoming = jnp.where(at_start, fresh_rows[step_idx : step_idx + 1], incoming)
        current = jnp.concatenate([incoming, current[:-1]], 0)
        attention_total = lax.psum(
            attention_part(current, modulation, allowed, w_qkv, w_out).astype(jnp.bfloat16), "head"
        ).astype(jnp.float32)
        current_wide = current.astype(jnp.float32)
        after_rows = (current_wide + modulation[:, None, 2] * attention_total).astype(jnp.bfloat16)
        feed_total = lax.psum(
            feed_part(after_rows, modulation, w_fc1, w_fc2).astype(jnp.bfloat16), "head"
        ).astype(jnp.float32)
        output_rows = after_rows.astype(jnp.float32) + modulation[:, None, 5] * feed_total
        current = (keep_here * current_wide + layer_here * output_rows).astype(jnp.bfloat16)
    return lax.dynamic_slice_in_dim(current, head_index * share_width, share_width, 2)


def solution(mesh):
    in_specs = (
        P("frame", None, "head"),
        P(None, None, "head"),
        P("frame"),
        P("frame", None),
        P(),
        P(),
        P(),
        P(None, None, "head"),
        P("head", None),
        P(None, "head"),
        P("head", None),
    )
    out_specs = P("frame", None, "head")
    return jax.shard_map(
        on_device, mesh=mesh, in_specs=in_specs, out_specs=out_specs, check_vma=False
    )
```

profile of v0, /device:TPU:0, one launch (start us, length us, event | category | flops | bytes accessed | tf_op | source)
XLA Modules:
  0.0 384.6 jit_solution(5901057133440401703)
XLA Ops:
  10.0 9.0 %all_gather.6 = bf16[2,64,1152]{1,0,2:T(2,128)(2,1)S(1)} all-gather(bf16[2,64,288]{1,0,2:T(2,128)(2,1)S(1)} %copy.44), channel_id=1, replica_groups=mesh['frame'=8,'head'=4] {'head'}, dimensions={2}, use_global_device_ids=true | all-gather | bytes 368640 | tf_op jit(solution)/shard_map/all_gather | solution.py:131
  22.2 13.6 %all-gather.2.cloned.1.call-done = bf16[8,64,1152]{1,0,2:T(8,128)(2,1)} async-done(((bf16[8,64,288]{1,0,2:T(8,128)(2,1)}), bf16[8,64,1152]{1,0,2:T(8,128)(2,1)}) %all-gather.2.cloned.1.call-update) | async-done | bytes 1179664 | tf_op jit(solution)/shard_map/all_gather | solution.py:130
  35.8 2.6 slice.96
  39.8 4.0 %collective-permute-start = (bf16[1,64,1152]{2,1,0:T(8,128)(2,1)S(1)}, bf16[1,64,1152]{2,1,0:T(8,128)(2,1)}, u32[]{:S(2)}, u32[]{:S(2)}) collective-permute-start(bf16[1,64,1152]{2,1,0:T(8,128)(2,1)S(1)} %copy.65), channel_id=1, source_target_pairs={{0,4},{4,8},{8,12},{12,16},{16,20},{20,24},{24,28},{1,5},{5,9},{9,... | collective-permute-start | bytes 442376 | tf_op jit(solution)/shard_map/ppermute | solution.py:31
  46.9 3.9 %copy.66 = bf16[7,64,1152]{2,1,0:T(8,128)(2,1)} copy(bf16[7,64,1152]{1,0,2:T(8,128)(2,1)} %bitcast.121) | data formatting | bytes 2064384
  54.1 3.6 fusion.74
  61.0 5.4 %collective-permute-start.1 = (bf16[2,8,64,288]{3,2,0,1:T(8,128)(2,1)}, bf16[2,8,64,288]{3,2,0,1:T(8,128)(2,1)}, u32[]{:S(2)}, u32[]{:S(2)}) collective-permute-start(bf16[2,8,64,288]{3,2,0,1:T(8,128)(2,1)} %slice.101), channel_id=1, source_target_pairs={{0,4},{4,8},{8,12},{12,16},{16,20},{20,24},{24,28},{1,5},{5,9},{9,... | collective-permute-start | bytes 1769480 | tf_op jit(solution)/shard_map/ppermute | solution.py:22
  68.9 12.5 %collective-permute-done.2 = bf16[2,8,64,288]{3,2,0,1:T(8,128)(2,1)} collective-permute-done((bf16[2,8,64,288]{3,2,0,1:T(8,128)(2,1)}, bf16[2,8,64,288]{3,2,0,1:T(8,128)(2,1)}, u32[]{:S(2)}, u32[]{:S(2)}) %collective-permute-start.2) | collective-permute-done | bytes 589856 | tf_op jit(solution)/shard_map/ppermute | solution.py:23
  81.4 17.0 %collective-permute-done.1 = bf16[2,8,64,288]{3,2,0,1:T(8,128)(2,1)} collective-permute-done((bf16[2,8,64,288]{3,2,0,1:T(8,128)(2,1)}, bf16[2,8,64,288]{3,2,0,1:T(8,128)(2,1)}, u32[]{:S(2)}, u32[]{:S(2)}) %collective-permute-start.1) | collective-permute-done | bytes 589856 | tf_op jit(solution)/shard_map/ppermute | solution.py:22
  102.2 4.3 %reshape_squeeze.20 = bf16[24,64,4,72]{3,2,1,0:T(4,128)(2,1)} reshape(bf16[1,24,64,288]{3,2,0,1:T(8,128)(2,1)} %get-tuple-element.11) | data formatting | bytes 1769472 | tf_op jit(solution)/shard_map/reshape;squeeze | solution.py:45
  106.5 4.2 %reshape_squeeze.18 = bf16[24,64,4,72]{3,2,1,0:T(4,128)(2,1)} reshape(bf16[1,24,64,288]{3,2,0,1:T(8,128)(2,1)} %get-tuple-element.12) | data formatting | bytes 1769472 | tf_op jit(solution)/shard_map/reshape;squeeze | solution.py:46
  110.7 4.7 %fusion.169 = (f32[64,4,8]{2,1,0:T(4,128)}, f32[64,4,8,24]{3,2,1,0:T(8,128)}) fusion(pred[8,24]{1,0:T(8,128)(4,1)S(1)} %fusion.142, bf16[24,64,4,72]{3,2,1,0:T(4,128)(2,1)} %reshape_squeeze.20, bf16[8,64,4,72]{3,2,1,0:T(4,128)(2,1)S(1)} %copy-done.9), kind=kOutput, calls=%fused_computation.179 | convolution fusion | flops 7323671 | bytes 1384640 | tf_op jit(solution)/shard_map/sub | solution.py:61
  115.4 2.9 fusion.102
  121.5 2.8 convolution_convert_fusion.3
  124.4 37.5 %all-reduce.5.cloned.1.call-done = bf16[8,64,1152]{2,1,0:T(8,128)(2,1)} async-done(((bf16[8,64,1152]{2,1,0:T(8,128)(2,1)}), bf16[8,64,1152]{2,1,0:T(8,128)(2,1)}) %all-reduce.5.cloned.1.call-update) | async-done | bytes 1179664 | tf_op jit(solution)/shard_map/psum | solution.py:137
  165.5 6.7 %convolution_convert_fusion.2 = bf16[8,64,1152]{2,1,0:T(8,128)(2,1)} fusion(bf16[1152,1152]{1,0:T(8,128)(2,1)S(1)} %copy-done, bf16[1152,1152]{1,0:T(8,128)(2,1)} %param.20, bf16[8,64,1152]{2,1,0:T(8,128)(2,1)} %copy-done.5, f32[8,1152]{1,0:T(8,128)} %get-tuple-element.16, f32[8,1152]{1,0:T(8,128)} %get-tuple-element.17, f32[8,64]{1,0:T(8,128)S(1)} %add_rsqrt_fusion.2, ...), kind=kOutput, calls=%fused_computation.13 | convolution fusion | flops 2727346176 | bytes 7745536 | tf_op jit(solution)/shard_map/dot_general | solution.py:88
  173.4 36.5 %all-reduce.7.cloned.1.call-done = bf16[8,64,1152]{2,1,0:T(8,128)(2,1)} async-done(((bf16[8,64,1152]{2,1,0:T(8,128)(2,1)}), bf16[8,64,1152]{2,1,0:T(8,128)(2,1)}) %all-reduce.7.cloned.1.call-update) | async-done | bytes 1179664 | tf_op jit(solution)/shard_map/psum | solution.py:142
  209.9 2.6 fusion.22
  213.6 4.0 %collective-permute-start.3 = (bf16[1,64,1152]{2,1,0:T(8,128)(2,1)S(1)}, bf16[1,64,1152]{2,1,0:T(8,128)(2,1)}, u32[]{:S(2)}, u32[]{:S(2)}) collective-permute-start(bf16[1,64,1152]{2,1,0:T(8,128)(2,1)S(1)} %slice.108), channel_id=1, source_target_pairs={{0,4},{4,8},{8,12},{12,16},{16,20},{20,24},{24,28},{1,5},{5,9},{9,... | collective-permute-start | bytes 442376 | tf_op jit(solution)/shard_map/ppermute | solution.py:31
  227.1 5.4 %collective-permute-start.4 = (bf16[2,8,64,288]{3,2,0,1:T(8,128)(2,1)}, bf16[2,8,64,288]{3,2,0,1:T(8,128)(2,1)}, u32[]{:S(2)}, u32[]{:S(2)}) collective-permute-start(bf16[2,8,64,288]{3,2,0,1:T(8,128)(2,1)} %slice.110), channel_id=1, source_target_pairs={{0,4},{4,8},{8,12},{12,16},{16,20},{20,24},{24,28},{1,5},{5,9},{9,... | collective-permute-start | bytes 1769480 | tf_op jit(solution)/shard_map/ppermute | solution.py:22
  235.5 11.3 %collective-permute-done.5 = bf16[2,8,64,288]{3,2,0,1:T(8,128)(2,1)} collective-permute-done((bf16[2,8,64,288]{3,2,0,1:T(8,128)(2,1)}, bf16[2,8,64,288]{3,2,0,1:T(8,128)(2,1)}, u32[]{:S(2)}, u32[]{:S(2)}) %collective-permute-start.5) | collective-permute-done | bytes 589856 | tf_op jit(solution)/shard_map/ppermute | solution.py:23
  246.8 16.1 %collective-permute-done.4 = bf16[2,8,64,288]{3,2,0,1:T(8,128)(2,1)} collective-permute-done((bf16[2,8,64,288]{3,2,0,1:T(8,128)(2,1)}, bf16[2,8,64,288]{3,2,0,1:T(8,128)(2,1)}, u32[]{:S(2)}, u32[]{:S(2)}) %collective-permute-start.4) | collective-permute-done | bytes 589856 | tf_op jit(solution)/shard_map/ppermute | solution.py:22
  266.8 4.2 %reshape_squeeze.23 = bf16[24,64,4,72]{3,2,1,0:T(4,128)(2,1)} reshape(bf16[1,24,64,288]{3,2,0,1:T(8,128)(2,1)} %get-tuple-element.9) | data formatting | bytes 1769472 | tf_op jit(solution)/shard_map/reshape;squeeze | solution.py:45
  271.0 4.2 %reshape_squeeze.21 = bf16[24,64,4,72]{3,2,1,0:T(4,128)(2,1)} reshape(bf16[1,24,64,288]{3,2,0,1:T(8,128)(2,1)} %get-tuple-element.10) | data formatting | bytes 1769472 | tf_op jit(solution)/shard_map/reshape;squeeze | solution.py:46
  275.2 4.9 %fusion.170 = (f32[64,4,8]{2,1,0:T(4,128)}, f32[64,4,8,24]{3,2,1,0:T(8,128)}) fusion(pred[8,24]{1,0:T(8,128)(4,1)S(1)} %fusion.142, bf16[24,64,4,72]{3,2,1,0:T(4,128)(2,1)} %reshape_squeeze.23, bf16[8,64,4,72]{3,2,1,0:T(4,128)(2,1)} %reshape_squeeze.22), kind=kOutput, calls=%fused_computation.180 | convolution fusion | flops 7323671 | bytes 1384640 | tf_op jit(solution)/shard_map/sub | solution.py:61
  280.1 2.8 fusion.99
  286.2 2.8 convolution_convert_fusion.1
  289.4 37.8 %all-reduce.9.cloned.1.call-done = bf16[8,64,1152]{2,1,0:T(8,128)(2,1)} async-done(((bf16[8,64,1152]{2,1,0:T(8,128)(2,1)}), bf16[8,64,1152]{2,1,0:T(8,128)(2,1)}) %all-reduce.9.cloned.1.call-update) | async-done | bytes 1179664 | tf_op jit(solution)/shard_map/psum | solution.py:137
  330.8 6.7 %convolution_convert_fusion = bf16[8,64,1152]{2,1,0:T(8,128)(2,1)} fusion(bf16[1152,1152]{1,0:T(8,128)(2,1)S(1)} %copy-done, bf16[1152,1152]{1,0:T(8,128)(2,1)} %param.20, bf16[8,64,1152]{2,1,0:T(8,128)(2,1)} %copy-done.3, f32[8,64]{1,0:T(8,128)S(1)} %add_rsqrt_fusion, f32[8,64]{1,0:T(8,128)S(1)} %broadcast_multiply_fusion, f32[8,1152]{1,0:T(8,128)S(1)} %copy-done.10, ...), kind=kOutput, calls=%fused_computation.11 | convolution fusion | flops 2727346176 | bytes 7745536 | tf_op jit(solution)/shard_map/dot_general | solution.py:88
  337.6 2.9 fusion.164
  342.0 33.0 %all-reduce.11.cloned.1.call-done = bf16[8,64,1152]{2,1,0:T(8,128)(2,1)} async-done(((bf16[8,64,1152]{2,1,0:T(8,128)(2,1)}), bf16[8,64,1152]{2,1,0:T(8,128)(2,1)}) %all-reduce.11.cloned.1.call-update) | async-done | bytes 1179664 | tf_op jit(solution)/shard_map/psum | solution.py:142
  375.1 3.0 fusion.133
  (104 shorter events, 57.8 us)
Async XLA Ops:
  6.5 158.9 %copy-start = (bf16[1152,1152]{1,0:T(8,128)(2,1)S(1)}, bf16[1152,1152]{1,0:T(8,128)(2,1)}, u32[]{:S(2)}) copy-start(bf16[1152,1152]{1,0:T(8,128)(2,1)} %param.21) | copy-start | bytes 7962628
  6.5 12.5 %copy-start.17 = (s32[8]{0:T(128)S(1)}, s32[8]{0:T(128)}, u32[]{:S(2)}) copy-start(s32[8]{0:T(128)} %param.13) | copy-start | bytes 100
  6.5 29.3 %all-gather.2.cloned.1.call-start = ((), (), s32[]{:S(2)}) async-start(), calls=%async_computation | async-start | bytes 2949120 | tf_op jit(solution)/shard_map/all_gather | solution.py:130
  8.9 153.0 %all-reduce.5.cloned.1.call-start = ((), (), s32[]{:S(2)}) async-start(), calls=%async_computation.1 | async-start | bytes 2359296 | tf_op jit(solution)/shard_map/psum | solution.py:137
  22.2 31.9 %copy-start.12 = (f32[8,1152]{1,0:T(8,128)}, f32[8,1152]{1,0:T(8,128)S(1)}, u32[]{:S(2)}) copy-start(f32[8,1152]{1,0:T(8,128)S(1)} %get-tuple-element.18) | copy-start | bytes 110596
  22.2 31.9 %copy-start.14 = (f32[8,1152]{1,0:T(8,128)}, f32[8,1152]{1,0:T(8,128)S(1)}, u32[]{:S(2)}) copy-start(f32[8,1152]{1,0:T(8,128)S(1)} %get-tuple-element.19) | copy-start | bytes 110596
  39.8 11.0 %collective-permute-start = (bf16[1,64,1152]{2,1,0:T(8,128)(2,1)S(1)}, bf16[1,64,1152]{2,1,0:T(8,128)(2,1)}, u32[]{:S(2)}, u32[]{:S(2)}) collective-permute-start(bf16[1,64,1152]{2,1,0:T(8,128)(2,1)S(1)} %copy.65), channel_id=1, source_target_pairs={{0,4},{4,8},{8,12},{12,16},{16,20},{20,24},{24,28},{1,5},{5,9},{9,... | collective-permute-start | bytes 442376 | tf_op jit(solution)/shard_map/ppermute | solution.py:31
  50.8 3.3 copy-start.1
  54.1 12.4 %copy-start.16 = (s32[8,17]{1,0:T(8,128)S(1)}, s32[8,17]{1,0:T(8,128)}, u32[]{:S(2)}) copy-start(s32[8,17]{1,0:T(8,128)} %param.14) | copy-start | bytes 1636
  57.7 1.1 copy-start.8
  59.8 21.6 %collective-permute-start.2 = (bf16[2,8,64,288]{3,2,0,1:T(8,128)(2,1)}, bf16[2,8,64,288]{3,2,0,1:T(8,128)(2,1)}, u32[]{:S(2)}, u32[]{:S(2)}) collective-permute-start(bf16[2,8,64,288]{3,2,0,1:T(8,128)(2,1)} %slice.101), channel_id=1, source_target_pairs={{4,0},{8,4},{12,8},{16,12},{20,16},{24,20},{28,24},{5,1},{9,5},{13... | collective-permute-start | bytes 1769480 | tf_op jit(solution)/shard_map/ppermute | solution.py:23
  61.0 37.4 %collective-permute-start.1 = (bf16[2,8,64,288]{3,2,0,1:T(8,128)(2,1)}, bf16[2,8,64,288]{3,2,0,1:T(8,128)(2,1)}, u32[]{:S(2)}, u32[]{:S(2)}) collective-permute-start(bf16[2,8,64,288]{3,2,0,1:T(8,128)(2,1)} %slice.101), channel_id=1, source_target_pairs={{0,4},{4,8},{8,12},{12,16},{16,20},{20,24},{24,28},{1,5},{5,9},{9,... | collective-permute-start | bytes 1769480 | tf_op jit(solution)/shard_map/ppermute | solution.py:22
  102.2 8.5 %copy-start.9 = (bf16[8,64,4,72]{3,2,1,0:T(4,128)(2,1)S(1)}, bf16[8,64,4,72]{3,2,1,0:T(4,128)(2,1)}, u32[]{:S(2)}) copy-start(bf16[8,64,4,72]{3,2,1,0:T(4,128)(2,1)} %reshape_squeeze.19) | copy-start | bytes 884740
  115.4 6.1 %copy-start.7 = (bf16[288,1152]{1,0:T(8,128)(2,1)S(1)}, bf16[288,1152]{1,0:T(8,128)(2,1)}, u32[]{:S(2)}) copy-start(bf16[288,1152]{1,0:T(8,128)(2,1)} %param.19) | copy-start | bytes 1990660
  124.4 85.5 %all-reduce.7.cloned.1.call-start = ((), (), s32[]{:S(2)}) async-start(), calls=%async_computation.2 | async-start | bytes 2359296 | tf_op jit(solution)/shard_map/psum | solution.py:142
  164.0 1.0 copy-start.5
  172.2 154.9 %all-reduce.9.cloned.1.call-start = ((), (), s32[]{:S(2)}) async-start(), calls=%async_computation.3 | async-start | bytes 2359296 | tf_op jit(solution)/shard_map/psum | solution.py:137
  212.5 1.0 copy-start.6
  213.6 7.4 %collective-permute-start.3 = (bf16[1,64,1152]{2,1,0:T(8,128)(2,1)S(1)}, bf16[1,64,1152]{2,1,0:T(8,128)(2,1)}, u32[]{:S(2)}, u32[]{:S(2)}) collective-permute-start(bf16[1,64,1152]{2,1,0:T(8,128)(2,1)S(1)} %slice.108), channel_id=1, source_target_pairs={{0,4},{4,8},{8,12},{12,16},{16,20},{20,24},{24,28},{1,5},{5,9},{9,... | collective-permute-start | bytes 442376 | tf_op jit(solution)/shard_map/ppermute | solution.py:31
  219.5 3.3 copy-start.13
  219.5 3.3 copy-start.15
  219.5 3.3 copy-start.18
  221.0 4.9 %copy-start.2 = (bf16[7,64,1152]{2,1,0:T(8,128)(2,1)}, bf16[7,64,1152]{2,1,0:T(8,128)(2,1)S(1)}, u32[]{:S(2)}) copy-start(bf16[7,64,1152]{2,1,0:T(8,128)(2,1)S(1)} %slice.109) | copy-start | bytes 3096580
  225.8 21.0 %collective-permute-start.5 = (bf16[2,8,64,288]{3,2,0,1:T(8,128)(2,1)}, bf16[2,8,64,288]{3,2,0,1:T(8,128)(2,1)}, u32[]{:S(2)}, u32[]{:S(2)}) collective-permute-start(bf16[2,8,64,288]{3,2,0,1:T(8,128)(2,1)} %slice.110), channel_id=1, source_target_pairs={{4,0},{8,4},{12,8},{16,12},{20,16},{24,20},{28,24},{5,1},{9,5},{13... | collective-permute-start | bytes 1769480 | tf_op jit(solution)/shard_map/ppermute | solution.py:23
  227.1 35.8 %collective-permute-start.4 = (bf16[2,8,64,288]{3,2,0,1:T(8,128)(2,1)}, bf16[2,8,64,288]{3,2,0,1:T(8,128)(2,1)}, u32[]{:S(2)}, u32[]{:S(2)}) collective-permute-start(bf16[2,8,64,288]{3,2,0,1:T(8,128)(2,1)} %slice.110), channel_id=1, source_target_pairs={{0,4},{4,8},{8,12},{12,16},{16,20},{20,24},{24,28},{1,5},{5,9},{9,... | collective-permute-start | bytes 1769480 | tf_op jit(solution)/shard_map/ppermute | solution.py:22
  289.1 41.7 %copy-start.10 = (f32[8,1152]{1,0:T(8,128)S(1)}, f32[8,1152]{1,0:T(8,128)}, u32[]{:S(2)}) copy-start(f32[8,1152]{1,0:T(8,128)} %get-tuple-element.16) | copy-start | bytes 110596
  289.1 41.7 %copy-start.11 = (f32[8,1152]{1,0:T(8,128)S(1)}, f32[8,1152]{1,0:T(8,128)}, u32[]{:S(2)}) copy-start(f32[8,1152]{1,0:T(8,128)} %get-tuple-element.17) | copy-start | bytes 110596
  289.1 86.0 %all-reduce.11.cloned.1.call-start = ((), (), s32[]{:S(2)}) async-start(), calls=%async_computation.4 | async-start | bytes 2359296 | tf_op jit(solution)/shard_map/psum | solution.py:142
  329.2 1.1 copy-start.3
  337.5 3.0 copy-start.4
Sparse Core Ops, SparseCore 0:
  9.0 26.7 all-gather.1
  124.5 37.3 all-reduce.4
  172.3 37.5 all-reduce.6
  289.2 37.9 all-reduce.8
  337.6 37.4 all-reduce.10
where the time goes:
time: 386 us; the launch traced here: 385 us
  waiting for transfers between devices  215 us (56%)
  local copies, waits for them, and re-layouts  56 us (15%)
  matrix products  43.4 us (11%)
  other arithmetic  25.1 us (7%)
  starting transfers between devices  22.2 us (6%)
  between operations  13.5 us (3%)
  blocking collectives  9 us (2%)
    psum x2, waiting for transfers between devices, on_device(): lax.psum(attention_part(current, modulation, allowed, w_qkv, w_out).astyp...  75.2 us
    psum x2, waiting for transfers between devices, on_device(): lax.psum(feed_part(after_rows, modulation, w_fc1, w_fc2).astype(jnp.bfloa...  69.6 us
    ppermute x2, waiting for transfers between devices, padded_2(): before = lax.ppermute(last, axis, up)  33.1 us
    ppermute x2, waiting for transfers between devices, padded_2(): after = lax.ppermute(first, axis, down)  23.8 us
    unnamed x44, local copies, waits for them, and re-layouts  16.1 us
    all_gather x1, waiting for transfers between devices, on_device(): lax.all_gather(latents, 'head', axis=2, tiled=True)  13.6 us
    dot_general x2, matrix products, feed_part(): return jnp.dot(hidden, w_fc2, preferred_element_type=jnp.float32)  13.4 us
    ppermute x2, starting transfers between devices, padded_2(): before = lax.ppermute(last, axis, up)  10.9 us
  transfers between devices with their start and end apart: 11, of which 9 were waited for; matrix products, arithmetic and copies ran while one was open for 7% of the time, Pallas kernels for 0%

commit v1 on v0

v1 whole, which is shorter than its diff:
```python
import functools
import math

import jax
import jax.numpy as jnp
from jax import lax
from jax.experimental import pallas as pl
from jax.experimental.pallas import tpu as pltpu
from jax.sharding import Mesh, PartitionSpec as P

HD = 72
W = 8
OFFSETS = 2 * W + 1
EPSILON = 1e-06
F32 = jnp.float32
BF16 = jnp.bfloat16
LANES = 128
VMEM_LIMIT = 56 * 1024 * 1024

VMEM_SPEC = pl.BlockSpec(memory_space=pltpu.VMEM)
SMEM_SPEC = pl.BlockSpec(memory_space=pltpu.SMEM)
ANY_SPEC = pl.BlockSpec(memory_space=pl.ANY)


def params():
    return pltpu.CompilerParams(vmem_limit_bytes=VMEM_LIMIT)


def padded_width(width):
    return -(-(width + 1 + OFFSETS) // LANES) * LANES


def normalise(values, shift_rows, scale_rows):
    center = values - jnp.mean(values, axis=-1, keepdims=True)
    spread = jnp.mean(center * center, axis=-1, keepdims=True)
    return center * lax.rsqrt(spread + EPSILON) * (1.0 + scale_rows) + shift_rows


def payload_kernel(x_ref, meta_ref, out_ref, rows_ref):
    frames, tokens, width = x_ref.shape
    wide = out_ref.shape[1]
    meta = meta_ref[...].astype(F32)
    for i in range(frames):
        tail = jnp.broadcast_to(meta[i : i + 1, :], (tokens, wide - width))
        row = jnp.concatenate([x_ref[i].astype(F32), tail], axis=1)
        for lane in range(0, wide, LANES):
            rows_ref[lane // LANES, pl.ds(i, tokens, stride=frames), :] = row[:, lane : lane + LANES]
    for lane in range(0, wide, LANES):
        out_ref[:, lane : lane + LANES] = rows_ref[lane // LANES].astype(BF16)


def make_payload(x, meta):
    frames, tokens, width = x.shape
    wide = padded_width(width)
    meta = jnp.pad(meta, ((0, 0), (0, wide - width - meta.shape[1])))
    return pl.pallas_call(
        payload_kernel,
        out_shape=jax.ShapeDtypeStruct((tokens * frames, wide), BF16),
        in_specs=[VMEM_SPEC, VMEM_SPEC],
        out_specs=VMEM_SPEC,
        scratch_shapes=[pltpu.VMEM((wide // LANES, tokens * frames, LANES), F32)],
        compiler_params=params(),
        name="payload",
    )(x, meta)


def prepare_kernel(width, meta_ref, table_ref, coef_ref, mod_ref, pair_ref, mask_ref):
    groups, here, wide = meta_ref.shape
    frames = groups * here
    levels = table_ref.shape[0]
    meta = meta_ref[...].astype(F32).reshape(frames, wide)
    level = meta[:, 0:1]
    ids = lax.broadcasted_iota(jnp.int32, (frames, levels), 1).astype(F32)
    hot = level == ids
    hot_bf = hot.astype(BF16)
    features = mod_ref.shape[2]
    for j in range(mod_ref.shape[0]):
        rows = table_ref[:, j * features : (j + 1) * features]
        high = rows.astype(BF16)
        rest = rows - high.astype(F32)
        middle = rest.astype(BF16)
        low = (rest - middle.astype(F32)).astype(BF16)
        total = jnp.dot(hot_bf, high, preferred_element_type=F32)
        total += jnp.dot(hot_bf, middle, preferred_element_type=F32)
        total += jnp.dot(hot_bf, low, preferred_element_type=F32)
        mod_ref[j] = total
    keep = jnp.sum(jnp.where(hot, coef_ref[0:1, :], 0.0), axis=1, keepdims=True)
    layer = jnp.sum(jnp.where(hot, coef_ref[1:2, :], 0.0), axis=1, keepdims=True)
    lane = lax.broadcasted_iota(jnp.int32, (frames, LANES), 1)
    pair_ref[...] = jnp.where(lane == 0, keep, layer)

    block = mask_ref.shape[0]
    repeat = block // frames
    row = lax.broadcasted_iota(jnp.int32, (frames, block), 0)
    column = lax.broadcasted_iota(jnp.int32, (frames, block), 1)
    for t in range(repeat):
        distance = column - t * frames - row
        inside = (column >= t * frames) & (column < (t + 1) * frames)
        is_open = jnp.zeros((frames, block), F32)
        for o in range(OFFSETS):
            is_open = jnp.where(distance == o - W, meta[:, 1 + o : 2 + o], is_open)
        mask_ref[t * frames : (t + 1) * frames, :] = jnp.where(inside, is_open, 0.0)


def prepare(meta, table, coefs, block):
    groups, here, _ = meta.shape
    frames = groups * here
    levels, kinds, features = table.shape
    return pl.pallas_call(
        functools.partial(prepare_kernel, features),
        out_shape=(
            jax.ShapeDtypeStruct((kinds, frames, features), F32),
            jax.ShapeDtypeStruct((frames, LANES), F32),
            jax.ShapeDtypeStruct((block, block), F32),
        ),
        in_specs=[VMEM_SPEC] * 3,
        out_specs=(VMEM_SPEC,) * 3,
        compiler_params=params(),
        name="prepare",
    )(meta, table.reshape(levels, kinds * features), coefs)


def start_copies(sources, targets, sems):
    copies = []
    for n, (source, target) in enumerate(zip(sources, targets)):
        copy = pltpu.make_async_copy(source, target, sems.at[n])
        copy.start()
        copies.append(copy)
    return copies


def attend(q, k, v, is_open):
    rows, share = q.shape
    heads = share // HD
    lane = lax.broadcasted_iota(jnp.int32, (1, share), 1)
    scaling = 1.0 / math.sqrt(HD)
    pieces = {}
    for h in range(heads):
        low = HD * h // LANES * LANES
        high = min(share, -(-HD * (h + 1) // LANES) * LANES)
        mine = (lane[:, low:high] >= HD * h) & (lane[:, low:high] < HD * (h + 1))
        qh = jnp.where(mine, q[:, low:high].astype(F32), 0.0).astype(BF16)
        scores = lax.dot_general(
            qh, k[:, low:high], (((1,), (1,)), ((), ())), preferred_element_type=F32
        )
        scores = jnp.where(is_open, scores * scaling, -1e30)
        top = jnp.max(scores, axis=-1, keepdims=True)
        weights = jnp.exp(scores - top)
        probabilities = (weights / jnp.sum(weights, axis=-1, keepdims=True)).astype(BF16)
        mixed = jnp.dot(probabilities, v[:, low:high], preferred_element_type=F32)
        mixed = jnp.where(mine, mixed, 0.0)
        for start in range(low, high, LANES):
            stop = min(start + LANES, high)
            part = mixed[:, start - low : stop - low]
            pieces[start] = part if start not in pieces else pieces[start] + part
    return jnp.concatenate([pieces[s] for s in sorted(pieces)], axis=1).astype(BF16)


def attention_rows(current, mod_ref, mask_ref, copies, weights, tokens, out_ref, normed_ref):
    for p, rows in enumerate(current):
        frames = rows.shape[0]
        normed_ref[p * frames : (p + 1) * frames, :] = normalise(
            rows, mod_ref[0], mod_ref[1]
        ).astype(BF16)
    qkv_me, qkv_other, out_me, out_other = weights
    rows_total = normed_ref.shape[0]
    block = mask_ref.shape[0]
    is_open = mask_ref[...] > 0.5
    normed = normed_ref[...]
    total = None
    for side, (qkv, w_out) in enumerate(((qkv_me, out_me), (qkv_other, out_other))):
        copies[2 * side].wait()
        q, k, v = (
            jnp.dot(normed, qkv[t], preferred_element_type=F32).astype(BF16) for t in range(3)
        )
        mixed = [
            attend(q[b : b + block], k[b : b + block], v[b : b + block], is_open)
            for b in range(0, rows_total, block)
        ]
        attended = mixed[0] if len(mixed) == 1 else jnp.concatenate(mixed, axis=0)
        copies[2 * side + 1].wait()
        part = jnp.dot(attended, w_out[...], preferred_element_type=F32)
        total = part if total is None else total + part
    out_ref[...] = total.astype(BF16)


def shifted_in(rows, fresh_row):
    frames = rows.shape[0]
    first = lax.broadcasted_iota(jnp.int32, (frames, 1), 0) == 0
    return jnp.where(first, fresh_row, pltpu.roll(rows, 1, 0))


def fresh_rows(place_ref, fresh_refs, step, tokens, split):
    me = place_ref[0]
    core = lax.rem(me, 2)
    own = []
    for ref in fresh_refs:
        value = ref[step].astype(F32)
        if split:
            value = jnp.where(core == 0, value[:tokens], value[tokens:])
        own.append(value)
    ordered = []
    for h in range(len(own)):
        pick = own[h]
        for d in range(len(own)):
            pick = jnp.where(lax.bitwise_xor(me, d) == h, own[d], pick)
        ordered.append(pick)
    return jnp.concatenate(ordered, axis=1)


def first_attention_kernel(
    split, place_ref, mine_ref, other_ref, f0, f1, f2, f3, mod_ref, mask_ref,
    qkv_me, qkv_other, out_me, out_other,
    cur_ref, part_ref, vq_me, vo_me, vq_other, vo_other, normed_ref, sems,
):
    copies = start_copies(
        (qkv_me, out_me, qkv_other, out_other), (vq_me, vo_me, vq_other, vo_other), sems
    )
    groups, cores, rows_here, _ = mine_ref.shape
    features = cur_ref.shape[1]
    frames = mod_ref.shape[1]
    here = frames // groups
    tokens = rows_here // here
    share = qkv_me.shape[2]
    fresh = fresh_rows(place_ref, (f0, f1, f2, f3), 0, tokens, split)
    first_half = place_ref[0] < 2
    blocks = []
    for g in range(groups):
        mine = [mine_ref[g, c].astype(F32)[:, :share] for c in range(cores)]
        other = [other_ref[g, c].astype(F32)[:, :share] for c in range(cores)]
        left = [jnp.where(first_half, a, b) for a, b in zip(mine, other)]
        right = [jnp.where(first_half, b, a) for a, b in zip(mine, other)]
        blocks.append(jnp.concatenate(left + right, axis=1))
    current = []
    for p in range(tokens):
        rows = jnp.concatenate([b[p * here : (p + 1) * here] for b in blocks], axis=0)
        rows = shifted_in(rows, fresh[p : p + 1])
        cur_ref[p * frames : (p + 1) * frames, :] = rows.astype(BF16)
        current.append(rows)
    attention_rows(
        current, mod_ref, mask_ref, copies, (vq_me, vq_other, vo_me, vo_other), tokens,
        part_ref, normed_ref,
    )


def next_attention_kernel(
    split, place_ref, old_ref, after_ref, mine_ref, other_ref, f0, f1, f2, f3, mod_ref, pair_ref,
    mask_ref, qkv_me, qkv_other, out_me, out_other,
    cur_ref, part_ref, vq_me, vo_me, vq_other, vo_other, normed_ref, sems,
):
    copies = start_copies(
        (qkv_me, out_me, qkv_other, out_other), (vq_me, vo_me, vq_other, vo_other), sems
    )
    frames = mod_ref.shape[1]
    tokens = old_ref.shape[0] // frames
    fresh = fresh_rows(place_ref, (f0, f1, f2, f3), 1, tokens, split)
    keep, layer = pair_ref[:, 0:1], pair_ref[:, 1:2]
    current = []
    for p in range(tokens):
        at = slice(p * frames, (p + 1) * frames)
        total = mine_ref[at, :].astype(F32) + other_ref[at, :].astype(F32)
        rows = keep * old_ref[at, :].astype(F32) + layer * (
            after_ref[at, :].astype(F32) + mod_ref[5] * total
        )
        rows = shifted_in(rows, fresh[p : p + 1]).astype(BF16)
        cur_ref[at, :] = rows
        current.append(rows.astype(F32))
    attention_rows(
        current, mod_ref, mask_ref, copies, (vq_me, vq_other, vo_me, vo_other), tokens,
        part_ref, normed_ref,
    )


def attention_call(kernel, vmem_args, weights, rows, features):
    qkv, w_out = weights[0], weights[2]
    return pl.pallas_call(
        kernel,
        out_shape=(jax.ShapeDtypeStruct((rows, features), BF16),) * 2,
        in_specs=[SMEM_SPEC] + [VMEM_SPEC] * (len(vmem_args) - 1) + [ANY_SPEC] * 4,
        out_specs=(VMEM_SPEC,) * 2,
        scratch_shapes=[
            pltpu.VMEM(qkv.shape, BF16),
            pltpu.VMEM(w_out.shape, BF16),
            pltpu.VMEM(qkv.shape, BF16),
            pltpu.VMEM(w_out.shape, BF16),
            pltpu.VMEM((rows, features), BF16),
            pltpu.SemaphoreType.DMA((4,)),
        ],
        compiler_params=params(),
        name="attention",
    )(*vmem_args, *weights)


def gelu(x):
    inner = math.sqrt(2.0 / math.pi) * (x + 0.044715 * (x * x * x))
    return x * (0.5 * (1.0 + jnp.tanh(inner)))


def pieces_of(width, size):
    return [(s, min(size, width - s)) for s in range(0, width, size)]


def feed_kernel(
    halves, place_ref, cur_ref, mine_ref, other_ref, mod_ref,
    fc1_me, fc1_other, fc2_me, fc2_other, *rest,
):
    outs, scratch = rest[: 3 if halves else 2], rest[3 if halves else 2 :]
    after_ref = outs[0]
    v1_me, v1_other, v2_me, v2_other, normed_ref, hidden_ref, sems = scratch
    copies = start_copies(
        (fc1_me, fc1_other, fc2_me, fc2_other), (v1_me, v1_other, v2_me, v2_other), sems
    )
    frames = mod_ref.shape[1]
    tokens = cur_ref.shape[0] // frames
    for p in range(tokens):
        at = slice(p * frames, (p + 1) * frames)
        total = mine_ref[at, :].astype(F32) + other_ref[at, :].astype(F32)
        after = (cur_ref[at, :].astype(F32) + mod_ref[2] * total).astype(BF16)
        after_ref[at, :] = after
        normed_ref[at, :] = normalise(after.astype(F32), mod_ref[3], mod_ref[4]).astype(BF16)
    normed = normed_ref[...]
    units = v1_me.shape[1]
    for side, w1 in enumerate((v1_me, v1_other)):
        copies[side].wait()
        for start, size in pieces_of(units, 256):
            hidden = gelu(
                jnp.dot(normed, w1[:, start : start + size], preferred_element_type=F32)
            )
            hidden_ref[:, side * units + start : side * units + start + size] = hidden.astype(BF16)
    copies[2].wait()
    copies[3].wait()
    features = v2_me.shape[1]
    if not halves:
        for start, size in pieces_of(features, 256):
            at = slice(start, start + size)
            outs[1][:, at] = (
                jnp.dot(hidden_ref[:, :units], v2_me[:, at], preferred_element_type=F32)
                + jnp.dot(hidden_ref[:, units:], v2_other[:, at], preferred_element_type=F32)
            ).astype(BF16)
        return
    total = jnp.dot(hidden_ref[:, :units], v2_me[...], preferred_element_type=F32) + jnp.dot(
        hidden_ref[:, units:], v2_other[...], preferred_element_type=F32
    )
    left, right = total[:, : features // 2], total[:, features // 2 :]
    first_half = place_ref[0] < 2
    outs[1][...] = jnp.where(first_half, left, right).astype(BF16)
    outs[2][...] = jnp.where(first_half, right, left).astype(BF16)


def feed_call(place, cur, mine, other, mod, weights, halves):
    rows, features = cur.shape
    fc1, fc2 = weights[0], weights[2]
    shape = jax.ShapeDtypeStruct((rows, features), BF16)
    half = jax.ShapeDtypeStruct((rows, features // 2), BF16)
    outs = (shape, half, half) if halves else (shape, shape)
    return pl.pallas_call(
        functools.partial(feed_kernel, halves),
        out_shape=outs,
        in_specs=[SMEM_SPEC] + [VMEM_SPEC] * 4 + [ANY_SPEC] * 4,
        out_specs=(VMEM_SPEC,) * len(outs),
        scratch_shapes=[
            pltpu.VMEM(fc1.shape, BF16),
            pltpu.VMEM(fc1.shape, BF16),
            pltpu.VMEM(fc2.shape, BF16),
            pltpu.VMEM(fc2.shape, BF16),
            pltpu.VMEM((rows, features), BF16),
            pltpu.VMEM((rows, 2 * fc1.shape[1]), BF16),
            pltpu.SemaphoreType.DMA((4,)),
        ],
        compiler_params=params(),
        name="feed",
    )(place, cur, mine, other, mod, *weights)


def finish_kernel(place_ref, old_ref, after_ref, mine_ref, other_ref, mod_ref, pair_ref, out_ref):
    groups, cores, rows_here, share = out_ref.shape
    frames, features = mod_ref.shape[1:]
    here = frames // groups
    tokens = rows_here // here
    half = features // 2
    first_half = place_ref[0] < 2
    keep, layer = pair_ref[:, 0:1], pair_ref[:, 1:2]

    def mine(value):
        return jnp.where(first_half, value[:, :half], value[:, half:])

    gate = mine(mod_ref[5])
    results = []
    for p in range(tokens):
        at = slice(p * frames, (p + 1) * frames)
        total = mine_ref[at, :].astype(F32) + other_ref[at, :].astype(F32)
        results.append(
            keep * mine(old_ref[at, :].astype(F32))
            + layer * (mine(after_ref[at, :].astype(F32)) + gate * total)
        )
    for c in range(cores):
        shares = [r[:, c * share : (c + 1) * share] for r in results]
        for g in range(groups):
            rows = [s[g * here : (g + 1) * here] for s in shares]
            out_ref[g, c] = jnp.concatenate(rows, axis=0).astype(BF16)


def finish(place, old, after, mine, other, mod, pair, groups):
    rows, features = old.shape
    share = features // 4
    return pl.pallas_call(
        finish_kernel,
        out_shape=jax.ShapeDtypeStruct((groups, 2, rows // groups, share), BF16),
        in_specs=[SMEM_SPEC] + [VMEM_SPEC] * 6,
        out_specs=VMEM_SPEC,
        compiler_params=params(),
        name="finish",
    )(place, old, after, mine, other, mod, pair)


def unpack_kernel(rows_ref, out_ref, wide_ref):
    frames, tokens, width = out_ref.shape
    slabs = wide_ref.shape[0]
    for s in range(slabs):
        value = rows_ref[:, s * LANES : min((s + 1) * LANES, width)].astype(F32)
        wide_ref[s, :, : value.shape[1]] = value
    for i in range(frames):
        pieces = [wide_ref[s, pl.ds(i, tokens, stride=frames), :] for s in range(slabs)]
        out_ref[i] = jnp.concatenate(pieces, axis=1)[:, :width].astype(BF16)


def unpack(rows, frames):
    count, width = rows.shape
    wide = -(-width // LANES) * LANES
    return pl.pallas_call(
        unpack_kernel,
        out_shape=jax.ShapeDtypeStruct((frames, count // frames, width), BF16),
        in_specs=[VMEM_SPEC],
        out_specs=VMEM_SPEC,
        scratch_shapes=[pltpu.VMEM((wide // LANES, count, LANES), F32)],
        compiler_params=params(),
        name="unpack",
    )(rows)


SWAP = [(0, 1), (1, 0)]


def on_device(
    latents, fresh, noise_level, window_mask, mod_table, keep_coef, layer_coef,
    w_qkv, w_out, w_fc1, w_fc2,
):
    here, tokens_all, share = latents.shape
    features = mod_table.shape[2]
    groups = lax.axis_size("frame")
    frames = groups * here
    frame_index = lax.axis_index("frame")
    y_index, core_index = lax.axis_index("y"), lax.axis_index("core")
    place = (2 * y_index + core_index).astype(jnp.int32).reshape(1)
    group_tokens = tokens_all // groups
    split = group_tokens % 2 == 0
    tokens = group_tokens // 2 if split else group_tokens
    block = max(frames, LANES)

    positions = (
        frame_index * here
        + jnp.arange(here, dtype=jnp.int32)[:, None]
        + jnp.arange(OFFSETS, dtype=jnp.int32)[None, :]
        - W
    )
    allowed = (window_mask == 1) & (positions >= 0) & (positions < frames)
    meta = jnp.concatenate([noise_level[:, None], allowed.astype(jnp.int32)], axis=1)

    fresh_here = lax.dynamic_slice_in_dim(fresh, frame_index * group_tokens, group_tokens, 1)
    fresh_parts = (
        fresh_here,
        lax.ppermute(fresh_here, "core", SWAP),
        lax.ppermute(fresh_here, "y", SWAP),
        lax.ppermute(fresh_here, ("y", "core"), [(i, i ^ 3) for i in range(4)]),
    )
    swap_core = functools.partial(lax.ppermute, axis_name="core", perm=SWAP)
    swap_y = functools.partial(lax.ppermute, axis_name="y", perm=SWAP)
    attention_weights = (w_qkv, swap_core(w_qkv), w_out, swap_core(w_out))
    feed_weights = (w_fc1, swap_core(w_fc1), w_fc2, swap_core(w_fc2))

    payload = make_payload(latents, meta)
    wide = payload.shape[1]
    if split:
        payload = payload.reshape(groups * 2, tokens * here, wide)
        received = lax.all_to_all(payload, ("frame", "core"), 0, 0, tiled=True)
        received = received.reshape(groups, 2, tokens * here, wide)
    else:
        payload = payload.reshape(groups, tokens * here, wide)
        received = lax.all_to_all(payload, "frame", 0, 0, tiled=True)
        partner = swap_core(received)
        first = core_index == 0
        received = jnp.stack(
            [jnp.where(first, received, partner), jnp.where(first, partner, received)], axis=1
        )
    received_other = swap_y(received)
    mod, pair, mask = prepare(
        received[:, 0, :here, share:], mod_table, jnp.stack([keep_coef, layer_coef]), block
    )

    rows = tokens * frames
    current, part = attention_call(
        functools.partial(first_attention_kernel, split),
        (place, received, received_other) + fresh_parts + (mod, mask),
        attention_weights, rows, features,
    )
    after, feed = feed_call(place, current, part, swap_y(part), mod, feed_weights, False)
    current, part = attention_call(
        functools.partial(next_attention_kernel, split),
        (place, current, after, feed, swap_y(feed)) + fresh_parts + (mod, pair, mask),
        attention_weights, rows, features,
    )
    after, feed_here, feed_there = feed_call(
        place, current, part, swap_y(part), mod, feed_weights, True
    )
    result = finish(place, current, after, feed_here, swap_y(feed_there), mod, pair, groups)
    if split:
        result = result.reshape(groups * 2, tokens * here, share)
        result = lax.all_to_all(result, ("frame", "core"), 0, 0, tiled=True)
    else:
        result = jnp.where(core_index == 0, result[:, 0], result[:, 1])
        result = lax.all_to_all(result, "frame", 0, 0, tiled=True)
    return unpack(result.reshape(tokens_all * here, share), here)


def solution(mesh):
    groups, heads = mesh.shape["frame"], mesh.shape["head"]
    inner = Mesh(mesh.devices.reshape(groups, heads // 2, 2), ("frame", "y", "core"))
    head = ("y", "core")
    in_specs = (
        P("frame", None, head),
        P(None, None, head),
        P("frame"),
        P("frame", None),
        P(),
        P(),
        P(),
        P(None, None, head),
        P(head, None),
        P(None, head),
        P(head, None),
    )
    return jax.shard_map(
        on_device, mesh=inner, in_specs=in_specs, out_specs=P("frame", None, head), check_vma=False
    )
```

time: 386 us -> 163 us (0.42)
  waiting for transfers between devices: 215 us -> 60.2 us
  Pallas kernels: 0 us -> 49.8 us
  matrix products: 43.4 us -> 0 us
  local copies, waits for them, and re-layouts: 56 us -> 19.2 us
  other arithmetic: 25.1 us -> 1.38 us
  between operations: 13.5 us -> 0.11 us
  blocking collectives: 9 us -> 16.4 us
  starting transfers between devices: 22.2 us -> 15 us
    psum x4 -> x0, waiting for transfers between devices: 145 us -> none  [the longest x2 75.2 us: on_device(): lax.psum(attention_part(current, modulation, allowed, w_qkv, w_out).astyp...]
    pallas_call x0 -> x8, Pallas kernels: none -> 49.8 us  [the longest x2 20.7 us: attention_call(): pl.pallas_call(kernel, out_shape=(jax.ShapeDtypeStruct((rows, features),...]
    dot_general x10 -> x0, matrix products: 33.7 us -> none  [the longest x2 13.4 us: feed_part(): return jnp.dot(hidden, w_fc2, preferred_element_type=jnp.float32)]
    another operation x6 -> x0, local copies, waits for them, and re-layouts: 20.3 us -> none  [the longest x2 8.53 us: window_attention(): key_heads = padded[0].reshape(span, token_count, head_count, HD)]
    all_to_all x0 -> x1, blocking collectives: none -> 16.4 us  [on_device(): result = lax.all_to_all(result, ('frame', 'core'), 0, 0, tiled=True)]
    all_gather x1 -> x0, waiting for transfers between devices: 13.6 us -> none  [on_device(): lax.all_gather(latents, 'head', axis=2, tiled=True)]
    ppermute x6 -> x12, starting transfers between devices: 21.5 us -> 7.97 us  [the longest x1 1.52 us: on_device(): lax.ppermute(fresh_here, 'y', SWAP)]
    slice x10 -> x0, local copies, waits for them, and re-layouts: 13 us -> none  [the longest x2 3.45 us: window_attention(): key_heads = padded[0].reshape(span, token_count, head_count, HD)]
  transfers between devices with their start and end apart: 11 -> 13, of which waited for: 9 -> 7; matrix products, arithmetic and copies ran while one was open for 7% -> 10% of each run, Pallas kernels for 0% -> 10%
where the time goes in v1:
time: 163 us; the launch traced here: 162 us
  waiting for transfers between devices  60.2 us (37%)
  Pallas kernels  49.8 us (31%)
  local copies, waits for them, and re-layouts  19.2 us (12%)
  blocking collectives  16.4 us (10%)
  starting transfers between devices  15 us (9%)
    ppermute x2, waiting for transfers between devices, on_device(): swap_y(part)  29.2 us
    pallas_call x2, Pallas kernels, attention_call(): pl.pallas_call(kernel, out_shape=(jax.ShapeDtypeStruct((rows, features),...  20.7 us
    pallas_call x2, Pallas kernels, feed_call(): pl.pallas_call(functools.partial(feed_kernel, halves), out_shape=outs, in...  18.3 us
    all_to_all x1, blocking collectives, on_device(): result = lax.all_to_all(result, ('frame', 'core'), 0, 0, tiled=True)  16.4 us
    ppermute x1, waiting for transfers between devices, on_device(): swap_y(feed)  14.7 us
    unnamed x27, local copies, waits for them, and re-layouts  9.31 us
    ppermute x1, waiting for transfers between devices, on_device(): swap_y(feed_there)  7.24 us
    all_to_all x1, starting transfers between devices, on_device(): received = lax.all_to_all(payload, ('frame', 'core'), 0, 0, tiled=True)  7.06 us
  transfers between devices with their start and end apart: 13, of which 7 were waited for; matrix products, arithmetic and copies ran while one was open for 10% of the time, Pallas kernels for 10%

profile of v1, /device:TPU:0, one launch (start us, length us, event | category | flops | bytes accessed | tf_op | source)
XLA Modules:
  0.0 162.1 jit_solution(15648195743916340808)
XLA Ops:
  1.0 0.7 copy.22
  1.7 0.8 fusion.4
  2.5 0.6 pad.4.meta_ref
  3.1 2.0 %payload.1 = bf16[512,384]{1,0:T(8,128)(2,1)} custom-call(bf16[8,64,288]{2,1,0:T(8,128)(2,1)} %x_ref.1, s32[8,96]{1,0:T(8,128)} %pad.4.meta_ref), custom_call_target="tpu_custom_call" | custom-call | tf_op jit(solution)/shard_map/payload/pallas_call | solution.py:56
  5.1 7.1 %all-to-all-start = ((bf16[16,32,384]{2,1,0:T(8,128)(2,1)}), bf16[16,32,384]{2,1,0:T(8,128)(2,1)}, u32[]{:S(2)}, u32[]{:S(2)}) async-start(bf16[16,32,384]{2,1,0:T(8,128)(2,1)} %bitcast.14), calls=%async_computation | async-start | bytes 786432 | tf_op jit(solution)/shard_map/all_to_all | solution.py:485
  12.6 1.4 collective-permute-start.3
  13.9 1.8 %collective-permute-done.3.f3 = bf16[2,8,288]{2,1,0:T(8,128)(2,1)S(1)} collective-permute-done((bf16[2,8,288]{2,1,0:T(8,128)(2,1)S(1)}, bf16[2,8,288]{2,1,0:T(8,128)(2,1)S(1)}, u32[]{:S(2)}, u32[]{:S(2)}) %collective-permute-start.3) | collective-permute-done | bytes 9248 | tf_op jit(solution)/shard_map/ppermute | solution.py:474
  15.7 1.5 collective-permute-start.2
  17.2 2.2 %collective-permute-done.2.f2 = bf16[2,8,288]{2,1,0:T(8,128)(2,1)S(1)} collective-permute-done((bf16[2,8,288]{2,1,0:T(8,128)(2,1)S(1)}, bf16[2,8,288]{2,1,0:T(8,128)(2,1)S(1)}, u32[]{:S(2)}, u32[]{:S(2)}) %collective-permute-start.2) | collective-permute-done | bytes 9248 | tf_op jit(solution)/shard_map/ppermute | solution.py:473
  19.4 5.1 %all-to-all-done = bf16[16,32,384]{2,1,0:T(8,128)(2,1)} async-done(((bf16[16,32,384]{2,1,0:T(8,128)(2,1)}), bf16[16,32,384]{2,1,0:T(8,128)(2,1)}, u32[]{:S(2)}, u32[]{:S(2)}) %all-to-all-start) | async-done | bytes 393248 | tf_op jit(solution)/shard_map/all_to_all | solution.py:485
  24.5 1.5 collective-permute-start
  26.0 4.2 %copy.24.qkv_me = bf16[3,1152,288]{2,1,0:T(8,128)(2,1)} copy(bf16[3,1152,288]{1,2,0:T(8,128)(2,1)} %param.18) | data formatting | bytes 3981312 | tf_op args[7]
  30.2 2.9 %copy.28 = f32[6,8,8,1152]{3,2,0,1:T(8,128)} copy(f32[6,8,8,1152]{3,2,1,0:T(8,128)} %bitcast.13) | data formatting | bytes 3538944 | tf_op jit(solution)/shard_map/reshape | solution.py:120
  33.7 1.4 slice_bitcast_fusion.meta_ref
  35.1 3.6 %prepare.1 = (f32[6,64,1152]{2,1,0:T(8,128)}, f32[64,128]{1,0:T(8,128)}, f32[128,128]{1,0:T(8,128)}) custom-call(bf16[8,8,96]{2,1,0:T(8,128)(2,1)} %slice_bitcast_fusion.meta_ref, f32[64,6912]{1,0:T(8,128)} %bitcast.12, f32[2,64]{1,0:T(2,128)} %pad_maximum_fusion.coef_ref), custom_call_target="tpu_custom_call" | custom-call | tf_op jit(solution)/shard_map/prepare/pallas_call | solution.py:109
  38.7 4.2 %copy.25.qkv_other = bf16[3,1152,288]{2,1,0:T(8,128)(2,1)} copy(bf16[3,1152,288]{1,2,0:T(8,128)(2,1)} %collective-permute-done.4) | data formatting | bytes 3981312 | tf_op jit(solution)/shard_map/ppermute | solution.py:478
  43.9 10.0 %attention.2 = (bf16[256,1152]{1,0:T(8,128)(2,1)}, bf16[256,1152]{1,0:T(8,128)(2,1)}) custom-call(s32[1]{0:T(128)} %bitcast.place_ref, bf16[8,2,32,384]{3,2,1,0:T(8,128)(2,1)} %bitcast.3.mine_ref, bf16[8,2,32,384]{3,2,1,0:T(8,128)(2,1)} %collective-permute-done.other_ref, bf16[2,8,288]{2,1,0:T(8,128)(2,1)} %copy-done.7, bf16[2,8,288]{2,1,0:T(8,128)(2,1)} %copy-done.10, ...), custom_call_target="tpu_custom_call" | custom-call | tf_op jit(solution)/shard_map/attention/pallas_call | solution.py:276
  54.4 15.4 %collective-permute-done.6.other_ref = bf16[256,1152]{1,0:T(8,128)(2,1)S(1)} collective-permute-done((bf16[256,1152]{1,0:T(8,128)(2,1)}, bf16[256,1152]{1,0:T(8,128)(2,1)S(1)}, u32[]{:S(2)}, u32[]{:S(2)}) %collective-permute-start.6) | collective-permute-done | bytes 589856 | tf_op jit(solution)/shard_map/ppermute | solution.py:506
  69.9 0.8 copy-done.4
  70.7 0.8 copy-done.1
  71.6 8.9 %feed.2 = (bf16[256,1152]{1,0:T(8,128)(2,1)}, bf16[256,1152]{1,0:T(8,128)(2,1)}) custom-call(s32[1]{0:T(128)} %bitcast.place_ref, bf16[256,1152]{1,0:T(8,128)(2,1)} %get-tuple-element.19.cur_ref.old_ref, bf16[256,1152]{1,0:T(8,128)(2,1)} %get-tuple-element.20.mine_ref, bf16[256,1152]{1,0:T(8,128)(2,1)} %copy-done.4, ...), custom_call_target="tpu_custom_call" | custom-call | tf_op jit(solution)/shard_map/feed/pallas_call | solution.py:356
  81.0 14.7 %collective-permute-done.9.other_ref = bf16[256,1152]{1,0:T(8,128)(2,1)S(1)} collective-permute-done((bf16[256,1152]{1,0:T(8,128)(2,1)}, bf16[256,1152]{1,0:T(8,128)(2,1)S(1)}, u32[]{:S(2)}, u32[]{:S(2)}) %collective-permute-start.9) | collective-permute-done | bytes 589856 | tf_op jit(solution)/shard_map/ppermute | solution.py:509
  95.7 0.8 copy-done.3
  96.5 10.7 %attention.3 = (bf16[256,1152]{1,0:T(8,128)(2,1)}, bf16[256,1152]{1,0:T(8,128)(2,1)}) custom-call(s32[1]{0:T(128)} %bitcast.place_ref, bf16[256,1152]{1,0:T(8,128)(2,1)} %get-tuple-element.19.cur_ref.old_ref, bf16[256,1152]{1,0:T(8,128)(2,1)} %get-tuple-element.21.after_ref, bf16[256,1152]{1,0:T(8,128)(2,1)} %get-tuple-element.22.mine_ref, ...), custom_call_target="tpu_custom_call" | custom-call | tf_op jit(solution)/shard_map/attention/pallas_call | solution.py:276
  107.8 13.8 %collective-permute-done.10.other_ref = bf16[256,1152]{1,0:T(8,128)(2,1)S(1)} collective-permute-done((bf16[256,1152]{1,0:T(8,128)(2,1)}, bf16[256,1152]{1,0:T(8,128)(2,1)S(1)}, u32[]{:S(2)}, u32[]{:S(2)}) %collective-permute-start.10) | collective-permute-done | bytes 589856 | tf_op jit(solution)/shard_map/ppermute | solution.py:513
  121.5 0.9 copy-done.5
  122.4 9.4 %feed.3 = (bf16[256,1152]{1,0:T(8,128)(2,1)}, bf16[256,576]{1,0:T(8,128)(2,1)}, bf16[256,576]{1,0:T(8,128)(2,1)}) custom-call(s32[1]{0:T(128)} %bitcast.place_ref, bf16[256,1152]{1,0:T(8,128)(2,1)} %get-tuple-element.24.cur_ref.old_ref, bf16[256,1152]{1,0:T(8,128)(2,1)} %get-tuple-element.25.mine_ref, bf16[256,1152]{1,0:T(8,128)(2,1)} %copy-done.5, ...), custom_call_target="tpu_custom_call" | custom-call | tf_op jit(solution)/shard_map/feed/pallas_call | solution.py:356
  132.4 7.2 %collective-permute-done.11.other_ref = bf16[256,576]{1,0:T(8,128)(2,1)S(1)} collective-permute-done((bf16[256,576]{1,0:T(8,128)(2,1)}, bf16[256,576]{1,0:T(8,128)(2,1)S(1)}, u32[]{:S(2)}, u32[]{:S(2)}) %collective-permute-start.11) | collective-permute-done | bytes 294944 | tf_op jit(solution)/shard_map/ppermute | solution.py:515
  139.7 0.8 copy-done.6
  140.4 3.3 %finish.1 = bf16[8,2,32,288]{3,2,1,0:T(8,128)(2,1)} custom-call(s32[1]{0:T(128)} %bitcast.place_ref, bf16[256,1152]{1,0:T(8,128)(2,1)} %get-tuple-element.24.cur_ref.old_ref, bf16[256,1152]{1,0:T(8,128)(2,1)} %get-tuple-element.26.after_ref, bf16[256,576]{1,0:T(8,128)(2,1)} %get-tuple-element.27.mine_ref, bf16[256,576]{1,0:T(8,128)(2,1)} %copy-done.6, ...), custom_call_target="tpu_custom_call" | custom-call | tf_op jit(solution)/shard_map/finish/pallas_call | solution.py:406
  143.8 16.4 %all_to_all.10 = bf16[16,32,288]{2,1,0:T(8,128)(2,1)} all-to-all(bf16[16,32,288]{2,1,0:T(8,128)(2,1)} %bitcast.15), channel_id=1, replica_groups=mesh['frame'=8,'y'=2,'core'=2] {'frame','core'}, dimensions={0} | all-to-all | bytes 589824 | tf_op jit(solution)/shard_map/all_to_all | solution.py:518
  160.2 1.9 %unpack.1 = bf16[8,64,288]{2,1,0:T(8,128)(2,1)} custom-call(bf16[512,288]{1,0:T(8,128)(2,1)} %bitcast.16), custom_call_target="tpu_custom_call" | custom-call | tf_op jit(solution)/shard_map/unpack/pallas_call | solution.py:430
  (40 shorter events, 5.2 us)
Async XLA Ops:
  0.0 12.6 %copy-start = (bf16[2,64,288]{2,1,0:T(8,128)(2,1)S(1)}, bf16[2,64,288]{2,1,0:T(8,128)(2,1)}, u32[]{:S(2)}) copy-start(bf16[2,64,288]{2,1,0:T(8,128)(2,1)} %param.12) | copy-start | bytes 221188
  0.0 33.7 %collective-permute-start.4 = (bf16[3,1152,288]{1,2,0:T(8,128)(2,1)}, bf16[3,1152,288]{1,2,0:T(8,128)(2,1)}, u32[]{:S(2)}, u32[]{:S(2)}) collective-permute-start(bf16[3,1152,288]{1,2,0:T(8,128)(2,1)} %param.18), channel_id=1, source_target_pairs={{0,1},{1,0},{2,3},{3,2},{4,5},{5,4},{6,7},{7,6},{8,9},{9,8},{10,11... | collective-permute-start | bytes 5971976 | tf_op jit(solution)/shard_map/ppermute | solution.py:478
  0.5 69.4 %collective-permute-start.7 = (bf16[1152,1152]{1,0:T(8,128)(2,1)}, bf16[1152,1152]{1,0:T(8,128)(2,1)S(1)}, u32[]{:S(2)}, u32[]{:S(2)}) collective-permute-start(bf16[1152,1152]{1,0:T(8,128)(2,1)} %fc1_me.3), channel_id=1, source_target_pairs={{0,1},{1,0},{2,3},{3,2},{4,5},{5,4},{6,7},{7,6},{8,9},{9,8},{10,11... | collective-permute-start | bytes 7962632 | tf_op jit(solution)/shard_map/ppermute | solution.py:479
  0.5 69.4 %collective-permute-start.8 = (bf16[1152,1152]{1,0:T(8,128)(2,1)}, bf16[1152,1152]{1,0:T(8,128)(2,1)}, u32[]{:S(2)}, u32[]{:S(2)}) collective-permute-start(bf16[1152,1152]{1,0:T(8,128)(2,1)} %fc2_me.3), channel_id=1, source_target_pairs={{0,1},{1,0},{2,3},{3,2},{4,5},{5,4},{6,7},{7,6},{8,9},{9,8},{10,11... | collective-permute-start | bytes 7962632 | tf_op jit(solution)/shard_map/ppermute | solution.py:479
  5.1 19.3 %all-to-all-start = ((bf16[16,32,384]{2,1,0:T(8,128)(2,1)}), bf16[16,32,384]{2,1,0:T(8,128)(2,1)}, u32[]{:S(2)}, u32[]{:S(2)}) async-start(bf16[16,32,384]{2,1,0:T(8,128)(2,1)} %bitcast.14), calls=%async_computation | async-start | bytes 786432 | tf_op jit(solution)/shard_map/all_to_all | solution.py:485
  12.2 30.8 %collective-permute-start.5 = (bf16[288,1152]{1,0:T(8,128)(2,1)}, bf16[288,1152]{1,0:T(8,128)(2,1)S(1)}, u32[]{:S(2)}, u32[]{:S(2)}) collective-permute-start(bf16[288,1152]{1,0:T(8,128)(2,1)} %out_me.3), channel_id=1, source_target_pairs={{0,1},{1,0},{2,3},{3,2},{4,5},{5,4},{6,7},{7,6},{8,9},{9,8},{10,11... | collective-permute-start | bytes 1990664 | tf_op jit(solution)/shard_map/ppermute | solution.py:478
  12.6 21.1 %copy-start.7 = (bf16[2,8,288]{2,1,0:T(8,128)(2,1)}, bf16[2,8,288]{2,1,0:T(8,128)(2,1)S(1)}, u32[]{:S(2)}) copy-start(bf16[2,8,288]{2,1,0:T(8,128)(2,1)S(1)} %constant_dynamic-slice_fusion.f0) | copy-start | bytes 27652
  12.6 3.1 %collective-permute-start.3 = (bf16[2,8,288]{2,1,0:T(8,128)(2,1)S(1)}, bf16[2,8,288]{2,1,0:T(8,128)(2,1)S(1)}, u32[]{:S(2)}, u32[]{:S(2)}) collective-permute-start(bf16[2,8,288]{2,1,0:T(8,128)(2,1)S(1)} %constant_dynamic-slice_fusion.f0), channel_id=1, source_target_pairs={{0,3},{1,2},{2,1},{3,0},{4,7},{5,6},{6,5},{7,4},{8,11},{9,10},{10,... | collective-permute-start | bytes 27656 | tf_op jit(solution)/shard_map/ppermute | solution.py:474
  15.7 17.4 %copy-start.8 = (bf16[2,8,288]{2,1,0:T(8,128)(2,1)}, bf16[2,8,288]{2,1,0:T(8,128)(2,1)S(1)}, u32[]{:S(2)}) copy-start(bf16[2,8,288]{2,1,0:T(8,128)(2,1)S(1)} %collective-permute-done.3.f3) | copy-start | bytes 27652
  15.7 3.7 %collective-permute-start.2 = (bf16[2,8,288]{2,1,0:T(8,128)(2,1)S(1)}, bf16[2,8,288]{2,1,0:T(8,128)(2,1)S(1)}, u32[]{:S(2)}, u32[]{:S(2)}) collective-permute-start(bf16[2,8,288]{2,1,0:T(8,128)(2,1)S(1)} %constant_dynamic-slice_fusion.f0), channel_id=1, source_target_pairs={{0,2},{2,0},{1,3},{3,1},{4,6},{6,4},{5,7},{7,5},{8,10},{10,8},{9,1... | collective-permute-start | bytes 27656 | tf_op jit(solution)/shard_map/ppermute | solution.py:473
  19.4 13.7 %copy-start.9 = (bf16[2,8,288]{2,1,0:T(8,128)(2,1)}, bf16[2,8,288]{2,1,0:T(8,128)(2,1)S(1)}, u32[]{:S(2)}) copy-start(bf16[2,8,288]{2,1,0:T(8,128)(2,1)S(1)} %collective-permute-done.2.f2) | copy-start | bytes 27652
  24.5 18.5 %collective-permute-start = (bf16[8,2,32,384]{3,2,1,0:T(8,128)(2,1)}, bf16[8,2,32,384]{3,2,1,0:T(8,128)(2,1)}, u32[]{:S(2)}, u32[]{:S(2)}) collective-permute-start(bf16[8,2,32,384]{3,2,1,0:T(8,128)(2,1)} %bitcast.3.mine_ref), channel_id=1, source_target_pairs={{0,2},{2,0},{1,3},{3,1},{4,6},{6,4},{5,7},{7,5},{8,10},{10,8},{9,1... | collective-permute-start | bytes 1179656 | tf_op jit(solution)/shard_map/ppermute | solution.py:495
  30.2 2.9 %copy-start.11 = (f32[64]{0:T(128)S(1)}, f32[64]{0:T(128)}, u32[]{:S(2)}) copy-start(f32[64]{0:T(128)} %param.17) | copy-start | bytes 772
  30.2 2.9 %copy-start.12 = (f32[64]{0:T(128)S(1)}, f32[64]{0:T(128)}, u32[]{:S(2)}) copy-start(f32[64]{0:T(128)} %param.16) | copy-start | bytes 772
  33.7 9.3 %collective-permute-start.1 = (bf16[2,8,288]{2,1,0:T(8,128)(2,1)S(1)}, bf16[2,8,288]{2,1,0:T(8,128)(2,1)S(1)}, u32[]{:S(2)}, u32[]{:S(2)}) collective-permute-start(bf16[2,8,288]{2,1,0:T(8,128)(2,1)S(1)} %constant_dynamic-slice_fusion.f0), channel_id=1, source_target_pairs={{0,1},{1,0},{2,3},{3,2},{4,5},{5,4},{6,7},{7,6},{8,9},{9,8},{10,11... | collective-permute-start | bytes 27656 | tf_op jit(solution)/shard_map/ppermute | solution.py:472
  43.0 0.6 copy-start.10
  43.0 0.9 copy-start.2
  53.9 16.0 %collective-permute-start.6 = (bf16[256,1152]{1,0:T(8,128)(2,1)}, bf16[256,1152]{1,0:T(8,128)(2,1)S(1)}, u32[]{:S(2)}, u32[]{:S(2)}) collective-permute-start(bf16[256,1152]{1,0:T(8,128)(2,1)} %get-tuple-element.20.mine_ref), channel_id=1, source_target_pairs={{0,2},{2,0},{1,3},{3,1},{4,6},{6,4},{5,7},{7,5},{8,10},{10,8},{9,1... | collective-permute-start | bytes 1769480 | tf_op jit(solution)/shard_map/ppermute | solution.py:506
  69.9 0.8 copy-start.4
  69.9 1.7 %copy-start.1 = (bf16[1152,1152]{1,0:T(8,128)(2,1)}, bf16[1152,1152]{1,0:T(8,128)(2,1)S(1)}, u32[]{:S(2)}) copy-start(bf16[1152,1152]{1,0:T(8,128)(2,1)S(1)} %collective-permute-done.7.fc1_other) | copy-start | bytes 7962628
  80.4 15.2 %collective-permute-start.9 = (bf16[256,1152]{1,0:T(8,128)(2,1)}, bf16[256,1152]{1,0:T(8,128)(2,1)S(1)}, u32[]{:S(2)}, u32[]{:S(2)}) collective-permute-start(bf16[256,1152]{1,0:T(8,128)(2,1)} %get-tuple-element.22.mine_ref), channel_id=1, source_target_pairs={{0,2},{2,0},{1,3},{3,1},{4,6},{6,4},{5,7},{7,5},{8,10},{10,8},{9,1... | collective-permute-start | bytes 1769480 | tf_op jit(solution)/shard_map/ppermute | solution.py:509
  95.7 0.8 copy-start.3
  107.2 14.3 %collective-permute-start.10 = (bf16[256,1152]{1,0:T(8,128)(2,1)}, bf16[256,1152]{1,0:T(8,128)(2,1)S(1)}, u32[]{:S(2)}, u32[]{:S(2)}) collective-permute-start(bf16[256,1152]{1,0:T(8,128)(2,1)} %get-tuple-element.25.mine_ref), channel_id=1, source_target_pairs={{0,2},{2,0},{1,3},{3,1},{4,6},{6,4},{5,7},{7,5},{8,10},{10,8},{9,1... | collective-permute-start | bytes 1769480 | tf_op jit(solution)/shard_map/ppermute | solution.py:513
  121.5 0.9 copy-start.5
  131.9 7.8 %collective-permute-start.11 = (bf16[256,576]{1,0:T(8,128)(2,1)}, bf16[256,576]{1,0:T(8,128)(2,1)S(1)}, u32[]{:S(2)}, u32[]{:S(2)}) collective-permute-start(bf16[256,576]{1,0:T(8,128)(2,1)} %get-tuple-element.28), channel_id=1, source_target_pairs={{0,2},{2,0},{1,3},{3,1},{4,6},{6,4},{5,7},{7,5},{8,10},{10,8},{9,1... | collective-permute-start | bytes 884744 | tf_op jit(solution)/shard_map/ppermute | solution.py:515
  139.7 0.8 copy-start.6

commit v2 on v1

--- a/solution.py
+++ b/solution.py
@@ -15,7 +15,7 @@
 F32 = jnp.float32
 BF16 = jnp.bfloat16
 LANES = 128
-VMEM_LIMIT = 56 * 1024 * 1024
+VMEM_LIMIT = 30 * 1024 * 1024
 
 VMEM_SPEC = pl.BlockSpec(memory_space=pltpu.VMEM)
 SMEM_SPEC = pl.BlockSpec(memory_space=pltpu.SMEM)
@@ -64,18 +64,18 @@
     )(x, meta)
 
 
-def prepare_kernel(width, meta_ref, table_ref, coef_ref, mod_ref, pair_ref, mask_ref):
+def prepare_kernel(meta_ref, table_ref, coef_ref, norm_ref, feed_ref, gate_ref, pair_ref, mask_ref):
     groups, here, wide = meta_ref.shape
     frames = groups * here
-    levels = table_ref.shape[0]
+    levels = table_ref.shape[1]
     meta = meta_ref[...].astype(F32).reshape(frames, wide)
     level = meta[:, 0:1]
     ids = lax.broadcasted_iota(jnp.int32, (frames, levels), 1).astype(F32)
     hot = level == ids
     hot_bf = hot.astype(BF16)
-    features = mod_ref.shape[2]
-    for j in range(mod_ref.shape[0]):
-        rows = table_ref[:, j * features : (j + 1) * features]
+    targets = [(norm_ref, 0), (norm_ref, 1), (feed_ref, 0), (feed_ref, 1), (feed_ref, 2), (gate_ref, 0)]
+    for j, (target, at) in enumerate(targets):
+        rows = table_ref[j]
         high = rows.astype(BF16)
         rest = rows - high.astype(F32)
         middle = rest.astype(BF16)
@@ -83,17 +83,16 @@
         total = jnp.dot(hot_bf, high, preferred_element_type=F32)
         total += jnp.dot(hot_bf, middle, preferred_element_type=F32)
         total += jnp.dot(hot_bf, low, preferred_element_type=F32)
-        mod_ref[j] = total
+        target[at] = total
     keep = jnp.sum(jnp.where(hot, coef_ref[0:1, :], 0.0), axis=1, keepdims=True)
     layer = jnp.sum(jnp.where(hot, coef_ref[1:2, :], 0.0), axis=1, keepdims=True)
     lane = lax.broadcasted_iota(jnp.int32, (frames, LANES), 1)
     pair_ref[...] = jnp.where(lane == 0, keep, layer)
 
     block = mask_ref.shape[0]
-    repeat = block // frames
     row = lax.broadcasted_iota(jnp.int32, (frames, block), 0)
     column = lax.broadcasted_iota(jnp.int32, (frames, block), 1)
-    for t in range(repeat):
+    for t in range(block // frames):
         distance = column - t * frames - row
         inside = (column >= t * frames) & (column < (t + 1) * frames)
         is_open = jnp.zeros((frames, block), F32)
@@ -105,28 +104,21 @@
 def prepare(meta, table, coefs, block):
     groups, here, _ = meta.shape
     frames = groups * here
-    levels, kinds, features = table.shape
+    features = table.shape[2]
     return pl.pallas_call(
-        functools.partial(prepare_kernel, features),
+        prepare_kernel,
         out_shape=(
-            jax.ShapeDtypeStruct((kinds, frames, features), F32),
+            jax.ShapeDtypeStruct((2, frames, features), F32),
+            jax.ShapeDtypeStruct((3, frames, features), F32),
+            jax.ShapeDtypeStruct((1, frames, features), F32),
             jax.ShapeDtypeStruct((frames, LANES), F32),
             jax.ShapeDtypeStruct((block, block), F32),
         ),
         in_specs=[VMEM_SPEC] * 3,
-        out_specs=(VMEM_SPEC,) * 3,
+        out_specs=(VMEM_SPEC,) * 5,
         compiler_params=params(),
         name="prepare",
-    )(meta, table.reshape(levels, kinds * features), coefs)
-
-
-def start_copies(sources, targets, sems):
-    copies = []
-    for n, (source, target) in enumerate(zip(sources, targets)):
-        copy = pltpu.make_async_copy(source, target, sems.at[n])
-        copy.start()
-        copies.append(copy)
-    return copies
+    )(meta, table, coefs)
 
 
 def attend(q, k, v, is_open):
@@ -156,29 +148,26 @@
     return jnp.concatenate([pieces[s] for s in sorted(pieces)], axis=1).astype(BF16)
 
 
-def attention_rows(current, mod_ref, mask_ref, copies, weights, tokens, out_ref, normed_ref):
-    for p, rows in enumerate(current):
-        frames = rows.shape[0]
-        normed_ref[p * frames : (p + 1) * frames, :] = normalise(
-            rows, mod_ref[0], mod_ref[1]
-        ).astype(BF16)
+def attention_rows(current, norm_ref, mask_ref, weights, out_ref):
+    normed = [normalise(rows, norm_ref[0], norm_ref[1]).astype(BF16) for rows in current]
+    normed = normed[0] if len(normed) == 1 else jnp.concatenate(normed, axis=0)
     qkv_me, qkv_other, out_me, out_other = weights
-    rows_total = normed_ref.shape[0]
+    rows_total = normed.shape[0]
     block = mask_ref.shape[0]
     is_open = mask_ref[...] > 0.5
-    normed = normed_ref[...]
     total = None
-    for side, (qkv, w_out) in enumerate(((qkv_me, out_me), (qkv_other, out_other))):
-        copies[2 * side].wait()
+    for qkv, w_out in ((qkv_me, out_me), (qkv_other, out_other)):
         q, k, v = (
-            jnp.dot(normed, qkv[t], preferred_element_type=F32).astype(BF16) for t in range(3)
+            lax.dot_general(
+                normed, qkv[t], (((1,), (1,)), ((), ())), preferred_element_type=F32
+            ).astype(BF16)
+            for t in range(3)
         )
         mixed = [
             attend(q[b : b + block], k[b : b + block], v[b : b + block], is_open)
             for b in range(0, rows_total, block)
         ]
         attended = mixed[0] if len(mixed) == 1 else jnp.concatenate(mixed, axis=0)
-        copies[2 * side + 1].wait()
         part = jnp.dot(attended, w_out[...], preferred_element_type=F32)
         total = part if total is None else total + part
     out_ref[...] = total.astype(BF16)
@@ -209,86 +198,65 @@
 
 
 def first_attention_kernel(
-    split, place_ref, mine_ref, other_ref, f0, f1, f2, f3, mod_ref, mask_ref,
-    qkv_me, qkv_other, out_me, out_other,
-    cur_ref, part_ref, vq_me, vo_me, vq_other, vo_other, normed_ref, sems,
+    split, chunk, place_ref, mine_ref, other_ref, f0, f1, f2, f3, norm_ref, mask_ref,
+    qkv_me, qkv_other, out_me, out_other, cur_ref, part_ref,
 ):
-    copies = start_copies(
-        (qkv_me, out_me, qkv_other, out_other), (vq_me, vo_me, vq_other, vo_other), sems
-    )
     groups, cores, rows_here, _ = mine_ref.shape
-    features = cur_ref.shape[1]
-    frames = mod_ref.shape[1]
+    frames = norm_ref.shape[1]
     here = frames // groups
     tokens = rows_here // here
-    share = qkv_me.shape[2]
+    share = qkv_me.shape[1]
     fresh = fresh_rows(place_ref, (f0, f1, f2, f3), 0, tokens, split)
     first_half = place_ref[0] < 2
+    start, count = chunk
+    at = slice(start * here, (start + count) * here)
     blocks = []
     for g in range(groups):
-        mine = [mine_ref[g, c].astype(F32)[:, :share] for c in range(cores)]
-        other = [other_ref[g, c].astype(F32)[:, :share] for c in range(cores)]
+        mine = [mine_ref[g, c].astype(F32)[at, :share] for c in range(cores)]
+        other = [other_ref[g, c].astype(F32)[at, :share] for c in range(cores)]
         left = [jnp.where(first_half, a, b) for a, b in zip(mine, other)]
         right = [jnp.where(first_half, b, a) for a, b in zip(mine, other)]
         blocks.append(jnp.concatenate(left + right, axis=1))
     current = []
-    for p in range(tokens):
+    for p in range(count):
         rows = jnp.concatenate([b[p * here : (p + 1) * here] for b in blocks], axis=0)
-        rows = shifted_in(rows, fresh[p : p + 1])
+        rows = shifted_in(rows, fresh[start + p : start + p + 1])
         cur_ref[p * frames : (p + 1) * frames, :] = rows.astype(BF16)
         current.append(rows)
-    attention_rows(
-        current, mod_ref, mask_ref, copies, (vq_me, vq_other, vo_me, vo_other), tokens,
-        part_ref, normed_ref,
-    )
+    attention_rows(current, norm_ref, mask_ref, (qkv_me, qkv_other, out_me, out_other), part_ref)
 
 
 def next_attention_kernel(
-    split, place_ref, old_ref, after_ref, mine_ref, other_ref, f0, f1, f2, f3, mod_ref, pair_ref,
-    mask_ref, qkv_me, qkv_other, out_me, out_other,
-    cur_ref, part_ref, vq_me, vo_me, vq_other, vo_other, normed_ref, sems,
+    split, chunk, all_tokens, place_ref, old_ref, after_ref, mine_ref, other_ref, f0, f1, f2, f3,
+    norm_ref, gate_ref, pair_ref, mask_ref,
+    qkv_me, qkv_other, out_me, out_other, cur_ref, part_ref,
 ):
-    copies = start_copies(
-        (qkv_me, out_me, qkv_other, out_other), (vq_me, vo_me, vq_other, vo_other), sems
-    )
-    frames = mod_ref.shape[1]
-    tokens = old_ref.shape[0] // frames
-    fresh = fresh_rows(place_ref, (f0, f1, f2, f3), 1, tokens, split)
+    frames = norm_ref.shape[1]
+    start, count = chunk
+    fresh = fresh_rows(place_ref, (f0, f1, f2, f3), 1, all_tokens, split)
     keep, layer = pair_ref[:, 0:1], pair_ref[:, 1:2]
     current = []
-    for p in range(tokens):
+    for p in range(count):
         at = slice(p * frames, (p + 1) * frames)
         total = mine_ref[at, :].astype(F32) + other_ref[at, :].astype(F32)
         rows = keep * old_ref[at, :].astype(F32) + layer * (
-            after_ref[at, :].astype(F32) + mod_ref[5] * total
-        )
-        rows = shifted_in(rows, fresh[p : p + 1]).astype(BF16)
+            after_ref[at, :].astype(F32) + gate_ref[0] * total
+        )
+        rows = shifted_in(rows, fresh[start + p : start + p + 1]).astype(BF16)
         cur_ref[at, :] = rows
         current.append(rows.astype(F32))
-    attention_rows(
-        current, mod_ref, mask_ref, copies, (vq_me, vq_other, vo_me, vo_other), tokens,
-        part_ref, normed_ref,
-    )
-
-
-def attention_call(kernel, vmem_args, weights, rows, features):
-    qkv, w_out = weights[0], weights[2]
+    attention_rows(current, norm_ref, mask_ref, (qkv_me, qkv_other, out_me, out_other), part_ref)
+
+
+def attention_call(kernel, arrays, rows, features):
     return pl.pallas_call(
         kernel,
         out_shape=(jax.ShapeDtypeStruct((rows, features), BF16),) * 2,
-        in_specs=[SMEM_SPEC] + [VMEM_SPEC] * (len(vmem_args) - 1) + [ANY_SPEC] * 4,
+        in_specs=[SMEM_SPEC] + [VMEM_SPEC] * (len(arrays) - 1),
         out_specs=(VMEM_SPEC,) * 2,
-        scratch_shapes=[
-            pltpu.VMEM(qkv.shape, BF16),
-            pltpu.VMEM(w_out.shape, BF16),
-            pltpu.VMEM(qkv.shape, BF16),
-            pltpu.VMEM(w_out.shape, BF16),
-            pltpu.VMEM((rows, features), BF16),
-            pltpu.SemaphoreType.DMA((4,)),
-        ],
         compiler_params=params(),
         name="attention",
-    )(*vmem_args, *weights)
+    )(*arrays)
 
 
 def gelu(x):
@@ -304,43 +272,37 @@
     halves, place_ref, cur_ref, mine_ref, other_ref, mod_ref,
     fc1_me, fc1_other, fc2_me, fc2_other, *rest,
 ):
-    outs, scratch = rest[: 3 if halves else 2], rest[3 if halves else 2 :]
+    outs, hidden_ref = rest[:-1], rest[-1]
     after_ref = outs[0]
-    v1_me, v1_other, v2_me, v2_other, normed_ref, hidden_ref, sems = scratch
-    copies = start_copies(
-        (fc1_me, fc1_other, fc2_me, fc2_other), (v1_me, v1_other, v2_me, v2_other), sems
-    )
     frames = mod_ref.shape[1]
     tokens = cur_ref.shape[0] // frames
+    normed = []
     for p in range(tokens):
         at = slice(p * frames, (p + 1) * frames)
         total = mine_ref[at, :].astype(F32) + other_ref[at, :].astype(F32)
-        after = (cur_ref[at, :].astype(F32) + mod_ref[2] * total).astype(BF16)
+        after = (cur_ref[at, :].astype(F32) + mod_ref[0] * total).astype(BF16)
         after_ref[at, :] = after
-        normed_ref[at, :] = normalise(after.astype(F32), mod_ref[3], mod_ref[4]).astype(BF16)
-    normed = normed_ref[...]
-    units = v1_me.shape[1]
-    for side, w1 in enumerate((v1_me, v1_other)):
-        copies[side].wait()
+        normed.append(normalise(after.astype(F32), mod_ref[1], mod_ref[2]).astype(BF16))
+    normed = normed[0] if tokens == 1 else jnp.concatenate(normed, axis=0)
+    units, features = fc2_me.shape
+    for side, w1 in enumerate((fc1_me, fc1_other)):
         for start, size in pieces_of(units, 256):
             hidden = gelu(
                 jnp.dot(normed, w1[:, start : start + size], preferred_element_type=F32)
             )
             hidden_ref[:, side * units + start : side * units + start + size] = hidden.astype(BF16)
-    copies[2].wait()
-    copies[3].wait()
-    features = v2_me.shape[1]
+
+    def product(at):
+        return jnp.dot(
+            hidden_ref[:, :units], fc2_me[:, at], preferred_element_type=F32
+        ) + jnp.dot(hidden_ref[:, units:], fc2_other[:, at], preferred_element_type=F32)
+
     if not halves:
         for start, size in pieces_of(features, 256):
             at = slice(start, start + size)
-            outs[1][:, at] = (
-                jnp.dot(hidden_ref[:, :units], v2_me[:, at], preferred_element_type=F32)
-                + jnp.dot(hidden_ref[:, units:], v2_other[:, at], preferred_element_type=F32)
-            ).astype(BF16)
+            outs[1][:, at] = product(at).astype(BF16)
         return
-    total = jnp.dot(hidden_ref[:, :units], v2_me[...], preferred_element_type=F32) + jnp.dot(
-        hidden_ref[:, units:], v2_other[...], preferred_element_type=F32
-    )
+    total = product(slice(None))
     left, right = total[:, : features // 2], total[:, features // 2 :]
     first_half = place_ref[0] < 2
     outs[1][...] = jnp.where(first_half, left, right).astype(BF16)
@@ -349,34 +311,25 @@
 
 def feed_call(place, cur, mine, other, mod, weights, halves):
     rows, features = cur.shape
-    fc1, fc2 = weights[0], weights[2]
     shape = jax.ShapeDtypeStruct((rows, features), BF16)
     half = jax.ShapeDtypeStruct((rows, features // 2), BF16)
     outs = (shape, half, half) if halves else (shape, shape)
     return pl.pallas_call(
         functools.partial(feed_kernel, halves),
         out_shape=outs,
-        in_specs=[SMEM_SPEC] + [VMEM_SPEC] * 4 + [ANY_SPEC] * 4,
+        in_specs=[SMEM_SPEC] + [VMEM_SPEC] * 8,
         out_specs=(VMEM_SPEC,) * len(outs),
-        scratch_shapes=[
-            pltpu.VMEM(fc1.shape, BF16),
-            pltpu.VMEM(fc1.shape, BF16),
-            pltpu.VMEM(fc2.shape, BF16),
-            pltpu.VMEM(fc2.shape, BF16),
-            pltpu.VMEM((rows, features), BF16),
-            pltpu.VMEM((rows, 2 * fc1.shape[1]), BF16),
-            pltpu.SemaphoreType.DMA((4,)),
-        ],
+        scratch_shapes=[pltpu.VMEM((rows, 2 * weights[0].shape[1]), BF16)],
         compiler_params=params(),
         name="feed",
     )(place, cur, mine, other, mod, *weights)
 
 
-def finish_kernel(place_ref, old_ref, after_ref, mine_ref, other_ref, mod_ref, pair_ref, out_ref):
-    groups, cores, rows_here, share = out_ref.shape
-    frames, features = mod_ref.shape[1:]
+def finish_kernel(chunks, place_ref, gate_ref, pair_ref, *refs):
+    out_ref = refs[-1]
+    groups, cores, _, share = out_ref.shape
+    _, frames, features = gate_ref.shape
     here = frames // groups
-    tokens = rows_here // here
     half = features // 2
     first_half = place_ref[0] < 2
     keep, layer = pair_ref[:, 0:1], pair_ref[:, 1:2]
@@ -384,15 +337,17 @@
     def mine(value):
         return jnp.where(first_half, value[:, :half], value[:, half:])
 
-    gate = mine(mod_ref[5])
+    gate = mine(gate_ref[0])
     results = []
-    for p in range(tokens):
-        at = slice(p * frames, (p + 1) * frames)
-        total = mine_ref[at, :].astype(F32) + other_ref[at, :].astype(F32)
-        results.append(
-            keep * mine(old_ref[at, :].astype(F32))
-            + layer * (mine(after_ref[at, :].astype(F32)) + gate * total)
-        )
+    for n in range(chunks):
+        old_ref, after_ref, mine_ref, other_ref = refs[4 * n : 4 * n + 4]
+        for p in range(old_ref.shape[0] // frames):
+            at = slice(p * frames, (p + 1) * frames)
+            total = mine_ref[at, :].astype(F32) + other_ref[at, :].astype(F32)
+            results.append(
+                keep * mine(old_ref[at, :].astype(F32))
+                + layer * (mine(after_ref[at, :].astype(F32)) + gate * total)
+            )
     for c in range(cores):
         shares = [r[:, c * share : (c + 1) * share] for r in results]
         for g in range(groups):
@@ -400,17 +355,18 @@
             out_ref[g, c] = jnp.concatenate(rows, axis=0).astype(BF16)
 
 
-def finish(place, old, after, mine, other, mod, pair, groups):
-    rows, features = old.shape
-    share = features // 4
+def finish(place, gate, pair, parts, groups):
+    features = gate.shape[2]
+    rows = sum(part[0].shape[0] for part in parts)
+    arrays = [array for part in parts for array in part]
     return pl.pallas_call(
-        finish_kernel,
-        out_shape=jax.ShapeDtypeStruct((groups, 2, rows // groups, share), BF16),
-        in_specs=[SMEM_SPEC] + [VMEM_SPEC] * 6,
+        functools.partial(finish_kernel, len(parts)),
+        out_shape=jax.ShapeDtypeStruct((groups, 2, rows // groups, features // 4), BF16),
+        in_specs=[SMEM_SPEC] + [VMEM_SPEC] * (2 + len(arrays)),
         out_specs=VMEM_SPEC,
         compiler_params=params(),
         name="finish",
-    )(place, old, after, mine, other, mod, pair)
+    )(place, gate, pair, *arrays)
 
 
 def unpack_kernel(rows_ref, out_ref, wide_ref):
@@ -475,6 +431,7 @@
     )
     swap_core = functools.partial(lax.ppermute, axis_name="core", perm=SWAP)
     swap_y = functools.partial(lax.ppermute, axis_name="y", perm=SWAP)
+    w_qkv = jnp.swapaxes(w_qkv, 1, 2)
     attention_weights = (w_qkv, swap_core(w_qkv), w_out, swap_core(w_out))
     feed_weights = (w_fc1, swap_core(w_fc1), w_fc2, swap_core(w_fc2))
 
@@ -493,26 +450,45 @@
             [jnp.where(first, received, partner), jnp.where(first, partner, received)], axis=1
         )
     received_other = swap_y(received)
-    mod, pair, mask = prepare(
-        received[:, 0, :here, share:], mod_table, jnp.stack([keep_coef, layer_coef]), block
+    norm_mod, feed_mod, gate_mod, pair, mask = prepare(
+        received[:, 0, :here, share:],
+        jnp.swapaxes(mod_table, 0, 1),
+        jnp.stack([keep_coef, layer_coef]),
+        block,
     )
 
-    rows = tokens * frames
-    current, part = attention_call(
-        functools.partial(first_attention_kernel, split),
-        (place, received, received_other) + fresh_parts + (mod, mask),
-        attention_weights, rows, features,
-    )
-    after, feed = feed_call(place, current, part, swap_y(part), mod, feed_weights, False)
-    current, part = attention_call(
-        functools.partial(next_attention_kernel, split),
-        (place, current, after, feed, swap_y(feed)) + fresh_parts + (mod, pair, mask),
-        attention_weights, rows, features,
-    )
-    after, feed_here, feed_there = feed_call(
-        place, current, part, swap_y(part), mod, feed_weights, True
-    )
-    result = finish(place, current, after, feed_here, swap_y(feed_there), mod, pair, groups)
+    chunk_count = 2 if tokens % 2 == 0 and tokens * frames // 2 % block == 0 else 1
+    size = tokens // chunk_count
+    chunks = [(n * size, size) for n in range(chunk_count)]
+    rows = size * frames
+
+    state = []
+    for chunk in chunks:
+        current, part = attention_call(
+            functools.partial(first_attention_kernel, split, chunk),
+            (place, received, received_other) + fresh_parts + (norm_mod, mask) + attention_weights,
+            rows, features,
+        )
+        state.append((current, part, swap_y(part)))
+    fed = []
+    for current, part, part_other in state:
+        after, feed = feed_call(place, current, part, part_other, feed_mod, feed_weights, False)
+        fed.append((current, after, feed, swap_y(feed)))
+    state = []
+    for chunk, arrays in zip(chunks, fed):
+        current, part = attention_call(
+            functools.partial(next_attention_kernel, split, chunk, tokens),
+            (place,) + arrays + fresh_parts + (norm_mod, gate_mod, pair, mask) + attention_weights,
+            rows, features,
+        )
+        state.append((current, part, swap_y(part)))
+    parts = []
+    for current, part, part_other in state:
+        after, feed_here, feed_there = feed_call(
+            place, current, part, part_other, feed_mod, feed_weights, True
+        )
+        parts.append((current, after, feed_here, swap_y(feed_there)))
+    result = finish(place, gate_mod, pair, parts, groups)
     if split:
         result = result.reshape(groups * 2, tokens * here, share)
         result = lax.all_to_all(result, ("frame", "core"), 0, 0, tiled=True)

time: 163 us -> 115 us (0.71)
  waiting for transfers between devices: 60.2 us -> 26 us
  local copies, waits for them, and re-layouts: 19.2 us -> 6.32 us
  starting transfers between devices: 15 us -> 20.9 us
  Pallas kernels: 49.8 us -> 44.6 us
    ppermute x4 -> x8, waiting for transfers between devices: 51.1 us -> 10.9 us  [the longest x4 5.7 us: on_device(): state.append((current, part, swap_y(part)))]
    ppermute x1, waiting for transfers between devices: 0.01 us -> 6.05 us  [on_device(): received_other = swap_y(received)]
    ppermute x4 -> x8, starting transfers between devices: 2.25 us -> 8.15 us  [the longest x4 4.6 us: on_device(): state.append((current, part, swap_y(part)))]
    pallas_call x2, Pallas kernels: 6.96 us -> 1.48 us  [the longest x1 0.91 us: prepare(): pl.pallas_call(prepare_kernel, out_shape=(jax.ShapeDtypeStruct((2, frames...]
    unnamed x27 -> x18, local copies, waits for them, and re-layouts: 9.31 us -> 4.79 us
    pallas_call x2 -> x4, Pallas kernels: 20.7 us -> 25 us  [attention_call(): pl.pallas_call(kernel, out_shape=(jax.ShapeDtypeStruct((rows, features),...]
    ppermute x1 -> x0, local copies, waits for them, and re-layouts: 4.22 us -> none  [on_device(): attention_weights = (w_qkv, swap_core(w_qkv), w_out, swap_core(w_out))]
    reshape x1 -> x0, local copies, waits for them, and re-layouts: 2.91 us -> none  [prepare(): table.reshape(levels, kinds * features)]
  transfers between devices with their start and end apart: 13 -> 17, of which waited for: 7 -> 9; matrix products, arithmetic and copies ran while one was open for 10% -> 3% of each run, Pallas kernels for 10% -> 38%
where the time goes in v2:
time: 115 us
  Pallas kernels  44.6 us (39%)
  waiting for transfers between devices  26 us (23%)
  starting transfers between devices  20.9 us (18%)
  blocking collectives  15.3 us (13%)
  local copies, waits for them, and re-layouts  6.32 us (5%)
  other arithmetic  1.52 us (1%)
    pallas_call x4, Pallas kernels, attention_call(): pl.pallas_call(kernel, out_shape=(jax.ShapeDtypeStruct((rows, features),...  25 us
    pallas_call x4, Pallas kernels, feed_call(): pl.pallas_call(functools.partial(feed_kernel, halves), out_shape=outs, in...  17 us
    all_to_all x1, blocking collectives, on_device(): result = lax.all_to_all(result, ('frame', 'core'), 0, 0, tiled=True)  15.3 us
    all_to_all x1, starting transfers between devices, on_device(): received = lax.all_to_all(payload, ('frame', 'core'), 0, 0, tiled=True)  7.08 us
    ppermute x1, waiting for transfers between devices, on_device(): received_other = swap_y(received)  6.05 us
    ppermute x4, waiting for transfers between devices, on_device(): state.append((current, part, swap_y(part)))  5.7 us
    unnamed x18, local copies, waits for them, and re-layouts  4.79 us
    ppermute x4, starting transfers between devices, on_device(): state.append((current, part, swap_y(part)))  4.6 us
  transfers between devices with their start and end apart: 17, of which 9 were waited for; matrix products, arithmetic and copies ran while one was open for 3% of the time, Pallas kernels for 38%

profile of v2, /device:TPU:0, one launch (start us, length us, event | category | flops | bytes accessed | tf_op | source)
XLA Modules:
  0.0 114.8 jit_solution(16311699942935294439)
XLA Ops:
  2.5 1.0 copy-done.8
  4.5 7.1 %all-to-all-start = ((bf16[16,32,384]{2,1,0:T(8,128)(2,1)}), bf16[16,32,384]{2,1,0:T(8,128)(2,1)}, u32[]{:S(2)}, u32[]{:S(2)}) async-start(bf16[16,32,384]{2,1,0:T(8,128)(2,1)} %bitcast.18), calls=%async_computation | async-start | bytes 786432 | tf_op jit(solution)/shard_map/all_to_all | solution.py:442
  12.0 1.3 %collective-permute-start.3 = (bf16[2,8,288]{2,1,0:T(8,128)(2,1)S(1)}, bf16[2,8,288]{2,1,0:T(8,128)(2,1)S(1)}, u32[]{:S(2)}, u32[]{:S(2)}) collective-permute-start(bf16[2,8,288]{2,1,0:T(8,128)(2,1)S(1)} %constant_dynamic-slice_fusion.f0), channel_id=1, source_target_pairs={{0,3},{1,2},{2,1},{3,0},{4,7},{5,6},{6,5},{7,4},{8,11},{9,10},{10,... | collective-permute-start | bytes 27656 | tf_op jit(solution)/shard_map/ppermute | solution.py:430
  13.3 1.8 %collective-permute-done.3.f3 = bf16[2,8,288]{2,1,0:T(8,128)(2,1)S(1)} collective-permute-done((bf16[2,8,288]{2,1,0:T(8,128)(2,1)S(1)}, bf16[2,8,288]{2,1,0:T(8,128)(2,1)S(1)}, u32[]{:S(2)}, u32[]{:S(2)}) %collective-permute-start.3) | collective-permute-done | bytes 9248 | tf_op jit(solution)/shard_map/ppermute | solution.py:430
  15.1 1.5 %collective-permute-start.2 = (bf16[2,8,288]{2,1,0:T(8,128)(2,1)S(1)}, bf16[2,8,288]{2,1,0:T(8,128)(2,1)S(1)}, u32[]{:S(2)}, u32[]{:S(2)}) collective-permute-start(bf16[2,8,288]{2,1,0:T(8,128)(2,1)S(1)} %constant_dynamic-slice_fusion.f0), channel_id=1, source_target_pairs={{0,2},{2,0},{1,3},{3,1},{4,6},{6,4},{5,7},{7,5},{8,10},{10,8},{9,1... | collective-permute-start | bytes 27656 | tf_op jit(solution)/shard_map/ppermute | solution.py:429
  16.6 2.2 %collective-permute-done.2.f2 = bf16[2,8,288]{2,1,0:T(8,128)(2,1)S(1)} collective-permute-done((bf16[2,8,288]{2,1,0:T(8,128)(2,1)S(1)}, bf16[2,8,288]{2,1,0:T(8,128)(2,1)S(1)}, u32[]{:S(2)}, u32[]{:S(2)}) %collective-permute-start.2) | collective-permute-done | bytes 9248 | tf_op jit(solution)/shard_map/ppermute | solution.py:429
  18.8 1.2 %collective-permute-done.1.f1 = bf16[2,8,288]{2,1,0:T(8,128)(2,1)S(1)} collective-permute-done((bf16[2,8,288]{2,1,0:T(8,128)(2,1)S(1)}, bf16[2,8,288]{2,1,0:T(8,128)(2,1)S(1)}, u32[]{:S(2)}, u32[]{:S(2)}) %collective-permute-start.1) | collective-permute-done | bytes 9248 | tf_op jit(solution)/shard_map/ppermute | solution.py:428
  20.0 3.9 %all-to-all-done = bf16[16,32,384]{2,1,0:T(8,128)(2,1)} async-done(((bf16[16,32,384]{2,1,0:T(8,128)(2,1)}), bf16[16,32,384]{2,1,0:T(8,128)(2,1)}, u32[]{:S(2)}, u32[]{:S(2)}) %all-to-all-start) | async-done | bytes 393248 | tf_op jit(solution)/shard_map/all_to_all | solution.py:442
  23.9 1.5 %collective-permute-start = (bf16[8,2,32,384]{3,2,1,0:T(8,128)(2,1)}, bf16[8,2,32,384]{3,2,1,0:T(8,128)(2,1)}, u32[]{:S(2)}, u32[]{:S(2)}) collective-permute-start(bf16[8,2,32,384]{3,2,1,0:T(8,128)(2,1)} %bitcast.3.mine_ref), channel_id=1, source_target_pairs={{0,2},{2,0},{1,3},{3,1},{4,6},{6,4},{5,7},{7,5},{8,10},{10,8},{9,1... | collective-permute-start | bytes 1179656 | tf_op jit(solution)/shard_map/ppermute | solution.py:452
  26.9 1.5 %copy-done.6 = f32[64,6,1152]{2,0,1:T(8,128)S(1)} copy-done((f32[64,6,1152]{2,0,1:T(8,128)S(1)}, f32[64,6,1152]{2,0,1:T(8,128)}, u32[]{:S(2)}) %copy-start.6) | copy-done | bytes 1769496
  28.4 0.9 prepare.1
  29.3 6.0 %collective-permute-done.other_ref = bf16[8,2,32,384]{3,2,1,0:T(8,128)(2,1)} collective-permute-done((bf16[8,2,32,384]{3,2,1,0:T(8,128)(2,1)}, bf16[8,2,32,384]{3,2,1,0:T(8,128)(2,1)}, u32[]{:S(2)}, u32[]{:S(2)}) %collective-permute-start) | collective-permute-done | bytes 393248 | tf_op jit(solution)/shard_map/ppermute | solution.py:452
  35.3 1.6 %copy-done.3 = bf16[3,1152,288]{1,2,0:T(8,128)(2,1)S(1)} copy-done((bf16[3,1152,288]{1,2,0:T(8,128)(2,1)S(1)}, bf16[3,1152,288]{1,2,0:T(8,128)(2,1)}, u32[]{:S(2)}) %copy-start.3) | copy-done | bytes 1990680
  36.9 6.3 %attention.4 = (bf16[128,1152]{1,0:T(8,128)(2,1)S(1)}, bf16[128,1152]{1,0:T(8,128)(2,1)S(1)}) custom-call(s32[1]{0:T(128)} %bitcast.place_ref, bf16[8,2,32,384]{3,2,1,0:T(8,128)(2,1)} %bitcast.3.mine_ref, bf16[8,2,32,384]{3,2,1,0:T(8,128)(2,1)} %collective-permute-done.other_ref, bf16[2,8,288]{2,1,0:T(8,128)(2,1)S(1)} %constant_dynamic-slice_fusion.f0, ...), custom_call_target="tpu_custom_call" | custom-call | tf_op jit(solution)/shard_map/attention/pallas_call | solution.py:252
  43.2 1.6 %collective-permute-start.6 = (bf16[128,1152]{1,0:T(8,128)(2,1)S(1)}, bf16[128,1152]{1,0:T(8,128)(2,1)S(1)}, u32[]{:S(2)}, u32[]{:S(2)}) collective-permute-start(bf16[128,1152]{1,0:T(8,128)(2,1)S(1)} %get-tuple-element.33.mine_ref), channel_id=1, source_target_pairs={{0,2},{2,0},{1,3},{3,1},{4,6},{6,4},{5,7},{7,5},{8,10},{10,8},{9,1... | collective-permute-start | bytes 884744 | tf_op jit(solution)/shard_map/ppermute | solution.py:472
  44.8 6.3 %attention.6 = (bf16[128,1152]{1,0:T(8,128)(2,1)S(1)}, bf16[128,1152]{1,0:T(8,128)(2,1)S(1)}) custom-call(s32[1]{0:T(128)} %bitcast.place_ref, bf16[8,2,32,384]{3,2,1,0:T(8,128)(2,1)} %bitcast.3.mine_ref, bf16[8,2,32,384]{3,2,1,0:T(8,128)(2,1)} %collective-permute-done.other_ref, bf16[2,8,288]{2,1,0:T(8,128)(2,1)S(1)} %constant_dynamic-slice_fusion.f0, ...), custom_call_target="tpu_custom_call" | custom-call | tf_op jit(solution)/shard_map/attention/pallas_call | solution.py:252
  51.0 0.9 collective-permute-start.12
  51.9 4.0 %feed.4 = (bf16[128,1152]{1,0:T(8,128)(2,1)S(1)}, bf16[128,1152]{1,0:T(8,128)(2,1)S(1)}) custom-call(s32[1]{0:T(128)} %bitcast.place_ref, bf16[128,1152]{1,0:T(8,128)(2,1)S(1)} %get-tuple-element.32.cur_ref.old_ref, bf16[128,1152]{1,0:T(8,128)(2,1)S(1)} %get-tuple-element.33.mine_ref, bf16[128,1152]{1,0:T(8,128)(2,1)S(1)} %collective-permute-done.6.other_ref, ...), custom_call_target="tpu_custom_call" | custom-call | tf_op jit(solution)/shard_map/feed/pallas_call | solution.py:317
  56.0 1.3 %collective-permute-start.9 = (bf16[128,1152]{1,0:T(8,128)(2,1)S(1)}, bf16[128,1152]{1,0:T(8,128)(2,1)S(1)}, u32[]{:S(2)}, u32[]{:S(2)}) collective-permute-start(bf16[128,1152]{1,0:T(8,128)(2,1)S(1)} %get-tuple-element.36.mine_ref), channel_id=1, source_target_pairs={{0,2},{2,0},{1,3},{3,1},{4,6},{6,4},{5,7},{7,5},{8,10},{10,8},{9,1... | collective-permute-start | bytes 884744 | tf_op jit(solution)/shard_map/ppermute | solution.py:476
  57.3 3.8 %collective-permute-done.12.other_ref = bf16[128,1152]{1,0:T(8,128)(2,1)S(1)} collective-permute-done((bf16[128,1152]{1,0:T(8,128)(2,1)S(1)}, bf16[128,1152]{1,0:T(8,128)(2,1)S(1)}, u32[]{:S(2)}, u32[]{:S(2)}) %collective-permute-start.12) | collective-permute-done | bytes 294944 | tf_op jit(solution)/shard_map/ppermute | solution.py:472
  61.0 4.2 %feed.6 = (bf16[128,1152]{1,0:T(8,128)(2,1)S(1)}, bf16[128,1152]{1,0:T(8,128)(2,1)S(1)}) custom-call(s32[1]{0:T(128)} %bitcast.place_ref, bf16[128,1152]{1,0:T(8,128)(2,1)S(1)} %get-tuple-element.42.cur_ref.old_ref, bf16[128,1152]{1,0:T(8,128)(2,1)S(1)} %get-tuple-element.43.mine_ref, bf16[128,1152]{1,0:T(8,128)(2,1)S(1)} %collective-permute-done.12.other_ref, ...), custom_call_target="tpu_custom_call" | custom-call | tf_op jit(solution)/shard_map/feed/pallas_call | solution.py:317
  65.3 1.3 %collective-permute-done.9.other_ref = bf16[128,1152]{1,0:T(8,128)(2,1)S(1)} collective-permute-done((bf16[128,1152]{1,0:T(8,128)(2,1)S(1)}, bf16[128,1152]{1,0:T(8,128)(2,1)S(1)}, u32[]{:S(2)}, u32[]{:S(2)}) %collective-permute-start.9) | collective-permute-done | bytes 294944 | tf_op jit(solution)/shard_map/ppermute | solution.py:476
  66.6 6.3 %attention.5 = (bf16[128,1152]{1,0:T(8,128)(2,1)S(1)}, bf16[128,1152]{1,0:T(8,128)(2,1)S(1)}) custom-call(s32[1]{0:T(128)} %bitcast.place_ref, bf16[128,1152]{1,0:T(8,128)(2,1)S(1)} %get-tuple-element.32.cur_ref.old_ref, bf16[128,1152]{1,0:T(8,128)(2,1)S(1)} %get-tuple-element.35.after_ref, bf16[128,1152]{1,0:T(8,128)(2,1)S(1)} %get-tuple-element.36.mine_ref, ...), custom_call_target="tpu_custom_call" | custom-call | tf_op jit(solution)/shard_map/attention/pallas_call | solution.py:252
  73.7 6.2 %attention.7 = (bf16[128,1152]{1,0:T(8,128)(2,1)S(1)}, bf16[128,1152]{1,0:T(8,128)(2,1)S(1)}) custom-call(s32[1]{0:T(128)} %bitcast.place_ref, bf16[128,1152]{1,0:T(8,128)(2,1)S(1)} %get-tuple-element.42.cur_ref.old_ref, bf16[128,1152]{1,0:T(8,128)(2,1)S(1)} %get-tuple-element.44.after_ref, bf16[128,1152]{1,0:T(8,128)(2,1)S(1)} %get-tuple-element.45.mine_ref, ...), custom_call_target="tpu_custom_call" | custom-call | tf_op jit(solution)/shard_map/attention/pallas_call | solution.py:252
  79.9 1.4 %collective-permute-start.14 = (bf16[128,1152]{1,0:T(8,128)(2,1)S(1)}, bf16[128,1152]{1,0:T(8,128)(2,1)S(1)}, u32[]{:S(2)}, u32[]{:S(2)}) collective-permute-start(bf16[128,1152]{1,0:T(8,128)(2,1)S(1)} %get-tuple-element.47.mine_ref), channel_id=1, source_target_pairs={{0,2},{2,0},{1,3},{3,1},{4,6},{6,4},{5,7},{7,5},{8,10},{10,8},{9,1... | collective-permute-start | bytes 884744 | tf_op jit(solution)/shard_map/ppermute | solution.py:484
  81.3 4.4 %feed.5 = (bf16[128,1152]{1,0:T(8,128)(2,1)S(1)}, bf16[128,576]{1,0:T(8,128)(2,1)S(1)}, bf16[128,576]{1,0:T(8,128)(2,1)S(1)}) custom-call(s32[1]{0:T(128)} %bitcast.place_ref, bf16[128,1152]{1,0:T(8,128)(2,1)S(1)} %get-tuple-element.37.cur_ref.refs_0_, bf16[128,1152]{1,0:T(8,128)(2,1)S(1)} %get-tuple-element.38.mine_ref, ...), custom_call_target="tpu_custom_call" | custom-call | tf_op jit(solution)/shard_map/feed/pallas_call | solution.py:317
  86.4 1.9 %collective-permute-done.14.other_ref = bf16[128,1152]{1,0:T(8,128)(2,1)S(1)} collective-permute-done((bf16[128,1152]{1,0:T(8,128)(2,1)S(1)}, bf16[128,1152]{1,0:T(8,128)(2,1)S(1)}, u32[]{:S(2)}, u32[]{:S(2)}) %collective-permute-start.14) | collective-permute-done | bytes 294944 | tf_op jit(solution)/shard_map/ppermute | solution.py:484
  88.3 4.4 %feed.7 = (bf16[128,1152]{1,0:T(8,128)(2,1)S(1)}, bf16[128,576]{1,0:T(8,128)(2,1)S(1)}, bf16[128,576]{1,0:T(8,128)(2,1)S(1)}) custom-call(s32[1]{0:T(128)} %bitcast.place_ref, bf16[128,1152]{1,0:T(8,128)(2,1)S(1)} %get-tuple-element.46.cur_ref.refs_4_, bf16[128,1152]{1,0:T(8,128)(2,1)S(1)} %get-tuple-element.47.mine_ref, ...), custom_call_target="tpu_custom_call" | custom-call | tf_op jit(solution)/shard_map/feed/pallas_call | solution.py:317
  92.7 1.5 %collective-permute-start.15 = (bf16[128,576]{1,0:T(8,128)(2,1)S(1)}, bf16[128,576]{1,0:T(8,128)(2,1)S(1)}, u32[]{:S(2)}, u32[]{:S(2)}) collective-permute-start(bf16[128,576]{1,0:T(8,128)(2,1)S(1)} %get-tuple-element.50), channel_id=1, source_target_pairs={{0,2},{2,0},{1,3},{3,1},{4,6},{6,4},{5,7},{7,5},{8,10},{10,8},{9,1... | collective-permute-start | bytes 442376 | tf_op jit(solution)/shard_map/ppermute | solution.py:490
  94.2 3.8 %collective-permute-done.15.refs_7_ = bf16[128,576]{1,0:T(8,128)(2,1)S(1)} collective-permute-done((bf16[128,576]{1,0:T(8,128)(2,1)S(1)}, bf16[128,576]{1,0:T(8,128)(2,1)S(1)}, u32[]{:S(2)}, u32[]{:S(2)}) %collective-permute-start.15) | collective-permute-done | bytes 147488 | tf_op jit(solution)/shard_map/ppermute | solution.py:490
  98.6 15.3 %all_to_all.10 = bf16[16,32,288]{2,1,0:T(8,128)(2,1)S(1)} all-to-all(bf16[16,32,288]{2,1,0:T(8,128)(2,1)S(1)} %bitcast.20), channel_id=1, replica_groups=mesh['frame'=8,'y'=2,'core'=2] {'frame','core'}, dimensions={0} | all-to-all | bytes 589824 | tf_op jit(solution)/shard_map/all_to_all | solution.py:494
  113.9 0.9 unpack.1
  (41 shorter events, 7.5 us)
Async XLA Ops:
  0.0 12.0 %copy-start = (bf16[2,64,288]{2,1,0:T(8,128)(2,1)S(1)}, bf16[2,64,288]{2,1,0:T(8,128)(2,1)}, u32[]{:S(2)}) copy-start(bf16[2,64,288]{2,1,0:T(8,128)(2,1)} %param.12) | copy-start | bytes 221188
  0.0 35.3 %copy-start.5 = (bf16[288,1152]{1,0:T(8,128)(2,1)S(1)}, bf16[288,1152]{1,0:T(8,128)(2,1)}, u32[]{:S(2)}) copy-start(bf16[288,1152]{1,0:T(8,128)(2,1)} %out_me.7) | copy-start | bytes 1990660
  0.0 51.9 %collective-permute-start.7 = (bf16[1152,1152]{1,0:T(8,128)(2,1)}, bf16[1152,1152]{1,0:T(8,128)(2,1)S(1)}, u32[]{:S(2)}, u32[]{:S(2)}) collective-permute-start(bf16[1152,1152]{1,0:T(8,128)(2,1)} %fc1_me.7), channel_id=1, source_target_pairs={{0,1},{1,0},{2,3},{3,2},{4,5},{5,4},{6,7},{7,6},{8,9},{9,8},{10,11... | collective-permute-start | bytes 7962632 | tf_op jit(solution)/shard_map/ppermute | solution.py:436
  0.5 51.4 %collective-permute-start.8 = (bf16[1152,1152]{1,0:T(8,128)(2,1)}, bf16[1152,1152]{1,0:T(8,128)(2,1)}, u32[]{:S(2)}, u32[]{:S(2)}) collective-permute-start(bf16[1152,1152]{1,0:T(8,128)(2,1)} %fc2_me.7), channel_id=1, source_target_pairs={{0,1},{1,0},{2,3},{3,2},{4,5},{5,4},{6,7},{7,6},{8,9},{9,8},{10,11... | collective-permute-start | bytes 7962632 | tf_op jit(solution)/shard_map/ppermute | solution.py:436
  0.5 34.8 %collective-permute-start.4 = (bf16[3,288,1152]{2,1,0:T(8,128)(2,1)}, bf16[3,288,1152]{2,1,0:T(8,128)(2,1)}, u32[]{:S(2)}, u32[]{:S(2)}) collective-permute-start(bf16[3,288,1152]{2,1,0:T(8,128)(2,1)} %bitcast.12), channel_id=1, source_target_pairs={{0,1},{1,0},{2,3},{3,2},{4,5},{5,4},{6,7},{7,6},{8,9},{9,8},{10,11... | collective-permute-start | bytes 5971976 | tf_op jit(solution)/shard_map/ppermute | solution.py:435
  2.5 1.0 copy-start.8
  3.8 0.7 copy-start.7
  4.5 19.3 %all-to-all-start = ((bf16[16,32,384]{2,1,0:T(8,128)(2,1)}), bf16[16,32,384]{2,1,0:T(8,128)(2,1)}, u32[]{:S(2)}, u32[]{:S(2)}) async-start(bf16[16,32,384]{2,1,0:T(8,128)(2,1)} %bitcast.18), calls=%async_computation | async-start | bytes 786432 | tf_op jit(solution)/shard_map/all_to_all | solution.py:442
  11.6 17.7 %collective-permute-start.5 = (bf16[288,1152]{1,0:T(8,128)(2,1)}, bf16[288,1152]{1,0:T(8,128)(2,1)}, u32[]{:S(2)}, u32[]{:S(2)}) collective-permute-start(bf16[288,1152]{1,0:T(8,128)(2,1)} %out_me.7), channel_id=1, source_target_pairs={{0,1},{1,0},{2,3},{3,2},{4,5},{5,4},{6,7},{7,6},{8,9},{9,8},{10,11... | collective-permute-start | bytes 1990664 | tf_op jit(solution)/shard_map/ppermute | solution.py:435
  12.0 3.1 %collective-permute-start.3 = (bf16[2,8,288]{2,1,0:T(8,128)(2,1)S(1)}, bf16[2,8,288]{2,1,0:T(8,128)(2,1)S(1)}, u32[]{:S(2)}, u32[]{:S(2)}) collective-permute-start(bf16[2,8,288]{2,1,0:T(8,128)(2,1)S(1)} %constant_dynamic-slice_fusion.f0), channel_id=1, source_target_pairs={{0,3},{1,2},{2,1},{3,0},{4,7},{5,6},{6,5},{7,4},{8,11},{9,10},{10,... | collective-permute-start | bytes 27656 | tf_op jit(solution)/shard_map/ppermute | solution.py:430
  15.1 3.7 %collective-permute-start.2 = (bf16[2,8,288]{2,1,0:T(8,128)(2,1)S(1)}, bf16[2,8,288]{2,1,0:T(8,128)(2,1)S(1)}, u32[]{:S(2)}, u32[]{:S(2)}) collective-permute-start(bf16[2,8,288]{2,1,0:T(8,128)(2,1)S(1)} %constant_dynamic-slice_fusion.f0), channel_id=1, source_target_pairs={{0,2},{2,0},{1,3},{3,1},{4,6},{6,4},{5,7},{7,5},{8,10},{10,8},{9,1... | collective-permute-start | bytes 27656 | tf_op jit(solution)/shard_map/ppermute | solution.py:429
  18.8 1.2 %collective-permute-start.1 = (bf16[2,8,288]{2,1,0:T(8,128)(2,1)S(1)}, bf16[2,8,288]{2,1,0:T(8,128)(2,1)S(1)}, u32[]{:S(2)}, u32[]{:S(2)}) collective-permute-start(bf16[2,8,288]{2,1,0:T(8,128)(2,1)S(1)} %constant_dynamic-slice_fusion.f0), channel_id=1, source_target_pairs={{0,1},{1,0},{2,3},{3,2},{4,5},{5,4},{6,7},{7,6},{8,9},{9,8},{10,11... | collective-permute-start | bytes 27656 | tf_op jit(solution)/shard_map/ppermute | solution.py:428
  23.9 11.4 %collective-permute-start = (bf16[8,2,32,384]{3,2,1,0:T(8,128)(2,1)}, bf16[8,2,32,384]{3,2,1,0:T(8,128)(2,1)}, u32[]{:S(2)}, u32[]{:S(2)}) collective-permute-start(bf16[8,2,32,384]{3,2,1,0:T(8,128)(2,1)} %bitcast.3.mine_ref), channel_id=1, source_target_pairs={{0,2},{2,0},{1,3},{3,1},{4,6},{6,4},{5,7},{7,5},{8,10},{10,8},{9,1... | collective-permute-start | bytes 1179656 | tf_op jit(solution)/shard_map/ppermute | solution.py:452
  26.9 1.5 %copy-start.6 = (f32[64,6,1152]{2,0,1:T(8,128)S(1)}, f32[64,6,1152]{2,0,1:T(8,128)}, u32[]{:S(2)}) copy-start(f32[64,6,1152]{2,0,1:T(8,128)} %param.15) | copy-start | bytes 5308420
  35.3 1.6 %copy-start.3 = (bf16[3,1152,288]{1,2,0:T(8,128)(2,1)S(1)}, bf16[3,1152,288]{1,2,0:T(8,128)(2,1)}, u32[]{:S(2)}) copy-start(bf16[3,1152,288]{1,2,0:T(8,128)(2,1)} %param.18) | copy-start | bytes 5971972
  43.2 8.7 %copy-start.1 = (bf16[1152,1152]{1,0:T(8,128)(2,1)S(1)}, bf16[1152,1152]{1,0:T(8,128)(2,1)}, u32[]{:S(2)}) copy-start(bf16[1152,1152]{1,0:T(8,128)(2,1)} %fc1_me.7) | copy-start | bytes 7962628
  43.2 8.7 %copy-start.2 = (bf16[1152,1152]{1,0:T(8,128)(2,1)S(1)}, bf16[1152,1152]{1,0:T(8,128)(2,1)}, u32[]{:S(2)}) copy-start(bf16[1152,1152]{1,0:T(8,128)(2,1)} %fc2_me.7) | copy-start | bytes 7962628
  43.2 8.7 %collective-permute-start.6 = (bf16[128,1152]{1,0:T(8,128)(2,1)S(1)}, bf16[128,1152]{1,0:T(8,128)(2,1)S(1)}, u32[]{:S(2)}, u32[]{:S(2)}) collective-permute-start(bf16[128,1152]{1,0:T(8,128)(2,1)S(1)} %get-tuple-element.33.mine_ref), channel_id=1, source_target_pairs={{0,2},{2,0},{1,3},{3,1},{4,6},{6,4},{5,7},{7,5},{8,10},{10,8},{9,1... | collective-permute-start | bytes 884744 | tf_op jit(solution)/shard_map/ppermute | solution.py:472
  51.0 10.0 %collective-permute-start.12 = (bf16[128,1152]{1,0:T(8,128)(2,1)S(1)}, bf16[128,1152]{1,0:T(8,128)(2,1)S(1)}, u32[]{:S(2)}, u32[]{:S(2)}) collective-permute-start(bf16[128,1152]{1,0:T(8,128)(2,1)S(1)} %get-tuple-element.43.mine_ref), channel_id=1, source_target_pairs={{0,2},{2,0},{1,3},{3,1},{4,6},{6,4},{5,7},{7,5},{8,10},{10,8},{9,1... | collective-permute-start | bytes 884744 | tf_op jit(solution)/shard_map/ppermute | solution.py:472
  56.0 10.7 %collective-permute-start.9 = (bf16[128,1152]{1,0:T(8,128)(2,1)S(1)}, bf16[128,1152]{1,0:T(8,128)(2,1)S(1)}, u32[]{:S(2)}, u32[]{:S(2)}) collective-permute-start(bf16[128,1152]{1,0:T(8,128)(2,1)S(1)} %get-tuple-element.36.mine_ref), channel_id=1, source_target_pairs={{0,2},{2,0},{1,3},{3,1},{4,6},{6,4},{5,7},{7,5},{8,10},{10,8},{9,1... | collective-permute-start | bytes 884744 | tf_op jit(solution)/shard_map/ppermute | solution.py:476
  61.0 5.6 %copy-start.4 = (bf16[3,1152,288]{1,2,0:T(8,128)(2,1)S(1)}, bf16[3,1152,288]{1,2,0:T(8,128)(2,1)}, u32[]{:S(2)}) copy-start(bf16[3,1152,288]{1,2,0:T(8,128)(2,1)} %param.18) | copy-start | bytes 5971972
  65.2 8.5 %collective-permute-start.13 = (bf16[128,1152]{1,0:T(8,128)(2,1)S(1)}, bf16[128,1152]{1,0:T(8,128)(2,1)S(1)}, u32[]{:S(2)}, u32[]{:S(2)}) collective-permute-start(bf16[128,1152]{1,0:T(8,128)(2,1)S(1)} %get-tuple-element.45.mine_ref), channel_id=1, source_target_pairs={{0,2},{2,0},{1,3},{3,1},{4,6},{6,4},{5,7},{7,5},{8,10},{10,8},{9,1... | collective-permute-start | bytes 884744 | tf_op jit(solution)/shard_map/ppermute | solution.py:476
  73.0 8.3 %collective-permute-start.10 = (bf16[128,1152]{1,0:T(8,128)(2,1)S(1)}, bf16[128,1152]{1,0:T(8,128)(2,1)S(1)}, u32[]{:S(2)}, u32[]{:S(2)}) collective-permute-start(bf16[128,1152]{1,0:T(8,128)(2,1)S(1)} %get-tuple-element.38.mine_ref), channel_id=1, source_target_pairs={{0,2},{2,0},{1,3},{3,1},{4,6},{6,4},{5,7},{7,5},{8,10},{10,8},{9,1... | collective-permute-start | bytes 884744 | tf_op jit(solution)/shard_map/ppermute | solution.py:484
  79.9 8.4 %collective-permute-start.14 = (bf16[128,1152]{1,0:T(8,128)(2,1)S(1)}, bf16[128,1152]{1,0:T(8,128)(2,1)S(1)}, u32[]{:S(2)}, u32[]{:S(2)}) collective-permute-start(bf16[128,1152]{1,0:T(8,128)(2,1)S(1)} %get-tuple-element.47.mine_ref), channel_id=1, source_target_pairs={{0,2},{2,0},{1,3},{3,1},{4,6},{6,4},{5,7},{7,5},{8,10},{10,8},{9,1... | collective-permute-start | bytes 884744 | tf_op jit(solution)/shard_map/ppermute | solution.py:484
  85.7 8.5 %collective-permute-start.11 = (bf16[128,576]{1,0:T(8,128)(2,1)S(1)}, bf16[128,576]{1,0:T(8,128)(2,1)S(1)}, u32[]{:S(2)}, u32[]{:S(2)}) collective-permute-start(bf16[128,576]{1,0:T(8,128)(2,1)S(1)} %get-tuple-element.41), channel_id=1, source_target_pairs={{0,2},{2,0},{1,3},{3,1},{4,6},{6,4},{5,7},{7,5},{8,10},{10,8},{9,1... | collective-permute-start | bytes 442376 | tf_op jit(solution)/shard_map/ppermute | solution.py:490
  92.7 5.3 %collective-permute-start.15 = (bf16[128,576]{1,0:T(8,128)(2,1)S(1)}, bf16[128,576]{1,0:T(8,128)(2,1)S(1)}, u32[]{:S(2)}, u32[]{:S(2)}) collective-permute-start(bf16[128,576]{1,0:T(8,128)(2,1)S(1)} %get-tuple-element.50), channel_id=1, source_target_pairs={{0,2},{2,0},{1,3},{3,1},{4,6},{6,4},{5,7},{7,5},{8,10},{10,8},{9,1... | collective-permute-start | bytes 442376 | tf_op jit(solution)/shard_map/ppermute | solution.py:490

commit v3 on v2

v3 whole, which is shorter than its diff:
```python
import functools
import math

import jax
import jax.numpy as jnp
from jax import lax
from jax.experimental import pallas as pl
from jax.experimental.pallas import tpu as pltpu
from jax.sharding import Mesh, PartitionSpec as P

HD = 72
W = 8
OFFSETS = 2 * W + 1
EPSILON = 1e-06
F32 = jnp.float32
BF16 = jnp.bfloat16
LANES = 128
VMEM_SPEC = pl.BlockSpec(memory_space=pltpu.VMEM)
SMEM_SPEC = pl.BlockSpec(memory_space=pltpu.SMEM)
HBM_SPEC = pl.BlockSpec(memory_space=pltpu.HBM)


def in_hbm(*arrays):
    return [pltpu.with_memory_space_constraint(array, pltpu.HBM) for array in arrays]


def params(*arrays):
    held = sum(math.prod(a.shape) * jnp.dtype(a.dtype).itemsize for a in arrays)
    return pltpu.CompilerParams(vmem_limit_bytes=held + 8 * 1024 * 1024)


def tiles_of(share):
    return share // LANES, share % LANES


def normalise(values, shift_rows, scale_rows):
    center = values - jnp.mean(values, axis=-1, keepdims=True)
    spread = jnp.mean(center * center, axis=-1, keepdims=True)
    return center * lax.rsqrt(spread + EPSILON) * (1.0 + scale_rows) + shift_rows


def payload_kernel(
    frames, frame_far, level_far, window_far, x_far, fresh_far, out_ref,
    rows_ref, frame_ref, level_ref, window_ref, x_ref, fresh_ref, sems,
):
    fars = (x_far, window_far, level_far, frame_far, fresh_far)
    nears = (x_ref, window_ref, level_ref, frame_ref, fresh_ref)
    copies = [pltpu.make_async_copy(a, b, sems.at[n]) for n, (a, b) in enumerate(zip(fars, nears))]
    for copy in copies:
        copy.start()
    for copy in copies:
        copy.wait()
    here, _, share = x_ref.shape
    targets, chunks, _, _ = out_ref.shape
    full, rest = tiles_of(share)
    size = x_ref.shape[1] // (targets * chunks)
    row = lax.broadcasted_iota(jnp.int32, (here, 1), 0)
    level = jnp.zeros((here, 1), jnp.int32)
    for i in range(here):
        level = jnp.where(row == i, level_ref[i], level)
    offset = lax.broadcasted_iota(jnp.int32, (here, OFFSETS), 1)
    position = frame_ref[0] * here + row + offset - W
    allowed = (window_ref[...] == 1) & (position >= 0) & (position < frames)
    meta = jnp.concatenate([level.astype(F32), allowed.astype(jnp.int32).astype(F32)], axis=1)
    tokens = x_ref.shape[1]
    piece = share // here
    blank = LANES - size * rest - 1 - OFFSETS - piece
    later = fresh_ref[1].astype(F32)
    for j in range(here):
        cut = later[:, j * piece : (j + 1) * piece]
        cut = jnp.concatenate([cut, jnp.zeros((tokens, LANES - piece), F32)], axis=1)
        rows_ref[full + 1, pl.ds(j, tokens, stride=here), :] = cut
    sent = lax.rem(frame_ref[0], size)
    for i in range(here):
        value = x_ref[i].astype(F32)
        if i == here - 1:
            leaves = (frame_ref[0] + 1) * here == frames
            value = jnp.where(leaves, fresh_ref[0].astype(F32), value)
        for t in range(full):
            rows_ref[t, pl.ds(i, tokens, stride=here), :] = value[:, t * LANES : (t + 1) * LANES]
        rows_ref[full, pl.ds(i, tokens, stride=here), :] = jnp.concatenate(
            [value[:, full * LANES :], jnp.zeros((tokens, LANES - rest), F32)], axis=1
        )
    for d in range(targets):
        for n in range(chunks):
            first = (d * chunks + n) * size * here
            pieces = [rows_ref[t, first : first + size * here, :] for t in range(full)]
            tails = [
                rows_ref[full, first + p * here : first + (p + 1) * here, :][:, :rest]
                for p in range(size)
            ]
            cuts = [
                rows_ref[full + 1, first + p * here : first + (p + 1) * here, :][:, :piece]
                for p in range(size)
            ]
            cut = cuts[0]
            for p in range(1, size):
                cut = jnp.where(sent == p, cuts[p], cut)
            tails += [meta, cut]
            if blank:
                tails.append(jnp.zeros((here, blank), F32))
            pieces.append(jnp.concatenate(tails, axis=1))
            out_ref[d, n] = jnp.concatenate(pieces, axis=0).astype(BF16)


def make_payload(frame_index, noise_level, window_mask, x, fresh, frames, targets, chunks):
    here, tokens, share = x.shape
    full, rest = tiles_of(share)
    size = tokens // (targets * chunks)
    out = jax.ShapeDtypeStruct((targets, chunks, (full * size + 1) * here, LANES), BF16)
    scratch = jax.ShapeDtypeStruct((full + 2, tokens * here, LANES), F32)
    return pl.pallas_call(
        functools.partial(payload_kernel, frames),
        out_shape=out,
        in_specs=[HBM_SPEC] * 5,
        out_specs=VMEM_SPEC,
        scratch_shapes=[
            pltpu.VMEM(scratch.shape, F32),
            pltpu.SMEM(frame_index.shape, jnp.int32),
            pltpu.SMEM(noise_level.shape, jnp.int32),
            pltpu.VMEM(window_mask.shape, jnp.int32),
            pltpu.VMEM(x.shape, BF16),
            pltpu.VMEM(fresh.shape, BF16),
            pltpu.SemaphoreType.DMA((5,)),
        ],
        compiler_params=params(x, fresh, out, scratch),
        name="payload",
    )(*in_hbm(frame_index, noise_level, window_mask, x, fresh))


def fresh_piece(block, size, here, share):
    _, rest = tiles_of(share)
    piece = share // here
    first = size * rest + 1 + OFFSETS
    tail = block[-here:, first : first + piece]
    return jnp.concatenate([tail[j : j + 1] for j in range(here)], axis=1)


def chunk_rows(block, size, here, share):
    full, rest = tiles_of(share)
    tail = block[full * size * here :]
    result = []
    for p in range(size):
        pieces = [block[(t * size + p) * here : (t * size + p + 1) * here] for t in range(full)]
        result.append(jnp.concatenate(pieces + [tail[:, p * rest : (p + 1) * rest]], axis=1))
    return result


def prepare_kernel(
    here, lane_at, place_ref, received_ref, table_ref, keep_ref, layer_ref,
    norm_ref, feed_ref, gate_ref, pair_ref, mask_ref, flag_ref,
):
    flag_ref[...] = jnp.where(place_ref[0] < 2, jnp.ones_like(flag_ref), 0.0)
    groups = received_ref.shape[0]
    frames = groups * here
    levels = table_ref.shape[1]
    meta = [received_ref[g, 0].astype(F32)[-here:, lane_at:] for g in range(groups)]
    meta = jnp.concatenate(meta, axis=0)
    level = meta[:, 0:1]
    ids = lax.broadcasted_iota(jnp.int32, (frames, levels), 1).astype(F32)
    hot = level == ids
    hot_bf = hot.astype(BF16)
    targets = [(norm_ref, 0), (norm_ref, 1), (feed_ref, 0), (feed_ref, 1), (feed_ref, 2), (gate_ref, 0)]
    for j, (target, at) in enumerate(targets):
        rows = table_ref[j]
        high = rows.astype(BF16)
        rest = rows - high.astype(F32)
        middle = rest.astype(BF16)
        low = (rest - middle.astype(F32)).astype(BF16)
        total = jnp.dot(hot_bf, high, preferred_element_type=F32)
        total += jnp.dot(hot_bf, middle, preferred_element_type=F32)
        total += jnp.dot(hot_bf, low, preferred_element_type=F32)
        target[at] = total
    keep = jnp.sum(jnp.where(hot, keep_ref[...], 0.0), axis=1, keepdims=True)
    layer = jnp.sum(jnp.where(hot, layer_ref[...], 0.0), axis=1, keepdims=True)
    lane = lax.broadcasted_iota(jnp.int32, (frames, LANES), 1)
    pair_ref[...] = jnp.where(lane == 0, keep, layer)

    block = mask_ref.shape[0]
    row = lax.broadcasted_iota(jnp.int32, (frames, block), 0)
    column = lax.broadcasted_iota(jnp.int32, (frames, block), 1)
    for t in range(block // frames):
        distance = column - t * frames - row
        inside = (column >= t * frames) & (column < (t + 1) * frames)
        is_open = jnp.zeros((frames, block), F32)
        for o in range(OFFSETS):
            is_open = jnp.where(distance == o - W, meta[:, 1 + o : 2 + o], is_open)
        mask_ref[t * frames : (t + 1) * frames, :] = jnp.where(inside, is_open, 0.0)


def prepare(place, received, table, keep, layer, here, lane_at, block):
    frames = received.shape[0] * here
    features = table.shape[2]
    outs = (
        jax.ShapeDtypeStruct((2, frames, features), F32),
        jax.ShapeDtypeStruct((3, frames, features), F32),
        jax.ShapeDtypeStruct((1, frames, features), F32),
        jax.ShapeDtypeStruct((frames, LANES), F32),
        jax.ShapeDtypeStruct((block, block), F32),
        jax.ShapeDtypeStruct((8, LANES), F32),
    )
    return pl.pallas_call(
        functools.partial(prepare_kernel, here, lane_at),
        out_shape=outs,
        in_specs=[SMEM_SPEC] + [VMEM_SPEC] * 4,
        out_specs=(VMEM_SPEC,) * len(outs),
        compiler_params=params(received, table, *outs),
        name="prepare",
    )(place, received, table, keep.reshape(1, -1), layer.reshape(1, -1))


def hold_kernel(places, *refs):
    sources, targets, sems = refs[: len(places)], refs[len(places) : -1], refs[-1]
    copies = []
    for source, (index, start) in zip(sources, places):
        rows = source.shape[0]
        parts = 3 if rows % 48 == 0 or rows % 3 == 0 and len(source.shape) > 2 else 1
        for n in range(parts):
            size = rows // parts
            copies.append(
                pltpu.make_async_copy(
                    source.at[pl.ds(n * size, size)],
                    targets[index].at[pl.ds(start + n * size, size)],
                    sems.at[len(copies)],
                )
            )
            copies[-1].start()
    for copy in copies:
        copy.wait()


def hold(*groups):
    places, outs = [], []
    for index, group in enumerate(groups):
        start = 0
        for array in group:
            places.append((index, start))
            start += array.shape[0]
        outs.append(jax.ShapeDtypeStruct((start,) + group[0].shape[1:], group[0].dtype))
    arrays = [array for group in groups for array in group]
    held = sum(math.prod(o.shape) * jnp.dtype(o.dtype).itemsize for o in outs)
    return pl.pallas_call(
        functools.partial(hold_kernel, tuple(places)),
        out_shape=tuple(outs),
        in_specs=[HBM_SPEC] * len(arrays),
        out_specs=(VMEM_SPEC,) * len(outs),
        scratch_shapes=[pltpu.SemaphoreType.DMA((3 * len(arrays),))],
        compiler_params=params(*outs),
        cost_estimate=pl.CostEstimate(flops=0, bytes_accessed=2 * held, transcendentals=0),
        name="hold",
    )(*in_hbm(*arrays))


def attention_rows(current, norm_ref, mask_ref, weights, out_ref):
    normed = [normalise(rows, norm_ref[0], norm_ref[1]).astype(BF16) for rows in current]
    normed = normed[0] if len(normed) == 1 else jnp.concatenate(normed, axis=0)
    qkv_me, qkv_other = weights
    share = qkv_me.shape[1]
    heads = share // HD
    block = mask_ref.shape[0]
    count = normed.shape[0] // block
    is_open = mask_ref[...] > 0.5
    lane = lax.broadcasted_iota(jnp.int32, (1, share), 1)
    head_lanes = [
        ((lane >= HD * h) & (lane < HD * (h + 1))).astype(jnp.int32).astype(F32).astype(BF16)
        for h in range(heads)
    ]
    scale = math.log2(math.e) / math.sqrt(HD)
    projected = []
    for side, qkv in enumerate((qkv_me, qkv_other)):
        projected.append(
            [
                lax.dot_general(
                    normed, qkv[t], (((1,), (1,)), ((), ())), preferred_element_type=F32
                ).astype(BF16)
                for t in range(3)
            ]
        )
    units = [(side, slice(b * block, (b + 1) * block)) for side in range(2) for b in range(count)]
    scores = []
    for side, at in units:
        query, key = projected[side][0][at], projected[side][1][at]
        keys = jnp.concatenate([key * lanes for lanes in head_lanes], axis=0)
        raw = lax.dot_general(query, keys, (((1,), (1,)), ((), ())), preferred_element_type=F32)
        scores += [
            jnp.where(is_open, raw[:, h * block : (h + 1) * block], -1e30) for h in range(heads)
        ]
    tops = [jnp.max(s, axis=-1, keepdims=True) for s in scores]
    weights_of = [jnp.exp2((s - t) * scale) for s, t in zip(scores, tops)]
    sums = [jnp.sum(w, axis=-1, keepdims=True) for w in weights_of]
    shares = [(w / total).astype(BF16) for w, total in zip(weights_of, sums)]
    attended = []
    for n, (side, at) in enumerate(units):
        value = projected[side][2][at]
        values = jnp.concatenate([value * lanes for lanes in head_lanes], axis=0)
        row = jnp.concatenate(shares[n * heads : (n + 1) * heads], axis=1)
        attended.append(jnp.dot(row, values, preferred_element_type=F32).astype(BF16))
    for n, (side, at) in enumerate(units):
        out_ref[at, side * share : (side + 1) * share] = attended[n]


def shifted_in(rows, fresh_row):
    frames = rows.shape[0]
    first = lax.broadcasted_iota(jnp.int32, (frames, 1), 0) == 0
    return jnp.where(first, fresh_row, pltpu.roll(rows, 1, 0))


def first_attention_kernel(
    count, mine_ref, other_ref, flag_ref, norm_ref, mask_ref,
    qkv_me, qkv_other, cur_ref, part_ref, fresh_ref,
):
    groups, cores = mine_ref.shape[:2]
    frames = norm_ref.shape[1]
    here = frames // groups
    share = qkv_me.shape[1]
    first_half = flag_ref[0:1, :] > 0.5
    blocks = []
    for g in range(groups):
        left, right = [], []
        for c in range(cores):
            mine, other = mine_ref[g, c].astype(F32), other_ref[g, c].astype(F32)
            left.append(jnp.where(first_half, mine, other))
            right.append(jnp.where(first_half, other, mine))
        if g < count:
            cuts = [fresh_piece(block, count, here, share) for block in left + right]
            fresh_ref[g : g + 1, :] = jnp.concatenate(cuts, axis=1)
        blocks.append([chunk_rows(block, count, here, share) for block in left + right])
    current = []
    for p in range(count):
        rows = [jnp.concatenate([part[p] for part in parts], axis=1) for parts in blocks]
        rows = pltpu.roll(jnp.concatenate(rows, axis=0), 1, 0)
        cur_ref[p * frames : (p + 1) * frames, :] = rows.astype(BF16)
        current.append(rows)
    attention_rows(current, norm_ref, mask_ref, (qkv_me, qkv_other), part_ref)


def next_attention_kernel(
    count, old_ref, after_ref, mine_ref, other_ref, fresh_ref, norm_ref, gate_ref, pair_ref,
    mask_ref, qkv_me, qkv_other, cur_ref, part_ref,
):
    frames = norm_ref.shape[1]
    keep, layer = pair_ref[:, 0:1], pair_ref[:, 1:2]
    current = []
    for p in range(count):
        at = slice(p * frames, (p + 1) * frames)
        total = mine_ref[at, :].astype(F32) + other_ref[at, :].astype(F32)
        rows = keep * old_ref[at, :].astype(F32) + layer * (
            after_ref[at, :].astype(F32) + gate_ref[0] * total
        )
        rows = shifted_in(rows, fresh_ref[p : p + 1, :]).astype(BF16)
        cur_ref[at, :] = rows
        current.append(rows.astype(F32))
    attention_rows(current, norm_ref, mask_ref, (qkv_me, qkv_other), part_ref)


def attention_call(kernel, arrays, rows, features, fresh_count=0):
    outs = (
        jax.ShapeDtypeStruct((rows, features), BF16),
        jax.ShapeDtypeStruct((rows, features // 2), BF16),
    )
    if fresh_count:
        outs += (jax.ShapeDtypeStruct((fresh_count, features), F32),)
    return pl.pallas_call(
        kernel,
        out_shape=outs,
        in_specs=[VMEM_SPEC] * len(arrays),
        out_specs=(VMEM_SPEC,) * len(outs),
        compiler_params=params(*arrays, *outs),
        name="attention",
    )(*arrays)


def gelu(x):
    inner = math.sqrt(2.0 / math.pi) * (x + 0.044715 * (x * x * x))
    return x * (0.5 * (1.0 + jnp.tanh(inner)))


def pieces_of(width, size):
    return [(s, min(size, width - s)) for s in range(0, width, size)]


def feed_kernel(
    halves, flag_ref, cur_ref, mine_ref, other_ref, mod_ref,
    out_all, fc1_me, fc1_other, fc2_me, fc2_other, *rest,
):
    outs, hidden_ref = rest[:-1], rest[-1]
    after_ref = outs[0]
    frames = mod_ref.shape[1]
    tokens = cur_ref.shape[0] // frames
    normed = []
    half = mine_ref.shape[1]
    attention_total = jnp.dot(mine_ref[...], out_all[:half], preferred_element_type=F32) + jnp.dot(
        other_ref[...], out_all[half:], preferred_element_type=F32
    )
    for p in range(tokens):
        at = slice(p * frames, (p + 1) * frames)
        after = (cur_ref[at, :].astype(F32) + mod_ref[0] * attention_total[at]).astype(BF16)
        after_ref[at, :] = after
        normed.append(normalise(after.astype(F32), mod_ref[1], mod_ref[2]).astype(BF16))
    normed = normed[0] if tokens == 1 else jnp.concatenate(normed, axis=0)
    units, features = fc2_me.shape
    for side, w1 in enumerate((fc1_me, fc1_other)):
        for start, size in pieces_of(units, 256):
            hidden = gelu(
                jnp.dot(normed, w1[:, start : start + size], preferred_element_type=F32)
            )
            hidden_ref[:, side * units + start : side * units + start + size] = hidden.astype(BF16)

    def product(at):
        return jnp.dot(
            hidden_ref[:, :units], fc2_me[:, at], preferred_element_type=F32
        ) + jnp.dot(hidden_ref[:, units:], fc2_other[:, at], preferred_element_type=F32)

    if not halves:
        for start, size in pieces_of(features, 256):
            at = slice(start, start + size)
            outs[1][:, at] = product(at).astype(BF16)
        return
    total = product(slice(None))
    left, right = total[:, : features // 2], total[:, features // 2 :]
    first_half = flag_ref[0:1, 0:1] > 0.5
    outs[1][...] = jnp.where(first_half, left, right).astype(BF16)
    outs[2][...] = jnp.where(first_half, right, left).astype(BF16)


def feed_call(flag, cur, mine, other, mod, weights, halves):
    rows, features = cur.shape
    shape = jax.ShapeDtypeStruct((rows, features), BF16)
    half = jax.ShapeDtypeStruct((rows, features // 2), BF16)
    outs = (shape, half, half) if halves else (shape, shape)
    return pl.pallas_call(
        functools.partial(feed_kernel, halves),
        out_shape=outs,
        in_specs=[VMEM_SPEC] * 10,
        out_specs=(VMEM_SPEC,) * len(outs),
        scratch_shapes=[pltpu.VMEM((rows, 2 * weights[1].shape[1]), BF16)],
        compiler_params=params(cur, mine, other, mod, *weights, *outs),
        name="feed",
    )(flag, cur, mine, other, mod, *weights)


def finish_kernel(chunks, flag_ref, gate_ref, pair_ref, *refs):
    out_ref = refs[-1]
    groups, cores = out_ref.shape[:2]
    _, frames, features = gate_ref.shape
    here = frames // groups
    half = features // 2
    share = half // cores
    full, rest = tiles_of(share)
    first_half = flag_ref[0:1, 0:1] > 0.5
    keep, layer = pair_ref[:, 0:1], pair_ref[:, 1:2]

    def mine(value):
        return jnp.where(first_half, value[:, :half], value[:, half:])

    gate = mine(gate_ref[0])
    results = []
    for n in range(chunks):
        old_ref, after_ref, mine_ref, other_ref = refs[4 * n : 4 * n + 4]
        for p in range(old_ref.shape[0] // frames):
            at = slice(p * frames, (p + 1) * frames)
            total = mine_ref[at, :].astype(F32) + other_ref[at, :].astype(F32)
            results.append(
                keep * mine(old_ref[at, :].astype(F32))
                + layer * (mine(after_ref[at, :].astype(F32)) + gate * total)
            )
    unused = LANES - len(results) * rest
    for c in range(cores):
        shares = [r[:, c * share : (c + 1) * share] for r in results]
        for g in range(groups):
            rows = [s[g * here : (g + 1) * here] for s in shares]
            pieces = [r[:, t * LANES : (t + 1) * LANES] for t in range(full) for r in rows]
            tails = [r[:, full * LANES :] for r in rows]
            if unused:
                tails.append(jnp.zeros((here, unused), F32))
            pieces.append(jnp.concatenate(tails, axis=1))
            out_ref[g, c] = jnp.concatenate(pieces, axis=0).astype(BF16)


def finish(flag, gate, pair, parts, groups):
    _, frames, features = gate.shape
    tokens = sum(part[0].shape[0] for part in parts) // frames
    full, _ = tiles_of(features // 4)
    arrays = [array for part in parts for array in part]
    out = jax.ShapeDtypeStruct((groups, 2, (full * tokens + 1) * (frames // groups), LANES), BF16)
    return pl.pallas_call(
        functools.partial(finish_kernel, len(parts)),
        out_shape=out,
        in_specs=[VMEM_SPEC] * (3 + len(arrays)),
        out_specs=VMEM_SPEC,
        compiler_params=params(gate, pair, out, *arrays),
        name="finish",
    )(flag, gate, pair, *arrays)


def unpack_kernel(rows_ref, out_ref, wide_ref):
    here, tokens, share = out_ref.shape
    sources = rows_ref.shape[0]
    size = tokens // sources
    full, rest = tiles_of(share)
    for d in range(sources):
        block = rows_ref[d].astype(F32)
        first = d * size * here
        for t in range(full):
            wide_ref[t, first : first + size * here, :] = block[t * size * here : (t + 1) * size * here]
        tail = block[full * size * here :]
        for p in range(size):
            wide_ref[full, first + p * here : first + (p + 1) * here, :rest] = tail[
                :, p * rest : (p + 1) * rest
            ]
    for i in range(here):
        pieces = [wide_ref[t, pl.ds(i, tokens, stride=here), :] for t in range(full + 1)]
        out_ref[i] = jnp.concatenate(pieces, axis=1)[:, :share].astype(BF16)


def unpack(rows, here, tokens, share):
    full, _ = tiles_of(share)
    out = jax.ShapeDtypeStruct((here, tokens, share), BF16)
    scratch = jax.ShapeDtypeStruct((full + 1, tokens * here, LANES), F32)
    return pl.pallas_call(
        unpack_kernel,
        out_shape=out,
        in_specs=[VMEM_SPEC],
        out_specs=VMEM_SPEC,
        scratch_shapes=[pltpu.VMEM(scratch.shape, F32)],
        compiler_params=params(rows, out, scratch),
        name="unpack",
    )(rows)


SWAP = [(0, 1), (1, 0)]


def on_device(
    latents, fresh, noise_level, window_mask, mod_table, keep_coef, layer_coef,
    w_qkv, w_out, w_fc1, w_fc2,
):
    here, tokens_all, share = latents.shape
    features = mod_table.shape[2]
    groups = lax.axis_size("frame")
    frames = groups * here
    frame_index = lax.axis_index("frame")
    y_index, core_index = lax.axis_index("y"), lax.axis_index("core")
    place = (2 * y_index + core_index).astype(jnp.int32).reshape(1)
    group_tokens = tokens_all // groups
    split = group_tokens % 2 == 0
    tokens = group_tokens // 2 if split else group_tokens
    block = max(frames, LANES)
    chunk_count = 2 if tokens % 2 == 0 and tokens * frames // 2 % block == 0 else 1
    size = tokens // chunk_count
    rows = size * frames

    swap_core = functools.partial(lax.ppermute, axis_name="core", perm=SWAP)
    swap_y = functools.partial(lax.ppermute, axis_name="y", perm=SWAP)
    w_qkv = jnp.swapaxes(w_qkv, 1, 2)
    out_far = swap_y(w_out)
    table, w_qkv, qkv_other, fc2_other, out_all = hold(
        (jnp.swapaxes(mod_table, 0, 1),),
        (w_qkv,),
        (swap_core(w_qkv),),
        (swap_core(w_fc2),),
        (w_out, swap_core(w_out), out_far, swap_core(out_far)),
    )
    attention_weights = (w_qkv, qkv_other)
    feed_weights = (out_all, w_fc1, swap_core(w_fc1), w_fc2, fc2_other)

    payload = make_payload(
        frame_index.astype(jnp.int32).reshape(1), noise_level, window_mask, latents, fresh,
        frames, tokens_all // tokens, chunk_count,
    )
    if split:
        received = lax.all_to_all(payload, ("frame", "core"), 0, 0, tiled=True)
        received = received.reshape((groups, 2) + received.shape[1:])
    else:
        received = lax.all_to_all(payload, "frame", 0, 0, tiled=True)
        partner = swap_core(received)
        first = core_index == 0
        received = jnp.stack(
            [jnp.where(first, received, partner), jnp.where(first, partner, received)], axis=1
        )
    arrived = [received[:, :, n] for n in range(chunk_count)]
    arrived_other = [swap_y(part) for part in arrived]
    norm_mod, feed_mod, gate_mod, pair, mask, flag = prepare(
        place, arrived[0], table, keep_coef, layer_coef, here, size * tiles_of(share)[1], block
    )

    state = []
    for mine, other in zip(arrived, arrived_other):
        current, part, later = attention_call(
            functools.partial(first_attention_kernel, size),
            (mine, other, flag, norm_mod, mask) + attention_weights,
            rows, features, size,
        )
        state.append((current, part, swap_y(part), later))
    fed = []
    for current, part, part_other, later in state:
        after, feed = feed_call(flag, current, part, part_other, feed_mod, feed_weights, False)
        fed.append((current, after, feed, swap_y(feed), later))
    state = []
    for arrays in fed:
        current, part = attention_call(
            functools.partial(next_attention_kernel, size),
            arrays + (norm_mod, gate_mod, pair, mask) + attention_weights,
            rows, features,
        )
        state.append((current, part, swap_y(part)))
    parts = []
    for current, part, part_other in state:
        after, feed_here, feed_there = feed_call(
            flag, current, part, part_other, feed_mod, feed_weights, True
        )
        parts.append((current, after, feed_here, swap_y(feed_there)))
    result = finish(flag, gate_mod, pair, parts, groups)
    if split:
        result = result.reshape((groups * 2,) + result.shape[2:])
        result = lax.all_to_all(result, ("frame", "core"), 0, 0, tiled=True)
    else:
        result = jnp.where(core_index == 0, result[:, 0], result[:, 1])
        result = lax.all_to_all(result, "frame", 0, 0, tiled=True)
    return unpack(result, here, tokens_all, share)


def solution(mesh):
    groups, heads = mesh.shape["frame"], mesh.shape["head"]
    inner = Mesh(mesh.devices.reshape(groups, heads // 2, 2), ("frame", "y", "core"))
    head = ("y", "core")
    in_specs = (
        P("frame", None, head),
        P(None, None, head),
        P("frame"),
        P("frame", None),
        P(),
        P(),
        P(),
        P(None, None, head),
        P(head, None),
        P(None, head),
        P(head, None),
    )
    return jax.shard_map(
        on_device, mesh=inner, in_specs=in_specs, out_specs=P("frame", None, head), check_vma=False
    )
```

time: 115 us -> 92 us (0.80)
  Pallas kernels: 44.6 us -> 32.3 us
  local copies, waits for them, and re-layouts: 6.32 us -> 0.08 us
  starting transfers between devices: 20.9 us -> 18.2 us
  other arithmetic: 1.52 us -> 0 us
    pallas_call x8 -> x9, Pallas kernels: 27.7 us -> 20.4 us  [the longest x4 11.3 us: attention_call(): pl.pallas_call(kernel, out_shape=outs, in_specs=[VMEM_SPEC] * len(arrays)...]
    pallas_call x4, Pallas kernels: 17 us -> 11.9 us  [feed_call(): pl.pallas_call(functools.partial(feed_kernel, halves), out_shape=outs, in...]
    unnamed x18 -> x8, local copies, waits for them, and re-layouts: 4.79 us -> 0.02 us
    ppermute x4 -> x2, starting transfers between devices: 4.6 us -> 0.6 us  [on_device(): state.append((current, part, swap_y(part)))]
    ppermute x4 -> x2, waiting for transfers between devices: 5.7 us -> 1.79 us  [on_device(): state.append((current, part, swap_y(part)))]
    ppermute x10 -> x12, waiting for transfers between devices: 12.5 us -> 16.1 us  [the longest x1 7.48 us: on_device(): out_far = swap_y(w_out)]
    ppermute x10 -> x12, starting transfers between devices: 7.07 us -> 10.2 us  [the longest x1 2.52 us: on_device(): out_far = swap_y(w_out)]
    all_to_all x1, starting transfers between devices: 7.08 us -> 5.92 us  [on_device(): received = lax.all_to_all(payload, ('frame', 'core'), 0, 0, tiled=True)]
  transfers between devices with their start and end apart: 17 -> 17, of which waited for: 9 -> 10; matrix products, arithmetic and copies ran while one was open for 3% -> 0% of each run, Pallas kernels for 38% -> 33%
where the time goes in v3:
time: 92 us; the launch traced here: 91.7 us
  Pallas kernels  32.3 us (35%)
  waiting for transfers between devices  25.2 us (27%)
  starting transfers between devices  18.2 us (20%)
  blocking collectives  15.8 us (17%)
    all_to_all x1, blocking collectives, on_device(): result = lax.all_to_all(result, ('frame', 'core'), 0, 0, tiled=True)  15.8 us
    pallas_call x4, Pallas kernels, feed_call(): pl.pallas_call(functools.partial(feed_kernel, halves), out_shape=outs, in...  11.9 us
    pallas_call x4, Pallas kernels, attention_call(): pl.pallas_call(kernel, out_shape=outs, in_specs=[VMEM_SPEC] * len(arrays)...  11.3 us
    ppermute x1, waiting for transfers between devices, on_device(): out_far = swap_y(w_out)  7.48 us
    ppermute x2, waiting for transfers between devices, on_device(): fed.append((current, after, feed, swap_y(feed), later))  7.21 us
    all_to_all x1, starting transfers between devices, on_device(): received = lax.all_to_all(payload, ('frame', 'core'), 0, 0, tiled=True)  5.92 us
    pallas_call x1, Pallas kernels, hold(): pl.pallas_call(functools.partial(hold_kernel, tuple(places)), out_shape=t...  4.33 us
    ppermute x2, waiting for transfers between devices, on_device(): parts.append((current, after, feed_here, swap_y(feed_there)))  4.09 us
  transfers between devices with their start and end apart: 17, of which 10 were waited for; matrix products, arithmetic and copies ran while one was open for 0% of the time, Pallas kernels for 33%

profile of v3, /device:TPU:0, one launch (start us, length us, event | category | flops | bytes accessed | tf_op | source)
XLA Modules:
  0.0 91.7 jit_solution(14591816458980972193)
XLA Ops:
  1.0 2.5 %collective-permute-start.3 = (bf16[288,1152]{1,0:T(8,128)(2,1)}, bf16[288,1152]{1,0:T(8,128)(2,1)}, u32[]{:S(2)}, u32[]{:S(2)}) collective-permute-start(bf16[288,1152]{1,0:T(8,128)(2,1)} %refs_4_.1), channel_id=1, source_target_pairs={{0,2},{2,0},{1,3},{3,1},{4,6},{6,4},{5,7},{7,5},{8,10},{10,8},{9,1... | collective-permute-start | bytes 1990664 | tf_op jit(solution)/shard_map/ppermute | solution.py:556
  3.5 2.1 %payload.1 = bf16[16,2,40,128]{3,2,1,0:T(8,128)(2,1)} custom-call(s32[1]{0:T(128)} %bitcast.1.frame_far, s32[8]{0:T(128)} %level_far.1, s32[8,17]{1,0:T(8,128)} %window_far.1, bf16[8,64,288]{2,1,0:T(8,128)(2,1)} %x_far.1, bf16[2,64,288]{2,1,0:T(8,128)(2,1)} %fresh_far.1), custom_call_target="tpu_custom_call" | custom-call | tf_op jit(solution)/shard_map/payload/pallas_call | solution.py:112
  5.6 5.9 %all-to-all-start = ((bf16[16,2,40,128]{3,2,1,0:T(8,128)(2,1)}), bf16[16,2,40,128]{3,2,1,0:T(8,128)(2,1)S(1)}, u32[]{:S(2)}, u32[]{:S(2)}) async-start(bf16[16,2,40,128]{3,2,1,0:T(8,128)(2,1)} %payload.1), calls=%async_computation | async-start | bytes 655360 | tf_op jit(solution)/shard_map/all_to_all | solution.py:572
  11.9 7.5 %collective-permute-done.3.refs_6_ = bf16[288,1152]{1,0:T(8,128)(2,1)} collective-permute-done((bf16[288,1152]{1,0:T(8,128)(2,1)}, bf16[288,1152]{1,0:T(8,128)(2,1)}, u32[]{:S(2)}, u32[]{:S(2)}) %collective-permute-start.3) | collective-permute-done | bytes 663584 | tf_op jit(solution)/shard_map/ppermute | solution.py:556
  19.4 3.2 %all-to-all-done = bf16[16,2,40,128]{3,2,1,0:T(8,128)(2,1)S(1)} async-done(((bf16[16,2,40,128]{3,2,1,0:T(8,128)(2,1)}), bf16[16,2,40,128]{3,2,1,0:T(8,128)(2,1)S(1)}, u32[]{:S(2)}, u32[]{:S(2)}) %all-to-all-start) | async-done | bytes 327712 | tf_op jit(solution)/shard_map/all_to_all | solution.py:572
  22.7 0.6 collective-permute-start.11
  23.2 1.5 %collective-permute-start.5 = (bf16[8,2,40,128]{3,2,1,0:T(8,128)(2,1)S(1)}, bf16[8,2,40,128]{3,2,1,0:T(8,128)(2,1)S(1)}, u32[]{:S(2)}, u32[]{:S(2)}) collective-permute-start(bf16[8,2,40,128]{3,2,1,0:T(8,128)(2,1)S(1)} %get-tuple-element.68.received_ref.mine_ref), channel_id=1, source_target_pairs={{0,2},{2,0},{1,3},{3,1},{4,6},{6,4},{5,7},{7,5},{8,10},{10,8},{9,1... | collective-permute-start | bytes 491528 | tf_op jit(solution)/shard_map/ppermute | solution.py:582
  24.8 4.3 %hold.1 = (f32[6,64,1152]{2,1,0:T(8,128)S(1)}, bf16[3,288,1152]{2,1,0:T(8,128)(2,1)S(1)}, bf16[3,288,1152]{2,1,0:T(8,128)(2,1)S(1)}, bf16[1152,1152]{1,0:T(8,128)(2,1)S(1)}, bf16[1152,1152]{1,0:T(8,128)(2,1)S(1)}) custom-call(f32[6,64,1152]{2,1,0:T(8,128)} %bitcast.17, bf16[3,288,1152]{2,1,0:T(8,128)(2,1)} %bitcast.16, ...), custom_call_target="tpu_custom_call" | custom-call | bytes 22118400 | tf_op jit(solution)/shard_map/hold/pallas_call | solution.py:242
  29.1 0.9 %prepare.1 = (f32[2,64,1152]{2,1,0:T(8,128)S(1)}, f32[3,64,1152]{2,1,0:T(8,128)S(1)}, f32[1,64,1152]{2,1,0:T(8,128)S(1)}, f32[64,128]{1,0:T(8,128)S(1)}, f32[128,128]{1,0:T(8,128)S(1)}, /*index=5*/f32[8,128]{1,0:T(8,128)S(1)}) custom-call(s32[1]{0:T(128)} %bitcast.place_ref, bf16[8,2,40,128]{3,2,1,0:T(8,128)(2,1)S(1)} %get-tuple-element.68.received_ref.mine_ref, ...), custom_call_target="tpu_custom_call" | custom-call | tf_op jit(solution)/shard_map/prepare/pallas_call | solution.py:202
  30.1 2.7 %attention.6 = (bf16[128,1152]{1,0:T(8,128)(2,1)S(1)}, bf16[128,576]{1,0:T(8,128)(2,1)S(1)}, f32[2,1152]{1,0:T(2,128)S(1)}) custom-call(bf16[8,2,40,128]{3,2,1,0:T(8,128)(2,1)S(1)} %get-tuple-element.67.mine_ref, bf16[8,2,40,128]{3,2,1,0:T(8,128)(2,1)S(1)} %collective-permute-done.11.other_ref, f32[8,128]{1,0:T(8,128)S(1)} %get-tuple-element.37.flag_ref, ...), custom_call_target="tpu_custom_call" | custom-call | tf_op jit(solution)/shard_map/attention/pallas_call | solution.py:363
  32.8 0.6 collective-permute-start.12
  33.4 2.7 %attention.4 = (bf16[128,1152]{1,0:T(8,128)(2,1)S(1)}, bf16[128,576]{1,0:T(8,128)(2,1)S(1)}, f32[2,1152]{1,0:T(2,128)S(1)}) custom-call(bf16[8,2,40,128]{3,2,1,0:T(8,128)(2,1)S(1)} %get-tuple-element.68.received_ref.mine_ref, bf16[8,2,40,128]{3,2,1,0:T(8,128)(2,1)S(1)} %collective-permute-done.5.other_ref, f32[8,128]{1,0:T(8,128)S(1)} %get-tuple-element.37.flag_ref, ...), custom_call_target="tpu_custom_call" | custom-call | tf_op jit(solution)/shard_map/attention/pallas_call | solution.py:363
  36.1 1.6 %collective-permute-start.6 = (bf16[128,576]{1,0:T(8,128)(2,1)S(1)}, bf16[128,576]{1,0:T(8,128)(2,1)S(1)}, u32[]{:S(2)}, u32[]{:S(2)}) collective-permute-start(bf16[128,576]{1,0:T(8,128)(2,1)S(1)} %get-tuple-element.45.mine_ref), channel_id=1, source_target_pairs={{0,2},{2,0},{1,3},{3,1},{4,6},{6,4},{5,7},{7,5},{8,10},{10,8},{9,1... | collective-permute-start | bytes 442376 | tf_op jit(solution)/shard_map/ppermute | solution.py:594
  37.7 1.3 %collective-permute-done.12.other_ref = bf16[128,576]{1,0:T(8,128)(2,1)S(1)} collective-permute-done((bf16[128,576]{1,0:T(8,128)(2,1)S(1)}, bf16[128,576]{1,0:T(8,128)(2,1)S(1)}, u32[]{:S(2)}, u32[]{:S(2)}) %collective-permute-start.12) | collective-permute-done | bytes 147488 | tf_op jit(solution)/shard_map/ppermute | solution.py:594
  39.0 2.8 %feed.6 = (bf16[128,1152]{1,0:T(8,128)(2,1)S(1)}, bf16[128,1152]{1,0:T(8,128)(2,1)S(1)}) custom-call(f32[8,128]{1,0:T(8,128)S(1)} %get-tuple-element.37.flag_ref, bf16[128,1152]{1,0:T(8,128)(2,1)S(1)} %get-tuple-element.57.cur_ref.old_ref, bf16[128,576]{1,0:T(8,128)(2,1)S(1)} %get-tuple-element.58.mine_ref, ...), custom_call_target="tpu_custom_call" | custom-call | tf_op jit(solution)/shard_map/feed/pallas_call | solution.py:431
  42.1 2.8 %feed.4 = (bf16[128,1152]{1,0:T(8,128)(2,1)S(1)}, bf16[128,1152]{1,0:T(8,128)(2,1)S(1)}) custom-call(f32[8,128]{1,0:T(8,128)S(1)} %get-tuple-element.37.flag_ref, bf16[128,1152]{1,0:T(8,128)(2,1)S(1)} %get-tuple-element.44.cur_ref.old_ref, bf16[128,576]{1,0:T(8,128)(2,1)S(1)} %get-tuple-element.45.mine_ref, ...), custom_call_target="tpu_custom_call" | custom-call | tf_op jit(solution)/shard_map/feed/pallas_call | solution.py:431
  44.9 1.9 %collective-permute-start.8 = (bf16[128,1152]{1,0:T(8,128)(2,1)S(1)}, bf16[128,1152]{1,0:T(8,128)(2,1)S(1)}, u32[]{:S(2)}, u32[]{:S(2)}) collective-permute-start(bf16[128,1152]{1,0:T(8,128)(2,1)S(1)} %get-tuple-element.50.mine_ref), channel_id=1, source_target_pairs={{0,2},{2,0},{1,3},{3,1},{4,6},{6,4},{5,7},{7,5},{8,10},{10,8},{9,1... | collective-permute-start | bytes 884744 | tf_op jit(solution)/shard_map/ppermute | solution.py:598
  46.8 4.8 %collective-permute-done.13.other_ref = bf16[128,1152]{1,0:T(8,128)(2,1)S(1)} collective-permute-done((bf16[128,1152]{1,0:T(8,128)(2,1)S(1)}, bf16[128,1152]{1,0:T(8,128)(2,1)S(1)}, u32[]{:S(2)}, u32[]{:S(2)}) %collective-permute-start.13) | collective-permute-done | bytes 294944 | tf_op jit(solution)/shard_map/ppermute | solution.py:598
  51.6 3.0 %attention.7 = (bf16[128,1152]{1,0:T(8,128)(2,1)S(1)}, bf16[128,576]{1,0:T(8,128)(2,1)S(1)}) custom-call(bf16[128,1152]{1,0:T(8,128)(2,1)S(1)} %get-tuple-element.57.cur_ref.old_ref, bf16[128,1152]{1,0:T(8,128)(2,1)S(1)} %get-tuple-element.59.after_ref, bf16[128,1152]{1,0:T(8,128)(2,1)S(1)} %get-tuple-element.60.mine_ref, ...), custom_call_target="tpu_custom_call" | custom-call | tf_op jit(solution)/shard_map/attention/pallas_call | solution.py:363
  54.7 2.4 %collective-permute-done.8.other_ref = bf16[128,1152]{1,0:T(8,128)(2,1)S(1)} collective-permute-done((bf16[128,1152]{1,0:T(8,128)(2,1)S(1)}, bf16[128,1152]{1,0:T(8,128)(2,1)S(1)}, u32[]{:S(2)}, u32[]{:S(2)}) %collective-permute-start.8) | collective-permute-done | bytes 294944 | tf_op jit(solution)/shard_map/ppermute | solution.py:598
  57.1 2.8 %attention.5 = (bf16[128,1152]{1,0:T(8,128)(2,1)S(1)}, bf16[128,576]{1,0:T(8,128)(2,1)S(1)}) custom-call(bf16[128,1152]{1,0:T(8,128)(2,1)S(1)} %get-tuple-element.44.cur_ref.old_ref, bf16[128,1152]{1,0:T(8,128)(2,1)S(1)} %get-tuple-element.49.after_ref, bf16[128,1152]{1,0:T(8,128)(2,1)S(1)} %get-tuple-element.50.mine_ref, ...), custom_call_target="tpu_custom_call" | custom-call | tf_op jit(solution)/shard_map/attention/pallas_call | solution.py:363
  59.9 0.5 collective-permute-start.9
  60.5 1.3 %collective-permute-done.14.other_ref = bf16[128,576]{1,0:T(8,128)(2,1)S(1)} collective-permute-done((bf16[128,576]{1,0:T(8,128)(2,1)S(1)}, bf16[128,576]{1,0:T(8,128)(2,1)S(1)}, u32[]{:S(2)}, u32[]{:S(2)}) %collective-permute-start.14) | collective-permute-done | bytes 147488 | tf_op jit(solution)/shard_map/ppermute | solution.py:606
  61.7 3.2 %feed.7 = (bf16[128,1152]{1,0:T(8,128)(2,1)S(1)}, bf16[128,576]{1,0:T(8,128)(2,1)S(1)}, bf16[128,576]{1,0:T(8,128)(2,1)S(1)}) custom-call(f32[8,128]{1,0:T(8,128)S(1)} %get-tuple-element.37.flag_ref, bf16[128,1152]{1,0:T(8,128)(2,1)S(1)} %get-tuple-element.62.cur_ref.refs_4_, bf16[128,576]{1,0:T(8,128)(2,1)S(1)} %get-tuple-element.63.mine_ref, ...), custom_call_target="tpu_custom_call" | custom-call | tf_op jit(solution)/shard_map/feed/pallas_call | solution.py:431
  65.2 0.5 collective-permute-done.9.other_ref
  65.7 3.2 %feed.5 = (bf16[128,1152]{1,0:T(8,128)(2,1)S(1)}, bf16[128,576]{1,0:T(8,128)(2,1)S(1)}, bf16[128,576]{1,0:T(8,128)(2,1)S(1)}) custom-call(f32[8,128]{1,0:T(8,128)S(1)} %get-tuple-element.37.flag_ref, bf16[128,1152]{1,0:T(8,128)(2,1)S(1)} %get-tuple-element.52.cur_ref.refs_0_, bf16[128,576]{1,0:T(8,128)(2,1)S(1)} %get-tuple-element.53.mine_ref, ...), custom_call_target="tpu_custom_call" | custom-call | tf_op jit(solution)/shard_map/feed/pallas_call | solution.py:431
  68.9 1.2 %collective-permute-start.10 = (bf16[128,576]{1,0:T(8,128)(2,1)S(1)}, bf16[128,576]{1,0:T(8,128)(2,1)S(1)}, u32[]{:S(2)}, u32[]{:S(2)}) collective-permute-start(bf16[128,576]{1,0:T(8,128)(2,1)S(1)} %get-tuple-element.56), channel_id=1, source_target_pairs={{0,2},{2,0},{1,3},{3,1},{4,6},{6,4},{5,7},{7,5},{8,10},{10,8},{9,1... | collective-permute-start | bytes 442376 | tf_op jit(solution)/shard_map/ppermute | solution.py:612
  70.1 1.0 %collective-permute-done.15.refs_7_ = bf16[128,576]{1,0:T(8,128)(2,1)S(1)} collective-permute-done((bf16[128,576]{1,0:T(8,128)(2,1)S(1)}, bf16[128,576]{1,0:T(8,128)(2,1)S(1)}, u32[]{:S(2)}, u32[]{:S(2)}) %collective-permute-start.15) | collective-permute-done | bytes 147488 | tf_op jit(solution)/shard_map/ppermute | solution.py:612
  71.1 3.1 %collective-permute-done.10.refs_3_ = bf16[128,576]{1,0:T(8,128)(2,1)S(1)} collective-permute-done((bf16[128,576]{1,0:T(8,128)(2,1)S(1)}, bf16[128,576]{1,0:T(8,128)(2,1)S(1)}, u32[]{:S(2)}, u32[]{:S(2)}) %collective-permute-start.10) | collective-permute-done | bytes 147488 | tf_op jit(solution)/shard_map/ppermute | solution.py:612
  74.2 0.8 finish.1
  75.0 15.8 %all_to_all.10.rows_ref = bf16[16,72,128]{2,1,0:T(8,128)(2,1)S(1)} all-to-all(bf16[16,72,128]{2,1,0:T(8,128)(2,1)S(1)} %bitcast.12), channel_id=1, replica_groups=mesh['frame'=8,'y'=2,'core'=2] {'frame','core'}, dimensions={0} | all-to-all | bytes 589824 | tf_op jit(solution)/shard_map/all_to_all | solution.py:616
  90.8 0.9 %unpack.1 = bf16[8,64,288]{2,1,0:T(8,128)(2,1)} custom-call(bf16[16,72,128]{2,1,0:T(8,128)(2,1)S(1)} %all_to_all.10.rows_ref), custom_call_target="tpu_custom_call" | custom-call | tf_op jit(solution)/shard_map/unpack/pallas_call | solution.py:520
  (26 shorter events, 2.1 us)
Async XLA Ops:
  0.0 24.8 %collective-permute-start.1 = (bf16[1152,1152]{1,0:T(8,128)(2,1)}, bf16[1152,1152]{1,0:T(8,128)(2,1)}, u32[]{:S(2)}, u32[]{:S(2)}) collective-permute-start(bf16[1152,1152]{1,0:T(8,128)(2,1)} %fc2_me.7), channel_id=1, source_target_pairs={{0,1},{1,0},{2,3},{3,2},{4,5},{5,4},{6,7},{7,6},{8,9},{9,8},{10,11... | collective-permute-start | bytes 7962632 | tf_op jit(solution)/shard_map/ppermute | solution.py:561
  0.5 37.3 %collective-permute-start.7 = (bf16[1152,1152]{1,0:T(8,128)(2,1)}, bf16[1152,1152]{1,0:T(8,128)(2,1)S(1)}, u32[]{:S(2)}, u32[]{:S(2)}) collective-permute-start(bf16[1152,1152]{1,0:T(8,128)(2,1)} %fc1_me.7), channel_id=1, source_target_pairs={{0,1},{1,0},{2,3},{3,2},{4,5},{5,4},{6,7},{7,6},{8,9},{9,8},{10,11... | collective-permute-start | bytes 7962632 | tf_op jit(solution)/shard_map/ppermute | solution.py:565
  0.5 24.3 %collective-permute-start = (bf16[3,288,1152]{2,1,0:T(8,128)(2,1)}, bf16[3,288,1152]{2,1,0:T(8,128)(2,1)}, u32[]{:S(2)}, u32[]{:S(2)}) collective-permute-start(bf16[3,288,1152]{2,1,0:T(8,128)(2,1)} %bitcast.15), channel_id=1, source_target_pairs={{0,1},{1,0},{2,3},{3,2},{4,5},{5,4},{6,7},{7,6},{8,9},{9,8},{10,11... | collective-permute-start | bytes 5971976 | tf_op jit(solution)/shard_map/ppermute | solution.py:560
  1.0 18.4 %collective-permute-start.3 = (bf16[288,1152]{1,0:T(8,128)(2,1)}, bf16[288,1152]{1,0:T(8,128)(2,1)}, u32[]{:S(2)}, u32[]{:S(2)}) collective-permute-start(bf16[288,1152]{1,0:T(8,128)(2,1)} %refs_4_.1), channel_id=1, source_target_pairs={{0,2},{2,0},{1,3},{3,1},{4,6},{6,4},{5,7},{7,5},{8,10},{10,8},{9,1... | collective-permute-start | bytes 1990664 | tf_op jit(solution)/shard_map/ppermute | solution.py:556
  5.6 17.0 %all-to-all-start = ((bf16[16,2,40,128]{3,2,1,0:T(8,128)(2,1)}), bf16[16,2,40,128]{3,2,1,0:T(8,128)(2,1)S(1)}, u32[]{:S(2)}, u32[]{:S(2)}) async-start(bf16[16,2,40,128]{3,2,1,0:T(8,128)(2,1)} %payload.1), calls=%async_computation | async-start | bytes 655360 | tf_op jit(solution)/shard_map/all_to_all | solution.py:572
  11.5 11.2 %collective-permute-start.2 = (bf16[288,1152]{1,0:T(8,128)(2,1)}, bf16[288,1152]{1,0:T(8,128)(2,1)}, u32[]{:S(2)}, u32[]{:S(2)}) collective-permute-start(bf16[288,1152]{1,0:T(8,128)(2,1)} %refs_4_.1), channel_id=1, source_target_pairs={{0,1},{1,0},{2,3},{3,2},{4,5},{5,4},{6,7},{7,6},{8,9},{9,8},{10,11... | collective-permute-start | bytes 1990664 | tf_op jit(solution)/shard_map/ppermute | solution.py:562
  19.4 3.9 %collective-permute-start.4 = (bf16[288,1152]{1,0:T(8,128)(2,1)}, bf16[288,1152]{1,0:T(8,128)(2,1)}, u32[]{:S(2)}, u32[]{:S(2)}) collective-permute-start(bf16[288,1152]{1,0:T(8,128)(2,1)} %collective-permute-done.3.refs_6_), channel_id=1, source_target_pairs={{0,1},{1,0},{2,3},{3,2},{4,5},{5,4},{6,7},{7,6},{8,9},{9,8},{10,11... | collective-permute-start | bytes 1990664 | tf_op jit(solution)/shard_map/ppermute | solution.py:562
  22.7 7.4 %collective-permute-start.11 = (bf16[8,2,40,128]{3,2,1,0:T(8,128)(2,1)S(1)}, bf16[8,2,40,128]{3,2,1,0:T(8,128)(2,1)S(1)}, u32[]{:S(2)}, u32[]{:S(2)}) collective-permute-start(bf16[8,2,40,128]{3,2,1,0:T(8,128)(2,1)S(1)} %get-tuple-element.67.mine_ref), channel_id=1, source_target_pairs={{0,2},{2,0},{1,3},{3,1},{4,6},{6,4},{5,7},{7,5},{8,10},{10,8},{9,1... | collective-permute-start | bytes 491528 | tf_op jit(solution)/shard_map/ppermute | solution.py:582
  23.2 10.2 %collective-permute-start.5 = (bf16[8,2,40,128]{3,2,1,0:T(8,128)(2,1)S(1)}, bf16[8,2,40,128]{3,2,1,0:T(8,128)(2,1)S(1)}, u32[]{:S(2)}, u32[]{:S(2)}) collective-permute-start(bf16[8,2,40,128]{3,2,1,0:T(8,128)(2,1)S(1)} %get-tuple-element.68.received_ref.mine_ref), channel_id=1, source_target_pairs={{0,2},{2,0},{1,3},{3,1},{4,6},{6,4},{5,7},{7,5},{8,10},{10,8},{9,1... | collective-permute-start | bytes 491528 | tf_op jit(solution)/shard_map/ppermute | solution.py:582
  24.8 4.4 %copy-start.2 = (f32[64]{0:T(128)S(1)}, f32[64]{0:T(128)}, u32[]{:S(2)}) copy-start(f32[64]{0:T(128)} %param.16) | copy-start | bytes 772
  24.8 4.4 %copy-start.3 = (f32[64]{0:T(128)S(1)}, f32[64]{0:T(128)}, u32[]{:S(2)}) copy-start(f32[64]{0:T(128)} %param.17) | copy-start | bytes 772
  30.1 8.9 %copy-start.1 = (bf16[1152,1152]{1,0:T(8,128)(2,1)S(1)}, bf16[1152,1152]{1,0:T(8,128)(2,1)}, u32[]{:S(2)}) copy-start(bf16[1152,1152]{1,0:T(8,128)(2,1)} %fc1_me.7) | copy-start | bytes 7962628
  32.8 6.2 %copy-start = (bf16[1152,1152]{1,0:T(8,128)(2,1)S(1)}, bf16[1152,1152]{1,0:T(8,128)(2,1)}, u32[]{:S(2)}) copy-start(bf16[1152,1152]{1,0:T(8,128)(2,1)} %fc2_me.7) | copy-start | bytes 7962628
  32.8 6.2 %collective-permute-start.12 = (bf16[128,576]{1,0:T(8,128)(2,1)S(1)}, bf16[128,576]{1,0:T(8,128)(2,1)S(1)}, u32[]{:S(2)}, u32[]{:S(2)}) collective-permute-start(bf16[128,576]{1,0:T(8,128)(2,1)S(1)} %get-tuple-element.58.mine_ref), channel_id=1, source_target_pairs={{0,2},{2,0},{1,3},{3,1},{4,6},{6,4},{5,7},{7,5},{8,10},{10,8},{9,1... | collective-permute-start | bytes 442376 | tf_op jit(solution)/shard_map/ppermute | solution.py:594
  36.1 5.9 %collective-permute-start.6 = (bf16[128,576]{1,0:T(8,128)(2,1)S(1)}, bf16[128,576]{1,0:T(8,128)(2,1)S(1)}, u32[]{:S(2)}, u32[]{:S(2)}) collective-permute-start(bf16[128,576]{1,0:T(8,128)(2,1)S(1)} %get-tuple-element.45.mine_ref), channel_id=1, source_target_pairs={{0,2},{2,0},{1,3},{3,1},{4,6},{6,4},{5,7},{7,5},{8,10},{10,8},{9,1... | collective-permute-start | bytes 442376 | tf_op jit(solution)/shard_map/ppermute | solution.py:594
  41.8 9.8 %collective-permute-start.13 = (bf16[128,1152]{1,0:T(8,128)(2,1)S(1)}, bf16[128,1152]{1,0:T(8,128)(2,1)S(1)}, u32[]{:S(2)}, u32[]{:S(2)}) collective-permute-start(bf16[128,1152]{1,0:T(8,128)(2,1)S(1)} %get-tuple-element.60.mine_ref), channel_id=1, source_target_pairs={{0,2},{2,0},{1,3},{3,1},{4,6},{6,4},{5,7},{7,5},{8,10},{10,8},{9,1... | collective-permute-start | bytes 884744 | tf_op jit(solution)/shard_map/ppermute | solution.py:598
  44.9 12.2 %collective-permute-start.8 = (bf16[128,1152]{1,0:T(8,128)(2,1)S(1)}, bf16[128,1152]{1,0:T(8,128)(2,1)S(1)}, u32[]{:S(2)}, u32[]{:S(2)}) collective-permute-start(bf16[128,1152]{1,0:T(8,128)(2,1)S(1)} %get-tuple-element.50.mine_ref), channel_id=1, source_target_pairs={{0,2},{2,0},{1,3},{3,1},{4,6},{6,4},{5,7},{7,5},{8,10},{10,8},{9,1... | collective-permute-start | bytes 884744 | tf_op jit(solution)/shard_map/ppermute | solution.py:598
  54.6 7.1 %collective-permute-start.14 = (bf16[128,576]{1,0:T(8,128)(2,1)S(1)}, bf16[128,576]{1,0:T(8,128)(2,1)S(1)}, u32[]{:S(2)}, u32[]{:S(2)}) collective-permute-start(bf16[128,576]{1,0:T(8,128)(2,1)S(1)} %get-tuple-element.63.mine_ref), channel_id=1, source_target_pairs={{0,2},{2,0},{1,3},{3,1},{4,6},{6,4},{5,7},{7,5},{8,10},{10,8},{9,1... | collective-permute-start | bytes 442376 | tf_op jit(solution)/shard_map/ppermute | solution.py:606
  59.9 5.8 %collective-permute-start.9 = (bf16[128,576]{1,0:T(8,128)(2,1)S(1)}, bf16[128,576]{1,0:T(8,128)(2,1)S(1)}, u32[]{:S(2)}, u32[]{:S(2)}) collective-permute-start(bf16[128,576]{1,0:T(8,128)(2,1)S(1)} %get-tuple-element.53.mine_ref), channel_id=1, source_target_pairs={{0,2},{2,0},{1,3},{3,1},{4,6},{6,4},{5,7},{7,5},{8,10},{10,8},{9,1... | collective-permute-start | bytes 442376 | tf_op jit(solution)/shard_map/ppermute | solution.py:606
  64.9 6.2 %collective-permute-start.15 = (bf16[128,576]{1,0:T(8,128)(2,1)S(1)}, bf16[128,576]{1,0:T(8,128)(2,1)S(1)}, u32[]{:S(2)}, u32[]{:S(2)}) collective-permute-start(bf16[128,576]{1,0:T(8,128)(2,1)S(1)} %get-tuple-element.66), channel_id=1, source_target_pairs={{0,2},{2,0},{1,3},{3,1},{4,6},{6,4},{5,7},{7,5},{8,10},{10,8},{9,1... | collective-permute-start | bytes 442376 | tf_op jit(solution)/shard_map/ppermute | solution.py:612
  68.9 5.3 %collective-permute-start.10 = (bf16[128,576]{1,0:T(8,128)(2,1)S(1)}, bf16[128,576]{1,0:T(8,128)(2,1)S(1)}, u32[]{:S(2)}, u32[]{:S(2)}) collective-permute-start(bf16[128,576]{1,0:T(8,128)(2,1)S(1)} %get-tuple-element.56), channel_id=1, source_target_pairs={{0,2},{2,0},{1,3},{3,1},{4,6},{6,4},{5,7},{7,5},{8,10},{10,8},{9,1... | collective-permute-start | bytes 442376 | tf_op jit(solution)/shard_map/ppermute | solution.py:612

commit v4 on v3

--- a/solution.py
+++ b/solution.py
@@ -27,6 +27,12 @@
 def params(*arrays):
     held = sum(math.prod(a.shape) * jnp.dtype(a.dtype).itemsize for a in arrays)
     return pltpu.CompilerParams(vmem_limit_bytes=held + 8 * 1024 * 1024)
+
+
+def takes(microseconds):
+    return pl.CostEstimate(
+        flops=0, bytes_accessed=int(microseconds * 3.3e6), transcendentals=0
+    )
 
 
 def tiles_of(share):
@@ -124,6 +130,7 @@
             pltpu.SemaphoreType.DMA((5,)),
         ],
         compiler_params=params(x, fresh, out, scratch),
+        cost_estimate=takes(2),
         name="payload",
     )(*in_hbm(frame_index, noise_level, window_mask, x, fresh))
 
@@ -147,9 +154,15 @@
 
 
 def prepare_kernel(
-    here, lane_at, place_ref, received_ref, table_ref, keep_ref, layer_ref,
-    norm_ref, feed_ref, gate_ref, pair_ref, mask_ref, flag_ref,
+    here, lane_at, places, place_ref, received_ref, table_far, keep_ref, layer_ref, *refs
 ):
+    sources, refs = refs[: len(places)], refs[len(places) :]
+    norm_ref, feed_ref, gate_ref, pair_ref, mask_ref, flag_ref = refs[:6]
+    held, (table_ref, table_sems, sems) = refs[6:-3], refs[-3:]
+    table_copies = start_copies(
+        (table_far,), [(0, 0, 0, table_far.shape[0])], (table_ref,), table_sems
+    )
+    copies = start_copies(sources, places, held, sems)
     flag_ref[...] = jnp.where(place_ref[0] < 2, jnp.ones_like(flag_ref), 0.0)
     groups = received_ref.shape[0]
     frames = groups * here
@@ -160,6 +173,8 @@
     ids = lax.broadcasted_iota(jnp.int32, (frames, levels), 1).astype(F32)
     hot = level == ids
     hot_bf = hot.astype(BF16)
+    for copy in table_copies:
+        copy.wait()
     targets = [(norm_ref, 0), (norm_ref, 1), (feed_ref, 0), (feed_ref, 1), (feed_ref, 2), (gate_ref, 0)]
     for j, (target, at) in enumerate(targets):
         rows = table_ref[j]
@@ -186,9 +201,11 @@
         for o in range(OFFSETS):
             is_open = jnp.where(distance == o - W, meta[:, 1 + o : 2 + o], is_open)
         mask_ref[t * frames : (t + 1) * frames, :] = jnp.where(inside, is_open, 0.0)
-
-
-def prepare(place, received, table, keep, layer, here, lane_at, block):
+    for copy in copies:
+        copy.wait()
+
+
+def prepare(place, received, table, keep, layer, weights, places, held, here, lane_at, block):
     frames = received.shape[0] * here
     features = table.shape[2]
     outs = (
@@ -198,57 +215,40 @@
         jax.ShapeDtypeStruct((frames, LANES), F32),
         jax.ShapeDtypeStruct((block, block), F32),
         jax.ShapeDtypeStruct((8, LANES), F32),
-    )
+    ) + tuple(jax.ShapeDtypeStruct(shape, BF16) for shape in held)
+    (table,) = in_hbm(table)
     return pl.pallas_call(
-        functools.partial(prepare_kernel, here, lane_at),
+        functools.partial(prepare_kernel, here, lane_at, tuple(places)),
         out_shape=outs,
-        in_specs=[SMEM_SPEC] + [VMEM_SPEC] * 4,
+        in_specs=[SMEM_SPEC, VMEM_SPEC, HBM_SPEC, VMEM_SPEC, VMEM_SPEC]
+        + [HBM_SPEC] * len(weights),
         out_specs=(VMEM_SPEC,) * len(outs),
+        scratch_shapes=[
+            pltpu.VMEM(table.shape, F32),
+            pltpu.SemaphoreType.DMA((3,)),
+            pltpu.SemaphoreType.DMA((3 * len(weights),)),
+        ],
         compiler_params=params(received, table, *outs),
+        cost_estimate=takes(5),
         name="prepare",
-    )(place, received, table, keep.reshape(1, -1), layer.reshape(1, -1))
-
-
-def hold_kernel(places, *refs):
-    sources, targets, sems = refs[: len(places)], refs[len(places) : -1], refs[-1]
+    )(place, received, table, keep.reshape(1, -1), layer.reshape(1, -1), *in_hbm(*weights))
+
+
+def start_copies(sources, places, targets, sems):
     copies = []
-    for source, (index, start) in zip(sources, places):
-        rows = source.shape[0]
+    for source, (index, to, at, rows) in zip(sources, places):
         parts = 3 if rows % 48 == 0 or rows % 3 == 0 and len(source.shape) > 2 else 1
         for n in range(parts):
             size = rows // parts
             copies.append(
                 pltpu.make_async_copy(
-                    source.at[pl.ds(n * size, size)],
-                    targets[index].at[pl.ds(start + n * size, size)],
+                    source.at[pl.ds(at + n * size, size)],
+                    targets[index].at[pl.ds(to + n * size, size)],
                     sems.at[len(copies)],
                 )
             )
             copies[-1].start()
-    for copy in copies:
-        copy.wait()
-
-
-def hold(*groups):
-    places, outs = [], []
-    for index, group in enumerate(groups):
-        start = 0
-        for array in group:
-            places.append((index, start))
-            start += array.shape[0]
-        outs.append(jax.ShapeDtypeStruct((start,) + group[0].shape[1:], group[0].dtype))
-    arrays = [array for group in groups for array in group]
-    held = sum(math.prod(o.shape) * jnp.dtype(o.dtype).itemsize for o in outs)
-    return pl.pallas_call(
-        functools.partial(hold_kernel, tuple(places)),
-        out_shape=tuple(outs),
-        in_specs=[HBM_SPEC] * len(arrays),
-        out_specs=(VMEM_SPEC,) * len(outs),
-        scratch_shapes=[pltpu.SemaphoreType.DMA((3 * len(arrays),))],
-        compiler_params=params(*outs),
-        cost_estimate=pl.CostEstimate(flops=0, bytes_accessed=2 * held, transcendentals=0),
-        name="hold",
-    )(*in_hbm(*arrays))
+    return copies
 
 
 def attention_rows(current, norm_ref, mask_ref, weights, out_ref):
@@ -295,8 +295,11 @@
         values = jnp.concatenate([value * lanes for lanes in head_lanes], axis=0)
         row = jnp.concatenate(shares[n * heads : (n + 1) * heads], axis=1)
         attended.append(jnp.dot(row, values, preferred_element_type=F32).astype(BF16))
-    for n, (side, at) in enumerate(units):
-        out_ref[at, side * share : (side + 1) * share] = attended[n]
+    sides = [attended[side * count : (side + 1) * count] for side in range(2)]
+    sides = [x[0] if count == 1 else jnp.concatenate(x, axis=0) for x in sides]
+    full, _ = tiles_of(share)
+    tiles = [x[:, t * LANES : (t + 1) * LANES] for x in sides for t in range(full)]
+    pack_half(out_ref, tiles, jnp.concatenate([x[:, full * LANES :] for x in sides], axis=1))
 
 
 def shifted_in(rows, fresh_row):
@@ -356,7 +359,7 @@
 def attention_call(kernel, arrays, rows, features, fresh_count=0):
     outs = (
         jax.ShapeDtypeStruct((rows, features), BF16),
-        jax.ShapeDtypeStruct((rows, features // 2), BF16),
+        jax.ShapeDtypeStruct((rows * features // 2 // LANES, LANES), BF16),
     )
     if fresh_count:
         outs += (jax.ShapeDtypeStruct((fresh_count, features), F32),)
@@ -366,8 +369,35 @@
         in_specs=[VMEM_SPEC] * len(arrays),
         out_specs=(VMEM_SPEC,) * len(outs),
         compiler_params=params(*arrays, *outs),
+        cost_estimate=takes(2.8),
         name="attention",
     )(*arrays)
+
+
+def pack_half(ref, tiles, tail):
+    rows = tail.shape[0]
+    for n, tile in enumerate(tiles):
+        ref[n * rows : (n + 1) * rows, :] = tile
+    ref[len(tiles) * rows :, :] = jnp.concatenate([tail[: rows // 2], tail[rows // 2 :]], axis=1)
+
+
+def pick_half(first_half, value):
+    middle = value.shape[1] // 2 // LANES
+    tiles = []
+    for t in range(middle):
+        left, right = (value[:, n * LANES : (n + 1) * LANES] for n in (t, t + middle + 1))
+        tiles.append(jnp.where(first_half, left, right))
+    split = value[:, middle * LANES : (middle + 1) * LANES]
+    cut = LANES // 2
+    return tiles, jnp.where(first_half[:, :cut], split[:, :cut], split[:, cut:])
+
+
+def unpack_half(ref, rows):
+    count = ref.shape[0] // rows
+    tail = ref[count * rows :, :]
+    tail = jnp.concatenate([tail[:, : LANES // 2], tail[:, LANES // 2 :]], axis=0)
+    tiles = [ref[n * rows : (n + 1) * rows, :] for n in range(count)]
+    return jnp.concatenate(tiles, axis=1), tail
 
 
 def gelu(x):
@@ -383,15 +413,19 @@
     halves, flag_ref, cur_ref, mine_ref, other_ref, mod_ref,
     out_all, fc1_me, fc1_other, fc2_me, fc2_other, *rest,
 ):
-    outs, hidden_ref = rest[:-1], rest[-1]
+    outs, hidden_ref = (rest[:-2], rest[-2]) if halves else (rest[:-1], rest[-1])
     after_ref = outs[0]
     frames = mod_ref.shape[1]
     tokens = cur_ref.shape[0] // frames
     normed = []
-    half = mine_ref.shape[1]
-    attention_total = jnp.dot(mine_ref[...], out_all[:half], preferred_element_type=F32) + jnp.dot(
-        other_ref[...], out_all[half:], preferred_element_type=F32
-    )
+    rows, half = cur_ref.shape[0], out_all.shape[0] // 2
+    attention_total = None
+    for n, ref in enumerate((mine_ref, other_ref)):
+        main, tail = unpack_half(ref, rows)
+        middle = n * half + main.shape[1]
+        part = jnp.dot(main, out_all[n * half : middle], preferred_element_type=F32)
+        part += jnp.dot(tail, out_all[middle : (n + 1) * half], preferred_element_type=F32)
+        attention_total = part if n == 0 else attention_total + part
     for p in range(tokens):
         at = slice(p * frames, (p + 1) * frames)
         after = (cur_ref[at, :].astype(F32) + mod_ref[0] * attention_total[at]).astype(BF16)
@@ -411,30 +445,31 @@
             hidden_ref[:, :units], fc2_me[:, at], preferred_element_type=F32
         ) + jnp.dot(hidden_ref[:, units:], fc2_other[:, at], preferred_element_type=F32)
 
+    target = rest[-1] if halves else outs[1]
+    for start, size in pieces_of(features, 256):
+        at = slice(start, start + size)
+        target[:, at] = product(at).astype(BF16)
     if not halves:
-        for start, size in pieces_of(features, 256):
-            at = slice(start, start + size)
-            outs[1][:, at] = product(at).astype(BF16)
         return
-    total = product(slice(None))
-    left, right = total[:, : features // 2], total[:, features // 2 :]
-    first_half = flag_ref[0:1, 0:1] > 0.5
-    outs[1][...] = jnp.where(first_half, left, right).astype(BF16)
-    outs[2][...] = jnp.where(first_half, right, left).astype(BF16)
+    first_half = flag_ref[0:1, :] > 0.5
+    pack_half(outs[1], *pick_half(first_half, target[...]))
+    pack_half(outs[2], *pick_half(jnp.logical_not(first_half), target[...]))
 
 
 def feed_call(flag, cur, mine, other, mod, weights, halves):
     rows, features = cur.shape
     shape = jax.ShapeDtypeStruct((rows, features), BF16)
-    half = jax.ShapeDtypeStruct((rows, features // 2), BF16)
-    outs = (shape, half, half) if halves else (shape, shape)
+    packed = jax.ShapeDtypeStruct((rows * features // 2 // LANES, LANES), BF16)
+    outs = (shape, packed, packed) if halves else (shape, shape)
     return pl.pallas_call(
         functools.partial(feed_kernel, halves),
         out_shape=outs,
         in_specs=[VMEM_SPEC] * 10,
         out_specs=(VMEM_SPEC,) * len(outs),
-        scratch_shapes=[pltpu.VMEM((rows, 2 * weights[1].shape[1]), BF16)],
+        scratch_shapes=[pltpu.VMEM((rows, 2 * weights[1].shape[1]), BF16)]
+        + ([pltpu.VMEM((rows, features), BF16)] if halves else []),
         compiler_params=params(cur, mine, other, mod, *weights, *outs),
+        cost_estimate=takes(2.8),
         name="feed",
     )(flag, cur, mine, other, mod, *weights)
 
@@ -447,23 +482,32 @@
     half = features // 2
     share = half // cores
     full, rest = tiles_of(share)
-    first_half = flag_ref[0:1, 0:1] > 0.5
+    first_half = flag_ref[0:1, :] > 0.5
     keep, layer = pair_ref[:, 0:1], pair_ref[:, 1:2]
-
-    def mine(value):
-        return jnp.where(first_half, value[:, :half], value[:, half:])
-
-    gate = mine(gate_ref[0])
+    gates = pick_half(first_half, gate_ref[0])
+    gates = gates[0] + [gates[1]]
     results = []
     for n in range(chunks):
         old_ref, after_ref, mine_ref, other_ref = refs[4 * n : 4 * n + 4]
-        for p in range(old_ref.shape[0] // frames):
+        rows = old_ref.shape[0]
+        (mine, mine_tail), (theirs, their_tail) = (
+            unpack_half(ref, rows) for ref in (mine_ref, other_ref)
+        )
+        main = mine.astype(F32) + theirs.astype(F32)
+        main_tail = mine_tail.astype(F32) + their_tail.astype(F32)
+        for p in range(rows // frames):
             at = slice(p * frames, (p + 1) * frames)
-            total = mine_ref[at, :].astype(F32) + other_ref[at, :].astype(F32)
-            results.append(
-                keep * mine(old_ref[at, :].astype(F32))
-                + layer * (mine(after_ref[at, :].astype(F32)) + gate * total)
+            old, after = (
+                pick_half(first_half, ref[at, :].astype(F32)) for ref in (old_ref, after_ref)
             )
+            old, after = old[0] + [old[1]], after[0] + [after[1]]
+            total = [main[at, t * LANES : (t + 1) * LANES] for t in range(len(old) - 1)]
+            total.append(main_tail[at])
+            done = [
+                keep * o + layer * (a + g * t) for o, a, g, t in zip(old, after, gates, total)
+            ]
+            left, right = jnp.concatenate(done, axis=1), jnp.concatenate(done[-1:] + done[:-1], axis=1)
+            results.append(jnp.where(first_half[:, 0:1], left, right))
     unused = LANES - len(results) * rest
     for c in range(cores):
         shares = [r[:, c * share : (c + 1) * share] for r in results]
@@ -489,6 +533,7 @@
         in_specs=[VMEM_SPEC] * (3 + len(arrays)),
         out_specs=VMEM_SPEC,
         compiler_params=params(gate, pair, out, *arrays),
+        cost_estimate=takes(0.8),
         name="finish",
     )(flag, gate, pair, *arrays)
 
@@ -524,6 +569,7 @@
         out_specs=VMEM_SPEC,
         scratch_shapes=[pltpu.VMEM(scratch.shape, F32)],
         compiler_params=params(rows, out, scratch),
+        cost_estimate=takes(0.9),
         name="unpack",
     )(rows)
 
@@ -553,17 +599,9 @@
     swap_core = functools.partial(lax.ppermute, axis_name="core", perm=SWAP)
     swap_y = functools.partial(lax.ppermute, axis_name="y", perm=SWAP)
     w_qkv = jnp.swapaxes(w_qkv, 1, 2)
+    qkv_other = swap_core(w_qkv)
     out_far = swap_y(w_out)
-    table, w_qkv, qkv_other, fc2_other, out_all = hold(
-        (jnp.swapaxes(mod_table, 0, 1),),
-        (w_qkv,),
-        (swap_core(w_qkv),),
-        (swap_core(w_fc2),),
-        (w_out, swap_core(w_out), out_far, swap_core(out_far)),
-    )
-    attention_weights = (w_qkv, qkv_other)
-    feed_weights = (out_all, w_fc1, swap_core(w_fc1), w_fc2, fc2_other)
-
+    out_core, out_corner, fc2_other = swap_core(w_out), swap_core(out_far), swap_core(w_fc2)
     payload = make_payload(
         frame_index.astype(jnp.int32).reshape(1), noise_level, window_mask, latents, fresh,
         frames, tokens_all // tokens, chunk_count,
@@ -578,20 +616,40 @@
         received = jnp.stack(
             [jnp.where(first, received, partner), jnp.where(first, partner, received)], axis=1
         )
+    received, qkv_other, out_core, out_far, fc2_other = lax.optimization_barrier(
+        (received, qkv_other, out_core, out_far, fc2_other)
+    )
+    full, rest = tiles_of(share)
     arrived = [received[:, :, n] for n in range(chunk_count)]
     arrived_other = [swap_y(part) for part in arrived]
-    norm_mod, feed_mod, gate_mod, pair, mask, flag = prepare(
-        place, arrived[0], table, keep_coef, layer_coef, here, size * tiles_of(share)[1], block
+    weights = [w_qkv, qkv_other]
+    places = [(n, 0, 0, w_qkv.shape[0]) for n in range(2)]
+    for n in range(2):
+        first, second = ((w_out, out_core), (out_far, out_corner))[n]
+        weights += [first, second, first, second]
+        to = 2 * n * share
+        places += [(2, to, 0, full * LANES), (2, to + full * LANES, 0, full * LANES)]
+        to += 2 * full * LANES
+        places += [(2, to, full * LANES, rest), (2, to + rest, full * LANES, rest)]
+    weights.append(fc2_other)
+    places.append((3, 0, 0, w_fc2.shape[0]))
+    held = (w_qkv.shape, w_qkv.shape, (4 * share, features), w_fc2.shape)
+    norm_mod, feed_mod, gate_mod, pair, mask, flag, w_qkv, qkv_other, out_all, fc2_other = prepare(
+        place, arrived[0], jnp.swapaxes(mod_table, 0, 1), keep_coef, layer_coef,
+        weights, places, held, here, size * rest, block,
     )
+    attention_weights = (w_qkv, qkv_other)
 
     state = []
-    for mine, other in zip(arrived, arrived_other):
-        current, part, later = attention_call(
+    for n in range(chunk_count):
+        results = attention_call(
             functools.partial(first_attention_kernel, size),
-            (mine, other, flag, norm_mod, mask) + attention_weights,
+            (arrived[n], arrived_other[n], flag, norm_mod, mask) + attention_weights,
             rows, features, size,
         )
+        current, part, later = results
         state.append((current, part, swap_y(part), later))
+    feed_weights = (out_all, w_fc1, swap_core(w_fc1), w_fc2, fc2_other)
     fed = []
     for current, part, part_other, later in state:
         after, feed = feed_call(flag, current, part, part_other, feed_mod, feed_weights, False)

time: 92 us -> 90.4 us (0.983)
  waiting for transfers between devices: 25.2 us -> 23.7 us
    pallas_call x2 -> x1, Pallas kernels: 5.26 us -> 5.11 us  [prepare(): pl.pallas_call(functools.partial(prepare_kernel, here, lane_at, tuple(pla...]
  transfers between devices with their start and end apart: 17 -> 17, of which waited for: 10 -> 9; matrix products, arithmetic and copies ran while one was open for 0% -> 0% of each run, Pallas kernels for 33% -> 33%
where the time goes in v4:
time: 90.4 us; the launch traced here: 90.1 us
  Pallas kernels  31.7 us (35%)
  waiting for transfers between devices  23.7 us (26%)
  starting transfers between devices  19 us (21%)
  blocking collectives  15.5 us (17%)
    all_to_all x1, blocking collectives, on_device(): result = lax.all_to_all(result, ('frame', 'core'), 0, 0, tiled=True)  15.5 us
    pallas_call x4, Pallas kernels, attention_call(): pl.pallas_call(kernel, out_shape=outs, in_specs=[VMEM_SPEC] * len(arrays)...  11.6 us
    pallas_call x4, Pallas kernels, feed_call(): pl.pallas_call(functools.partial(feed_kernel, halves), out_shape=outs, in...  11.4 us
    ppermute x1, waiting for transfers between devices, on_device(): out_far = swap_y(w_out)  7.65 us
    ppermute x2, waiting for transfers between devices, on_device(): fed.append((current, after, feed, swap_y(feed), later))  7.09 us
    all_to_all x1, starting transfers between devices, on_device(): received = lax.all_to_all(payload, ('frame', 'core'), 0, 0, tiled=True)  5.92 us
    pallas_call x1, Pallas kernels, prepare(): pl.pallas_call(functools.partial(prepare_kernel, here, lane_at, tuple(pla...  5.11 us
    ppermute x2, waiting for transfers between devices, on_device(): parts.append((current, after, feed_here, swap_y(feed_there)))  3.96 us
  transfers between devices with their start and end apart: 17, of which 9 were waited for; matrix products, arithmetic and copies ran while one was open for 0% of the time, Pallas kernels for 33%

profile of v4, /device:TPU:0, one launch (start us, length us, event | category | flops | bytes accessed | tf_op | source)
XLA Modules:
  0.0 90.1 jit_solution(2933114973009385874)
XLA Ops:
  1.0 2.6 %collective-permute-start.2 = (bf16[288,1152]{1,0:T(8,128)(2,1)}, bf16[288,1152]{1,0:T(8,128)(2,1)}, u32[]{:S(2)}, u32[]{:S(2)}) collective-permute-start(bf16[288,1152]{1,0:T(8,128)(2,1)} %refs_4_.1), channel_id=1, source_target_pairs={{0,2},{2,0},{1,3},{3,1},{4,6},{6,4},{5,7},{7,5},{8,10},{10,8},{9,1... | collective-permute-start | bytes 1990664 | tf_op jit(solution)/shard_map/ppermute | solution.py:603
  3.7 2.1 %payload.1 = bf16[16,2,40,128]{3,2,1,0:T(8,128)(2,1)} custom-call(s32[1]{0:T(128)} %bitcast.1.frame_far, s32[8]{0:T(128)} %level_far.1, s32[8,17]{1,0:T(8,128)} %window_far.1, bf16[8,64,288]{2,1,0:T(8,128)(2,1)} %x_far.1, bf16[2,64,288]{2,1,0:T(8,128)(2,1)} %fresh_far.1), custom_call_target="tpu_custom_call" | custom-call | bytes 6600000 | tf_op jit(solution)/shard_map/payload/pallas_call | solution.py:118
  5.8 5.9 %all-to-all-start = ((bf16[16,2,40,128]{3,2,1,0:T(8,128)(2,1)}), bf16[16,2,40,128]{3,2,1,0:T(8,128)(2,1)S(1)}, u32[]{:S(2)}, u32[]{:S(2)}) async-start(bf16[16,2,40,128]{3,2,1,0:T(8,128)(2,1)} %payload.1), calls=%async_computation | async-start | bytes 655360 | tf_op jit(solution)/shard_map/all_to_all | solution.py:610
  11.7 7.7 %collective-permute-done.2.refs_6_.refs_8_ = bf16[288,1152]{1,0:T(8,128)(2,1)} collective-permute-done((bf16[288,1152]{1,0:T(8,128)(2,1)}, bf16[288,1152]{1,0:T(8,128)(2,1)}, u32[]{:S(2)}, u32[]{:S(2)}) %collective-permute-start.2) | collective-permute-done | bytes 663584 | tf_op jit(solution)/shard_map/ppermute | solution.py:603
  19.4 3.4 %all-to-all-done = bf16[16,2,40,128]{3,2,1,0:T(8,128)(2,1)S(1)} async-done(((bf16[16,2,40,128]{3,2,1,0:T(8,128)(2,1)}), bf16[16,2,40,128]{3,2,1,0:T(8,128)(2,1)S(1)}, u32[]{:S(2)}, u32[]{:S(2)}) %all-to-all-start) | async-done | bytes 327712 | tf_op jit(solution)/shard_map/all_to_all | solution.py:610
  22.9 0.6 collective-permute-start.11
  23.5 1.5 %collective-permute-start.5 = (bf16[8,2,40,128]{3,2,1,0:T(8,128)(2,1)S(1)}, bf16[8,2,40,128]{3,2,1,0:T(8,128)(2,1)S(1)}, u32[]{:S(2)}, u32[]{:S(2)}) collective-permute-start(bf16[8,2,40,128]{3,2,1,0:T(8,128)(2,1)S(1)} %get-tuple-element.76.received_ref.mine_ref), channel_id=1, source_target_pairs={{0,2},{2,0},{1,3},{3,1},{4,6},{6,4},{5,7},{7,5},{8,10},{10,8},{9,1... | collective-permute-start | bytes 491528 | tf_op jit(solution)/shard_map/ppermute | solution.py:624
  25.0 5.1 %prepare.1 = (f32[2,64,1152]{2,1,0:T(8,128)S(1)}, f32[3,64,1152]{2,1,0:T(8,128)S(1)}, f32[1,64,1152]{2,1,0:T(8,128)S(1)}, f32[64,128]{1,0:T(8,128)S(1)}, f32[128...) custom-call(s32[1]{0:T(128)} %bitcast.place_ref, ...), custom_call_target="tpu_custom_call" | custom-call | bytes 16500000 | tf_op jit(solution)/shard_map/prepare/pallas_call | solution.py:220
  30.2 2.8 %attention.6 = (bf16[128,1152]{1,0:T(8,128)(2,1)S(1)}, bf16[576,128]{1,0:T(8,128)(2,1)S(1)}, f32[2,1152]{1,0:T(2,128)S(1)}) custom-call(bf16[8,2,40,128]{3,2,1,0:T(8,128)(2,1)S(1)} %get-tuple-element.75.mine_ref, bf16[8,2,40,128]{3,2,1,0:T(8,128)(2,1)S(1)} %collective-permute-done.11.other_ref, f32[8,128]{1,0:T(8,128)S(1)} %get-tuple-element.45.flag_ref, ...), custom_call_target="tpu_custom_call" | custom-call | bytes 9240000 | tf_op jit(solution)/shard_map/attention/pallas_call | solution.py:366
  33.0 0.6 collective-permute-start.12
  33.5 2.8 %attention.4 = (bf16[128,1152]{1,0:T(8,128)(2,1)S(1)}, bf16[576,128]{1,0:T(8,128)(2,1)S(1)}, f32[2,1152]{1,0:T(2,128)S(1)}) custom-call(bf16[8,2,40,128]{3,2,1,0:T(8,128)(2,1)S(1)} %get-tuple-element.76.received_ref.mine_ref, bf16[8,2,40,128]{3,2,1,0:T(8,128)(2,1)S(1)} %collective-permute-done.5.other_ref, f32[8,128]{1,0:T(8,128)S(1)} %get-tuple-element.45.flag_ref, ...), custom_call_target="tpu_custom_call" | custom-call | bytes 9240000 | tf_op jit(solution)/shard_map/attention/pallas_call | solution.py:366
  36.3 1.6 %collective-permute-start.6 = (bf16[576,128]{1,0:T(8,128)(2,1)S(1)}, bf16[576,128]{1,0:T(8,128)(2,1)S(1)}, u32[]{:S(2)}, u32[]{:S(2)}) collective-permute-start(bf16[576,128]{1,0:T(8,128)(2,1)S(1)} %get-tuple-element.53.mine_ref), channel_id=1, source_target_pairs={{0,2},{2,0},{1,3},{3,1},{4,6},{6,4},{5,7},{7,5},{8,10},{10,8},{9,1... | collective-permute-start | bytes 442376 | tf_op jit(solution)/shard_map/ppermute | solution.py:651
  37.9 0.5 collective-permute-done.12.other_ref
  38.4 2.8 %feed.6 = (bf16[128,1152]{1,0:T(8,128)(2,1)S(1)}, bf16[128,1152]{1,0:T(8,128)(2,1)S(1)}) custom-call(f32[8,128]{1,0:T(8,128)S(1)} %get-tuple-element.45.flag_ref, bf16[128,1152]{1,0:T(8,128)(2,1)S(1)} %get-tuple-element.65.cur_ref.old_ref, bf16[576,128]{1,0:T(8,128)(2,1)S(1)} %get-tuple-element.66.mine_ref, ...), custom_call_target="tpu_custom_call" | custom-call | bytes 9240000 | tf_op jit(solution)/shard_map/feed/pallas_call | solution.py:464
  41.2 0.5 collective-permute-start.13
  41.7 2.8 %feed.4 = (bf16[128,1152]{1,0:T(8,128)(2,1)S(1)}, bf16[128,1152]{1,0:T(8,128)(2,1)S(1)}) custom-call(f32[8,128]{1,0:T(8,128)S(1)} %get-tuple-element.45.flag_ref, bf16[128,1152]{1,0:T(8,128)(2,1)S(1)} %get-tuple-element.52.cur_ref.old_ref, bf16[576,128]{1,0:T(8,128)(2,1)S(1)} %get-tuple-element.53.mine_ref, ...), custom_call_target="tpu_custom_call" | custom-call | bytes 9240000 | tf_op jit(solution)/shard_map/feed/pallas_call | solution.py:464
  44.6 1.6 %collective-permute-start.8 = (bf16[128,1152]{1,0:T(8,128)(2,1)S(1)}, bf16[128,1152]{1,0:T(8,128)(2,1)S(1)}, u32[]{:S(2)}, u32[]{:S(2)}) collective-permute-start(bf16[128,1152]{1,0:T(8,128)(2,1)S(1)} %get-tuple-element.58.mine_ref), channel_id=1, source_target_pairs={{0,2},{2,0},{1,3},{3,1},{4,6},{6,4},{5,7},{7,5},{8,10},{10,8},{9,1... | collective-permute-start | bytes 884744 | tf_op jit(solution)/shard_map/ppermute | solution.py:656
  46.2 5.0 %collective-permute-done.13.other_ref = bf16[128,1152]{1,0:T(8,128)(2,1)S(1)} collective-permute-done((bf16[128,1152]{1,0:T(8,128)(2,1)S(1)}, bf16[128,1152]{1,0:T(8,128)(2,1)S(1)}, u32[]{:S(2)}, u32[]{:S(2)}) %collective-permute-start.13) | collective-permute-done | bytes 294944 | tf_op jit(solution)/shard_map/ppermute | solution.py:656
  51.2 3.1 %attention.7 = (bf16[128,1152]{1,0:T(8,128)(2,1)S(1)}, bf16[576,128]{1,0:T(8,128)(2,1)S(1)}) custom-call(bf16[128,1152]{1,0:T(8,128)(2,1)S(1)} %get-tuple-element.65.cur_ref.old_ref, bf16[128,1152]{1,0:T(8,128)(2,1)S(1)} %get-tuple-element.67.after_ref, bf16[128,1152]{1,0:T(8,128)(2,1)S(1)} %get-tuple-element.68.mine_ref, ...), custom_call_target="tpu_custom_call" | custom-call | bytes 9240000 | tf_op jit(solution)/shard_map/attention/pallas_call | solution.py:366
  54.6 2.1 %collective-permute-done.8.other_ref = bf16[128,1152]{1,0:T(8,128)(2,1)S(1)} collective-permute-done((bf16[128,1152]{1,0:T(8,128)(2,1)S(1)}, bf16[128,1152]{1,0:T(8,128)(2,1)S(1)}, u32[]{:S(2)}, u32[]{:S(2)}) %collective-permute-start.8) | collective-permute-done | bytes 294944 | tf_op jit(solution)/shard_map/ppermute | solution.py:656
  56.7 2.9 %attention.5 = (bf16[128,1152]{1,0:T(8,128)(2,1)S(1)}, bf16[576,128]{1,0:T(8,128)(2,1)S(1)}) custom-call(bf16[128,1152]{1,0:T(8,128)(2,1)S(1)} %get-tuple-element.52.cur_ref.old_ref, bf16[128,1152]{1,0:T(8,128)(2,1)S(1)} %get-tuple-element.57.after_ref, bf16[128,1152]{1,0:T(8,128)(2,1)S(1)} %get-tuple-element.58.mine_ref, ...), custom_call_target="tpu_custom_call" | custom-call | bytes 9240000 | tf_op jit(solution)/shard_map/attention/pallas_call | solution.py:366
  59.6 0.6 collective-permute-start.9
  60.1 0.6 collective-permute-done.14.other_ref
  60.8 2.9 %feed.7 = (bf16[128,1152]{1,0:T(8,128)(2,1)S(1)}, bf16[576,128]{1,0:T(8,128)(2,1)S(1)}, bf16[576,128]{1,0:T(8,128)(2,1)S(1)}) custom-call(f32[8,128]{1,0:T(8,128)S(1)} %get-tuple-element.45.flag_ref, bf16[128,1152]{1,0:T(8,128)(2,1)S(1)} %get-tuple-element.70.cur_ref.refs_4_, bf16[576,128]{1,0:T(8,128)(2,1)S(1)} %get-tuple-element.71.mine_ref, ...), custom_call_target="tpu_custom_call" | custom-call | bytes 9240000 | tf_op jit(solution)/shard_map/feed/pallas_call | solution.py:464
  63.6 0.9 %collective-permute-start.15 = (bf16[576,128]{1,0:T(8,128)(2,1)S(1)}, bf16[576,128]{1,0:T(8,128)(2,1)S(1)}, u32[]{:S(2)}, u32[]{:S(2)}) collective-permute-start(bf16[576,128]{1,0:T(8,128)(2,1)S(1)} %get-tuple-element.74), channel_id=1, source_target_pairs={{0,2},{2,0},{1,3},{3,1},{4,6},{6,4},{5,7},{7,5},{8,10},{10,8},{9,1... | collective-permute-start | bytes 442376 | tf_op jit(solution)/shard_map/ppermute | solution.py:670
  65.0 2.9 %feed.5 = (bf16[128,1152]{1,0:T(8,128)(2,1)S(1)}, bf16[576,128]{1,0:T(8,128)(2,1)S(1)}, bf16[576,128]{1,0:T(8,128)(2,1)S(1)}) custom-call(f32[8,128]{1,0:T(8,128)S(1)} %get-tuple-element.45.flag_ref, bf16[128,1152]{1,0:T(8,128)(2,1)S(1)} %get-tuple-element.60.cur_ref.refs_0_, bf16[576,128]{1,0:T(8,128)(2,1)S(1)} %get-tuple-element.61.mine_ref, ...), custom_call_target="tpu_custom_call" | custom-call | bytes 9240000 | tf_op jit(solution)/shard_map/feed/pallas_call | solution.py:464
  67.8 1.2 %collective-permute-start.10 = (bf16[576,128]{1,0:T(8,128)(2,1)S(1)}, bf16[576,128]{1,0:T(8,128)(2,1)S(1)}, u32[]{:S(2)}, u32[]{:S(2)}) collective-permute-start(bf16[576,128]{1,0:T(8,128)(2,1)S(1)} %get-tuple-element.64), channel_id=1, source_target_pairs={{0,2},{2,0},{1,3},{3,1},{4,6},{6,4},{5,7},{7,5},{8,10},{10,8},{9,1... | collective-permute-start | bytes 442376 | tf_op jit(solution)/shard_map/ppermute | solution.py:670
  69.1 0.5 collective-permute-done.15.refs_7_
  69.6 3.5 %collective-permute-done.10.refs_3_ = bf16[576,128]{1,0:T(8,128)(2,1)S(1)} collective-permute-done((bf16[576,128]{1,0:T(8,128)(2,1)S(1)}, bf16[576,128]{1,0:T(8,128)(2,1)S(1)}, u32[]{:S(2)}, u32[]{:S(2)}) %collective-permute-start.10) | collective-permute-done | bytes 147488 | tf_op jit(solution)/shard_map/ppermute | solution.py:670
  73.0 0.7 finish.1
  73.7 15.5 %all_to_all.10.rows_ref = bf16[16,72,128]{2,1,0:T(8,128)(2,1)S(1)} all-to-all(bf16[16,72,128]{2,1,0:T(8,128)(2,1)S(1)} %bitcast.12), channel_id=1, replica_groups=mesh['frame'=8,'y'=2,'core'=2] {'frame','core'}, dimensions={0} | all-to-all | bytes 589824 | tf_op jit(solution)/shard_map/all_to_all | solution.py:674
  89.2 0.9 %unpack.1 = bf16[8,64,288]{2,1,0:T(8,128)(2,1)} custom-call(bf16[16,72,128]{2,1,0:T(8,128)(2,1)S(1)} %all_to_all.10.rows_ref), custom_call_target="tpu_custom_call" | custom-call | bytes 2970000 | tf_op jit(solution)/shard_map/unpack/pallas_call | solution.py:565
  (25 shorter events, 1.9 us)
Async XLA Ops:
  0.0 25.0 %copy-start.2 = (f32[64]{0:T(128)S(1)}, f32[64]{0:T(128)}, u32[]{:S(2)}) copy-start(f32[64]{0:T(128)} %param.16) | copy-start | bytes 772
  0.0 25.0 %copy-start.3 = (f32[64]{0:T(128)S(1)}, f32[64]{0:T(128)}, u32[]{:S(2)}) copy-start(f32[64]{0:T(128)} %param.17) | copy-start | bytes 772
  0.0 22.9 %collective-permute-start.3 = (bf16[1152,1152]{1,0:T(8,128)(2,1)}, bf16[1152,1152]{1,0:T(8,128)(2,1)}, u32[]{:S(2)}, u32[]{:S(2)}) collective-permute-start(bf16[1152,1152]{1,0:T(8,128)(2,1)} %fc2_me.7), channel_id=1, source_target_pairs={{0,1},{1,0},{2,3},{3,2},{4,5},{5,4},{6,7},{7,6},{8,9},{9,8},{10,11... | collective-permute-start | bytes 7962632 | tf_op jit(solution)/shard_map/ppermute | solution.py:604
  0.5 37.4 %collective-permute-start.7 = (bf16[1152,1152]{1,0:T(8,128)(2,1)}, bf16[1152,1152]{1,0:T(8,128)(2,1)S(1)}, u32[]{:S(2)}, u32[]{:S(2)}) collective-permute-start(bf16[1152,1152]{1,0:T(8,128)(2,1)} %fc1_me.7), channel_id=1, source_target_pairs={{0,1},{1,0},{2,3},{3,2},{4,5},{5,4},{6,7},{7,6},{8,9},{9,8},{10,11... | collective-permute-start | bytes 7962632 | tf_op jit(solution)/shard_map/ppermute | solution.py:652
  0.5 22.3 %collective-permute-start = (bf16[3,288,1152]{2,1,0:T(8,128)(2,1)}, bf16[3,288,1152]{2,1,0:T(8,128)(2,1)}, u32[]{:S(2)}, u32[]{:S(2)}) collective-permute-start(bf16[3,288,1152]{2,1,0:T(8,128)(2,1)} %bitcast.15), channel_id=1, source_target_pairs={{0,1},{1,0},{2,3},{3,2},{4,5},{5,4},{6,7},{7,6},{8,9},{9,8},{10,11... | collective-permute-start | bytes 5971976 | tf_op jit(solution)/shard_map/ppermute | solution.py:602
  1.0 18.4 %collective-permute-start.2 = (bf16[288,1152]{1,0:T(8,128)(2,1)}, bf16[288,1152]{1,0:T(8,128)(2,1)}, u32[]{:S(2)}, u32[]{:S(2)}) collective-permute-start(bf16[288,1152]{1,0:T(8,128)(2,1)} %refs_4_.1), channel_id=1, source_target_pairs={{0,2},{2,0},{1,3},{3,1},{4,6},{6,4},{5,7},{7,5},{8,10},{10,8},{9,1... | collective-permute-start | bytes 1990664 | tf_op jit(solution)/shard_map/ppermute | solution.py:603
  3.6 19.3 %collective-permute-start.1 = (bf16[288,1152]{1,0:T(8,128)(2,1)}, bf16[288,1152]{1,0:T(8,128)(2,1)}, u32[]{:S(2)}, u32[]{:S(2)}) collective-permute-start(bf16[288,1152]{1,0:T(8,128)(2,1)} %refs_4_.1), channel_id=1, source_target_pairs={{0,1},{1,0},{2,3},{3,2},{4,5},{5,4},{6,7},{7,6},{8,9},{9,8},{10,11... | collective-permute-start | bytes 1990664 | tf_op jit(solution)/shard_map/ppermute | solution.py:604
  5.8 17.0 %all-to-all-start = ((bf16[16,2,40,128]{3,2,1,0:T(8,128)(2,1)}), bf16[16,2,40,128]{3,2,1,0:T(8,128)(2,1)S(1)}, u32[]{:S(2)}, u32[]{:S(2)}) async-start(bf16[16,2,40,128]{3,2,1,0:T(8,128)(2,1)} %payload.1), calls=%async_computation | async-start | bytes 655360 | tf_op jit(solution)/shard_map/all_to_all | solution.py:610
  19.4 5.6 %collective-permute-start.4 = (bf16[288,1152]{1,0:T(8,128)(2,1)}, bf16[288,1152]{1,0:T(8,128)(2,1)}, u32[]{:S(2)}, u32[]{:S(2)}) collective-permute-start(bf16[288,1152]{1,0:T(8,128)(2,1)} %collective-permute-done.2.refs_6_.refs_8_), channel_id=1, source_target_pairs={{0,1},{1,0},{2,3},{3,2},{4,5},{5,4},{6,7},{7,6},{8,9},{9,8},{10,11... | collective-permute-start | bytes 1990664 | tf_op jit(solution)/shard_map/ppermute | solution.py:604
  22.9 7.2 %collective-permute-start.11 = (bf16[8,2,40,128]{3,2,1,0:T(8,128)(2,1)S(1)}, bf16[8,2,40,128]{3,2,1,0:T(8,128)(2,1)S(1)}, u32[]{:S(2)}, u32[]{:S(2)}) collective-permute-start(bf16[8,2,40,128]{3,2,1,0:T(8,128)(2,1)S(1)} %get-tuple-element.75.mine_ref), channel_id=1, source_target_pairs={{0,2},{2,0},{1,3},{3,1},{4,6},{6,4},{5,7},{7,5},{8,10},{10,8},{9,1... | collective-permute-start | bytes 491528 | tf_op jit(solution)/shard_map/ppermute | solution.py:624
  23.5 10.0 %collective-permute-start.5 = (bf16[8,2,40,128]{3,2,1,0:T(8,128)(2,1)S(1)}, bf16[8,2,40,128]{3,2,1,0:T(8,128)(2,1)S(1)}, u32[]{:S(2)}, u32[]{:S(2)}) collective-permute-start(bf16[8,2,40,128]{3,2,1,0:T(8,128)(2,1)S(1)} %get-tuple-element.76.received_ref.mine_ref), channel_id=1, source_target_pairs={{0,2},{2,0},{1,3},{3,1},{4,6},{6,4},{5,7},{7,5},{8,10},{10,8},{9,1... | collective-permute-start | bytes 491528 | tf_op jit(solution)/shard_map/ppermute | solution.py:624
  30.2 8.2 %copy-start.1 = (bf16[1152,1152]{1,0:T(8,128)(2,1)S(1)}, bf16[1152,1152]{1,0:T(8,128)(2,1)}, u32[]{:S(2)}) copy-start(bf16[1152,1152]{1,0:T(8,128)(2,1)} %fc1_me.7) | copy-start | bytes 7962628
  33.0 5.4 %copy-start = (bf16[1152,1152]{1,0:T(8,128)(2,1)S(1)}, bf16[1152,1152]{1,0:T(8,128)(2,1)}, u32[]{:S(2)}) copy-start(bf16[1152,1152]{1,0:T(8,128)(2,1)} %fc2_me.7) | copy-start | bytes 7962628
  33.0 5.4 %collective-permute-start.12 = (bf16[576,128]{1,0:T(8,128)(2,1)S(1)}, bf16[576,128]{1,0:T(8,128)(2,1)S(1)}, u32[]{:S(2)}, u32[]{:S(2)}) collective-permute-start(bf16[576,128]{1,0:T(8,128)(2,1)S(1)} %get-tuple-element.66.mine_ref), channel_id=1, source_target_pairs={{0,2},{2,0},{1,3},{3,1},{4,6},{6,4},{5,7},{7,5},{8,10},{10,8},{9,1... | collective-permute-start | bytes 442376 | tf_op jit(solution)/shard_map/ppermute | solution.py:651
  36.3 5.4 %collective-permute-start.6 = (bf16[576,128]{1,0:T(8,128)(2,1)S(1)}, bf16[576,128]{1,0:T(8,128)(2,1)S(1)}, u32[]{:S(2)}, u32[]{:S(2)}) collective-permute-start(bf16[576,128]{1,0:T(8,128)(2,1)S(1)} %get-tuple-element.53.mine_ref), channel_id=1, source_target_pairs={{0,2},{2,0},{1,3},{3,1},{4,6},{6,4},{5,7},{7,5},{8,10},{10,8},{9,1... | collective-permute-start | bytes 442376 | tf_op jit(solution)/shard_map/ppermute | solution.py:651
  41.2 10.0 %collective-permute-start.13 = (bf16[128,1152]{1,0:T(8,128)(2,1)S(1)}, bf16[128,1152]{1,0:T(8,128)(2,1)S(1)}, u32[]{:S(2)}, u32[]{:S(2)}) collective-permute-start(bf16[128,1152]{1,0:T(8,128)(2,1)S(1)} %get-tuple-element.68.mine_ref), channel_id=1, source_target_pairs={{0,2},{2,0},{1,3},{3,1},{4,6},{6,4},{5,7},{7,5},{8,10},{10,8},{9,1... | collective-permute-start | bytes 884744 | tf_op jit(solution)/shard_map/ppermute | solution.py:656
  44.6 12.1 %collective-permute-start.8 = (bf16[128,1152]{1,0:T(8,128)(2,1)S(1)}, bf16[128,1152]{1,0:T(8,128)(2,1)S(1)}, u32[]{:S(2)}, u32[]{:S(2)}) collective-permute-start(bf16[128,1152]{1,0:T(8,128)(2,1)S(1)} %get-tuple-element.58.mine_ref), channel_id=1, source_target_pairs={{0,2},{2,0},{1,3},{3,1},{4,6},{6,4},{5,7},{7,5},{8,10},{10,8},{9,1... | collective-permute-start | bytes 884744 | tf_op jit(solution)/shard_map/ppermute | solution.py:656
  54.3 6.5 %collective-permute-start.14 = (bf16[576,128]{1,0:T(8,128)(2,1)S(1)}, bf16[576,128]{1,0:T(8,128)(2,1)S(1)}, u32[]{:S(2)}, u32[]{:S(2)}) collective-permute-start(bf16[576,128]{1,0:T(8,128)(2,1)S(1)} %get-tuple-element.71.mine_ref), channel_id=1, source_target_pairs={{0,2},{2,0},{1,3},{3,1},{4,6},{6,4},{5,7},{7,5},{8,10},{10,8},{9,1... | collective-permute-start | bytes 442376 | tf_op jit(solution)/shard_map/ppermute | solution.py:664
  59.6 5.4 %collective-permute-start.9 = (bf16[576,128]{1,0:T(8,128)(2,1)S(1)}, bf16[576,128]{1,0:T(8,128)(2,1)S(1)}, u32[]{:S(2)}, u32[]{:S(2)}) collective-permute-start(bf16[576,128]{1,0:T(8,128)(2,1)S(1)} %get-tuple-element.61.mine_ref), channel_id=1, source_target_pairs={{0,2},{2,0},{1,3},{3,1},{4,6},{6,4},{5,7},{7,5},{8,10},{10,8},{9,1... | collective-permute-start | bytes 442376 | tf_op jit(solution)/shard_map/ppermute | solution.py:664
  63.6 5.9 %collective-permute-start.15 = (bf16[576,128]{1,0:T(8,128)(2,1)S(1)}, bf16[576,128]{1,0:T(8,128)(2,1)S(1)}, u32[]{:S(2)}, u32[]{:S(2)}) collective-permute-start(bf16[576,128]{1,0:T(8,128)(2,1)S(1)} %get-tuple-element.74), channel_id=1, source_target_pairs={{0,2},{2,0},{1,3},{3,1},{4,6},{6,4},{5,7},{7,5},{8,10},{10,8},{9,1... | collective-permute-start | bytes 442376 | tf_op jit(solution)/shard_map/ppermute | solution.py:670
  67.8 5.2 %collective-permute-start.10 = (bf16[576,128]{1,0:T(8,128)(2,1)S(1)}, bf16[576,128]{1,0:T(8,128)(2,1)S(1)}, u32[]{:S(2)}, u32[]{:S(2)}) collective-permute-start(bf16[576,128]{1,0:T(8,128)(2,1)S(1)} %get-tuple-element.64), channel_id=1, source_target_pairs={{0,2},{2,0},{1,3},{3,1},{4,6},{6,4},{5,7},{7,5},{8,10},{10,8},{9,1... | collective-permute-start | bytes 442376 | tf_op jit(solution)/shard_map/ppermute | solution.py:670

commit v5 on v4

--- a/solution.py
+++ b/solution.py
@@ -200,7 +200,8 @@
         is_open = jnp.zeros((frames, block), F32)
         for o in range(OFFSETS):
             is_open = jnp.where(distance == o - W, meta[:, 1 + o : 2 + o], is_open)
-        mask_ref[t * frames : (t + 1) * frames, :] = jnp.where(inside, is_open, 0.0)
+        is_open = jnp.where(inside, is_open, 0.0)
+        mask_ref[t * frames : (t + 1) * frames, :] = jnp.where(is_open > 0.5, 0.0, -1e30)
     for copy in copies:
         copy.wait()
 
@@ -259,7 +260,7 @@
     heads = share // HD
     block = mask_ref.shape[0]
     count = normed.shape[0] // block
-    is_open = mask_ref[...] > 0.5
+    bias = mask_ref[...]
     lane = lax.broadcasted_iota(jnp.int32, (1, share), 1)
     head_lanes = [
         ((lane >= HD * h) & (lane < HD * (h + 1))).astype(jnp.int32).astype(F32).astype(BF16)
@@ -283,12 +284,12 @@
         keys = jnp.concatenate([key * lanes for lanes in head_lanes], axis=0)
         raw = lax.dot_general(query, keys, (((1,), (1,)), ((), ())), preferred_element_type=F32)
         scores += [
-            jnp.where(is_open, raw[:, h * block : (h + 1) * block], -1e30) for h in range(heads)
+            raw[:, h * block : (h + 1) * block] + bias for h in range(heads)
         ]
     tops = [jnp.max(s, axis=-1, keepdims=True) for s in scores]
     weights_of = [jnp.exp2((s - t) * scale) for s, t in zip(scores, tops)]
-    sums = [jnp.sum(w, axis=-1, keepdims=True) for w in weights_of]
-    shares = [(w / total).astype(BF16) for w, total in zip(weights_of, sums)]
+    parts = [1.0 / jnp.sum(w, axis=-1, keepdims=True) for w in weights_of]
+    shares = [(w * part).astype(BF16) for w, part in zip(weights_of, parts)]
     attended = []
     for n, (side, at) in enumerate(units):
         value = projected[side][2][at]
@@ -401,8 +402,9 @@
 
 
 def gelu(x):
-    inner = math.sqrt(2.0 / math.pi) * (x + 0.044715 * (x * x * x))
-    return x * (0.5 * (1.0 + jnp.tanh(inner)))
+    scale = math.sqrt(2.0 / math.pi)
+    half = 0.5 * x
+    return half + half * jnp.tanh(x * (scale + (0.044715 * scale) * (x * x)))
 
 
 def pieces_of(width, size):
@@ -622,19 +624,19 @@
     full, rest = tiles_of(share)
     arrived = [received[:, :, n] for n in range(chunk_count)]
     arrived_other = [swap_y(part) for part in arrived]
-    weights = [w_qkv, qkv_other]
-    places = [(n, 0, 0, w_qkv.shape[0]) for n in range(2)]
+    weights = [qkv_other]
+    places = [(0, 0, 0, w_qkv.shape[0])]
     for n in range(2):
         first, second = ((w_out, out_core), (out_far, out_corner))[n]
         weights += [first, second, first, second]
         to = 2 * n * share
-        places += [(2, to, 0, full * LANES), (2, to + full * LANES, 0, full * LANES)]
+        places += [(1, to, 0, full * LANES), (1, to + full * LANES, 0, full * LANES)]
         to += 2 * full * LANES
-        places += [(2, to, full * LANES, rest), (2, to + rest, full * LANES, rest)]
+        places += [(1, to, full * LANES, rest), (1, to + rest, full * LANES, rest)]
     weights.append(fc2_other)
-    places.append((3, 0, 0, w_fc2.shape[0]))
-    held = (w_qkv.shape, w_qkv.shape, (4 * share, features), w_fc2.shape)
-    norm_mod, feed_mod, gate_mod, pair, mask, flag, w_qkv, qkv_other, out_all, fc2_other = prepare(
+    places.append((2, 0, 0, w_fc2.shape[0]))
+    held = (w_qkv.shape, (4 * share, features), w_fc2.shape)
+    norm_mod, feed_mod, gate_mod, pair, mask, flag, qkv_other, out_all, fc2_other = prepare(
         place, arrived[0], jnp.swapaxes(mod_table, 0, 1), keep_coef, layer_coef,
         weights, places, held, here, size * rest, block,
     )

time: 90.4 us -> 90 us (level)
  transfers between devices with their start and end apart: 17 -> 17, of which waited for: 9 -> 10; matrix products, arithmetic and copies ran while one was open for 0% -> 0% of each run, Pallas kernels for 33% -> 33%
where the time goes in v5:
time: 90 us; the launch traced here: 89.7 us
  Pallas kernels  31.4 us (35%)
  waiting for transfers between devices  24.1 us (27%)
  starting transfers between devices  18.8 us (21%)
  blocking collectives  15.3 us (17%)
    all_to_all x1, blocking collectives, on_device(): result = lax.all_to_all(result, ('frame', 'core'), 0, 0, tiled=True)  15.3 us
    pallas_call x4, Pallas kernels, attention_call(): pl.pallas_call(kernel, out_shape=outs, in_specs=[VMEM_SPEC] * len(arrays)...  11.6 us
    pallas_call x4, Pallas kernels, feed_call(): pl.pallas_call(functools.partial(feed_kernel, halves), out_shape=outs, in...  11.6 us
    ppermute x1, waiting for transfers between devices, on_device(): out_far = swap_y(w_out)  7.65 us
    ppermute x2, waiting for transfers between devices, on_device(): fed.append((current, after, feed, swap_y(feed), later))  6.61 us
    all_to_all x1, starting transfers between devices, on_device(): received = lax.all_to_all(payload, ('frame', 'core'), 0, 0, tiled=True)  5.92 us
    pallas_call x1, Pallas kernels, prepare(): pl.pallas_call(functools.partial(prepare_kernel, here, lane_at, tuple(pla...  4.64 us
    ppermute x2, waiting for transfers between devices, on_device(): parts.append((current, after, feed_here, swap_y(feed_there)))  4.3 us
  transfers between devices with their start and end apart: 17, of which 10 were waited for; matrix products, arithmetic and copies ran while one was open for 0% of the time, Pallas kernels for 33%

profile of v5, /device:TPU:0, one launch (start us, length us, event | category | flops | bytes accessed | tf_op | source)
XLA Modules:
  0.0 89.7 jit_solution(13892585236514352437)
XLA Ops:
  1.0 2.6 %collective-permute-start.2 = (bf16[288,1152]{1,0:T(8,128)(2,1)}, bf16[288,1152]{1,0:T(8,128)(2,1)}, u32[]{:S(2)}, u32[]{:S(2)}) collective-permute-start(bf16[288,1152]{1,0:T(8,128)(2,1)} %refs_3_.1), channel_id=1, source_target_pairs={{0,2},{2,0},{1,3},{3,1},{4,6},{6,4},{5,7},{7,5},{8,10},{10,8},{9,1... | collective-permute-start | bytes 1990664 | tf_op jit(solution)/shard_map/ppermute | solution.py:605
  3.7 2.1 %payload.1 = bf16[16,2,40,128]{3,2,1,0:T(8,128)(2,1)} custom-call(s32[1]{0:T(128)} %bitcast.1.frame_far, s32[8]{0:T(128)} %level_far.1, s32[8,17]{1,0:T(8,128)} %window_far.1, bf16[8,64,288]{2,1,0:T(8,128)(2,1)} %x_far.1, bf16[2,64,288]{2,1,0:T(8,128)(2,1)} %fresh_far.1), custom_call_target="tpu_custom_call" | custom-call | bytes 6600000 | tf_op jit(solution)/shard_map/payload/pallas_call | solution.py:118
  5.8 5.9 %all-to-all-start = ((bf16[16,2,40,128]{3,2,1,0:T(8,128)(2,1)}), bf16[16,2,40,128]{3,2,1,0:T(8,128)(2,1)S(1)}, u32[]{:S(2)}, u32[]{:S(2)}) async-start(bf16[16,2,40,128]{3,2,1,0:T(8,128)(2,1)} %payload.1), calls=%async_computation | async-start | bytes 655360 | tf_op jit(solution)/shard_map/all_to_all | solution.py:612
  11.7 7.7 %collective-permute-done.2.refs_5_.refs_7_ = bf16[288,1152]{1,0:T(8,128)(2,1)} collective-permute-done((bf16[288,1152]{1,0:T(8,128)(2,1)}, bf16[288,1152]{1,0:T(8,128)(2,1)}, u32[]{:S(2)}, u32[]{:S(2)}) %collective-permute-start.2) | collective-permute-done | bytes 663584 | tf_op jit(solution)/shard_map/ppermute | solution.py:605
  19.4 3.4 %all-to-all-done = bf16[16,2,40,128]{3,2,1,0:T(8,128)(2,1)S(1)} async-done(((bf16[16,2,40,128]{3,2,1,0:T(8,128)(2,1)}), bf16[16,2,40,128]{3,2,1,0:T(8,128)(2,1)S(1)}, u32[]{:S(2)}, u32[]{:S(2)}) %all-to-all-start) | async-done | bytes 327712 | tf_op jit(solution)/shard_map/all_to_all | solution.py:612
  22.9 0.6 collective-permute-start.11
  23.5 1.5 %collective-permute-start.5 = (bf16[8,2,40,128]{3,2,1,0:T(8,128)(2,1)S(1)}, bf16[8,2,40,128]{3,2,1,0:T(8,128)(2,1)S(1)}, u32[]{:S(2)}, u32[]{:S(2)}) collective-permute-start(bf16[8,2,40,128]{3,2,1,0:T(8,128)(2,1)S(1)} %get-tuple-element.74.received_ref.mine_ref), channel_id=1, source_target_pairs={{0,2},{2,0},{1,3},{3,1},{4,6},{6,4},{5,7},{7,5},{8,10},{10,8},{9,1... | collective-permute-start | bytes 491528 | tf_op jit(solution)/shard_map/ppermute | solution.py:626
  25.0 4.6 %prepare.1 = (f32[2,64,1152]{2,1,0:T(8,128)S(1)}, f32[3,64,1152]{2,1,0:T(8,128)S(1)}, f32[1,64,1152]{2,1,0:T(8,128)S(1)}, f32[64,128]{1,0:T(8,128)S(1)}, f32[128...) custom-call(s32[1]{0:T(128)} %bitcast.place_ref, ...), custom_call_target="tpu_custom_call" | custom-call | bytes 16500000 | tf_op jit(solution)/shard_map/prepare/pallas_call | solution.py:221
  30.1 2.8 %attention.6 = (bf16[128,1152]{1,0:T(8,128)(2,1)S(1)}, bf16[576,128]{1,0:T(8,128)(2,1)S(1)}, f32[2,1152]{1,0:T(2,128)S(1)}) custom-call(bf16[8,2,40,128]{3,2,1,0:T(8,128)(2,1)S(1)} %get-tuple-element.73.mine_ref, bf16[8,2,40,128]{3,2,1,0:T(8,128)(2,1)S(1)} %collective-permute-done.11.other_ref, f32[8,128]{1,0:T(8,128)S(1)} %get-tuple-element.44.flag_ref, ...), custom_call_target="tpu_custom_call" | custom-call | bytes 9240000 | tf_op jit(solution)/shard_map/attention/pallas_call | solution.py:367
  32.9 0.6 collective-permute-start.12
  33.4 2.8 %attention.4 = (bf16[128,1152]{1,0:T(8,128)(2,1)S(1)}, bf16[576,128]{1,0:T(8,128)(2,1)S(1)}, f32[2,1152]{1,0:T(2,128)S(1)}) custom-call(bf16[8,2,40,128]{3,2,1,0:T(8,128)(2,1)S(1)} %get-tuple-element.74.received_ref.mine_ref, bf16[8,2,40,128]{3,2,1,0:T(8,128)(2,1)S(1)} %collective-permute-done.5.other_ref, f32[8,128]{1,0:T(8,128)S(1)} %get-tuple-element.44.flag_ref, ...), custom_call_target="tpu_custom_call" | custom-call | bytes 9240000 | tf_op jit(solution)/shard_map/attention/pallas_call | solution.py:367
  36.2 1.6 %collective-permute-start.6 = (bf16[576,128]{1,0:T(8,128)(2,1)S(1)}, bf16[576,128]{1,0:T(8,128)(2,1)S(1)}, u32[]{:S(2)}, u32[]{:S(2)}) collective-permute-start(bf16[576,128]{1,0:T(8,128)(2,1)S(1)} %get-tuple-element.51.mine_ref), channel_id=1, source_target_pairs={{0,2},{2,0},{1,3},{3,1},{4,6},{6,4},{5,7},{7,5},{8,10},{10,8},{9,1... | collective-permute-start | bytes 442376 | tf_op jit(solution)/shard_map/ppermute | solution.py:653
  37.8 0.5 collective-permute-done.12.other_ref
  38.3 2.9 %feed.6 = (bf16[128,1152]{1,0:T(8,128)(2,1)S(1)}, bf16[128,1152]{1,0:T(8,128)(2,1)S(1)}) custom-call(f32[8,128]{1,0:T(8,128)S(1)} %get-tuple-element.44.flag_ref, bf16[128,1152]{1,0:T(8,128)(2,1)S(1)} %get-tuple-element.63.cur_ref.old_ref, bf16[576,128]{1,0:T(8,128)(2,1)S(1)} %get-tuple-element.64.mine_ref, ...), custom_call_target="tpu_custom_call" | custom-call | bytes 9240000 | tf_op jit(solution)/shard_map/feed/pallas_call | solution.py:466
  41.5 2.9 %feed.4 = (bf16[128,1152]{1,0:T(8,128)(2,1)S(1)}, bf16[128,1152]{1,0:T(8,128)(2,1)S(1)}) custom-call(f32[8,128]{1,0:T(8,128)S(1)} %get-tuple-element.44.flag_ref, bf16[128,1152]{1,0:T(8,128)(2,1)S(1)} %get-tuple-element.50.cur_ref.old_ref, bf16[576,128]{1,0:T(8,128)(2,1)S(1)} %get-tuple-element.51.mine_ref, ...), custom_call_target="tpu_custom_call" | custom-call | bytes 9240000 | tf_op jit(solution)/shard_map/feed/pallas_call | solution.py:466
  44.4 1.8 %collective-permute-start.8 = (bf16[128,1152]{1,0:T(8,128)(2,1)S(1)}, bf16[128,1152]{1,0:T(8,128)(2,1)S(1)}, u32[]{:S(2)}, u32[]{:S(2)}) collective-permute-start(bf16[128,1152]{1,0:T(8,128)(2,1)S(1)} %get-tuple-element.56.mine_ref), channel_id=1, source_target_pairs={{0,2},{2,0},{1,3},{3,1},{4,6},{6,4},{5,7},{7,5},{8,10},{10,8},{9,1... | collective-permute-start | bytes 884744 | tf_op jit(solution)/shard_map/ppermute | solution.py:658
  46.2 5.0 %collective-permute-done.13.other_ref = bf16[128,1152]{1,0:T(8,128)(2,1)S(1)} collective-permute-done((bf16[128,1152]{1,0:T(8,128)(2,1)S(1)}, bf16[128,1152]{1,0:T(8,128)(2,1)S(1)}, u32[]{:S(2)}, u32[]{:S(2)}) %collective-permute-start.13) | collective-permute-done | bytes 294944 | tf_op jit(solution)/shard_map/ppermute | solution.py:658
  51.2 3.1 %attention.7 = (bf16[128,1152]{1,0:T(8,128)(2,1)S(1)}, bf16[576,128]{1,0:T(8,128)(2,1)S(1)}) custom-call(bf16[128,1152]{1,0:T(8,128)(2,1)S(1)} %get-tuple-element.63.cur_ref.old_ref, bf16[128,1152]{1,0:T(8,128)(2,1)S(1)} %get-tuple-element.65.after_ref, bf16[128,1152]{1,0:T(8,128)(2,1)S(1)} %get-tuple-element.66.mine_ref, ...), custom_call_target="tpu_custom_call" | custom-call | bytes 9240000 | tf_op jit(solution)/shard_map/attention/pallas_call | solution.py:367
  54.6 1.7 %collective-permute-done.8.other_ref = bf16[128,1152]{1,0:T(8,128)(2,1)S(1)} collective-permute-done((bf16[128,1152]{1,0:T(8,128)(2,1)S(1)}, bf16[128,1152]{1,0:T(8,128)(2,1)S(1)}, u32[]{:S(2)}, u32[]{:S(2)}) %collective-permute-start.8) | collective-permute-done | bytes 294944 | tf_op jit(solution)/shard_map/ppermute | solution.py:658
  56.2 2.9 %attention.5 = (bf16[128,1152]{1,0:T(8,128)(2,1)S(1)}, bf16[576,128]{1,0:T(8,128)(2,1)S(1)}) custom-call(bf16[128,1152]{1,0:T(8,128)(2,1)S(1)} %get-tuple-element.50.cur_ref.old_ref, bf16[128,1152]{1,0:T(8,128)(2,1)S(1)} %get-tuple-element.55.after_ref, bf16[128,1152]{1,0:T(8,128)(2,1)S(1)} %get-tuple-element.56.mine_ref, ...), custom_call_target="tpu_custom_call" | custom-call | bytes 9240000 | tf_op jit(solution)/shard_map/attention/pallas_call | solution.py:367
  59.1 0.9 %collective-permute-start.9 = (bf16[576,128]{1,0:T(8,128)(2,1)S(1)}, bf16[576,128]{1,0:T(8,128)(2,1)S(1)}, u32[]{:S(2)}, u32[]{:S(2)}) collective-permute-start(bf16[576,128]{1,0:T(8,128)(2,1)S(1)} %get-tuple-element.59.mine_ref), channel_id=1, source_target_pairs={{0,2},{2,0},{1,3},{3,1},{4,6},{6,4},{5,7},{7,5},{8,10},{10,8},{9,1... | collective-permute-start | bytes 442376 | tf_op jit(solution)/shard_map/ppermute | solution.py:666
  60.1 0.6 collective-permute-done.14.other_ref
  60.6 2.9 %feed.7 = (bf16[128,1152]{1,0:T(8,128)(2,1)S(1)}, bf16[576,128]{1,0:T(8,128)(2,1)S(1)}, bf16[576,128]{1,0:T(8,128)(2,1)S(1)}) custom-call(f32[8,128]{1,0:T(8,128)S(1)} %get-tuple-element.44.flag_ref, bf16[128,1152]{1,0:T(8,128)(2,1)S(1)} %get-tuple-element.68.cur_ref.refs_4_, bf16[576,128]{1,0:T(8,128)(2,1)S(1)} %get-tuple-element.69.mine_ref, ...), custom_call_target="tpu_custom_call" | custom-call | bytes 9240000 | tf_op jit(solution)/shard_map/feed/pallas_call | solution.py:466
  63.5 0.6 collective-permute-start.15
  64.1 0.6 collective-permute-done.9.other_ref
  64.8 2.9 %feed.5 = (bf16[128,1152]{1,0:T(8,128)(2,1)S(1)}, bf16[576,128]{1,0:T(8,128)(2,1)S(1)}, bf16[576,128]{1,0:T(8,128)(2,1)S(1)}) custom-call(f32[8,128]{1,0:T(8,128)S(1)} %get-tuple-element.44.flag_ref, bf16[128,1152]{1,0:T(8,128)(2,1)S(1)} %get-tuple-element.58.cur_ref.refs_0_, bf16[576,128]{1,0:T(8,128)(2,1)S(1)} %get-tuple-element.59.mine_ref, ...), custom_call_target="tpu_custom_call" | custom-call | bytes 9240000 | tf_op jit(solution)/shard_map/feed/pallas_call | solution.py:466
  67.7 0.9 %collective-permute-start.10 = (bf16[576,128]{1,0:T(8,128)(2,1)S(1)}, bf16[576,128]{1,0:T(8,128)(2,1)S(1)}, u32[]{:S(2)}, u32[]{:S(2)}) collective-permute-start(bf16[576,128]{1,0:T(8,128)(2,1)S(1)} %get-tuple-element.62), channel_id=1, source_target_pairs={{0,2},{2,0},{1,3},{3,1},{4,6},{6,4},{5,7},{7,5},{8,10},{10,8},{9,1... | collective-permute-start | bytes 442376 | tf_op jit(solution)/shard_map/ppermute | solution.py:672
  68.6 0.6 collective-permute-done.15.refs_7_
  69.2 3.7 %collective-permute-done.10.refs_3_ = bf16[576,128]{1,0:T(8,128)(2,1)S(1)} collective-permute-done((bf16[576,128]{1,0:T(8,128)(2,1)S(1)}, bf16[576,128]{1,0:T(8,128)(2,1)S(1)}, u32[]{:S(2)}, u32[]{:S(2)}) %collective-permute-start.10) | collective-permute-done | bytes 147488 | tf_op jit(solution)/shard_map/ppermute | solution.py:672
  72.9 0.7 finish.1
  73.6 15.3 %all_to_all.10.rows_ref = bf16[16,72,128]{2,1,0:T(8,128)(2,1)S(1)} all-to-all(bf16[16,72,128]{2,1,0:T(8,128)(2,1)S(1)} %bitcast.17), channel_id=1, replica_groups=mesh['frame'=8,'y'=2,'core'=2] {'frame','core'}, dimensions={0} | all-to-all | bytes 589824 | tf_op jit(solution)/shard_map/all_to_all | solution.py:676
  88.8 0.9 %unpack.1 = bf16[8,64,288]{2,1,0:T(8,128)(2,1)} custom-call(bf16[16,72,128]{2,1,0:T(8,128)(2,1)S(1)} %all_to_all.10.rows_ref), custom_call_target="tpu_custom_call" | custom-call | bytes 2970000 | tf_op jit(solution)/shard_map/unpack/pallas_call | solution.py:567
  (27 shorter events, 2.3 us)
Async XLA Ops:
  0.0 25.0 %copy-start.3 = (f32[64]{0:T(128)S(1)}, f32[64]{0:T(128)}, u32[]{:S(2)}) copy-start(f32[64]{0:T(128)} %param.16) | copy-start | bytes 772
  0.0 25.0 %copy-start.4 = (f32[64]{0:T(128)S(1)}, f32[64]{0:T(128)}, u32[]{:S(2)}) copy-start(f32[64]{0:T(128)} %param.17) | copy-start | bytes 772
  0.0 22.9 %collective-permute-start.3 = (bf16[1152,1152]{1,0:T(8,128)(2,1)}, bf16[1152,1152]{1,0:T(8,128)(2,1)}, u32[]{:S(2)}, u32[]{:S(2)}) collective-permute-start(bf16[1152,1152]{1,0:T(8,128)(2,1)} %fc2_me.7), channel_id=1, source_target_pairs={{0,1},{1,0},{2,3},{3,2},{4,5},{5,4},{6,7},{7,6},{8,9},{9,8},{10,11... | collective-permute-start | bytes 7962632 | tf_op jit(solution)/shard_map/ppermute | solution.py:606
  0.5 37.3 %collective-permute-start.7 = (bf16[1152,1152]{1,0:T(8,128)(2,1)}, bf16[1152,1152]{1,0:T(8,128)(2,1)S(1)}, u32[]{:S(2)}, u32[]{:S(2)}) collective-permute-start(bf16[1152,1152]{1,0:T(8,128)(2,1)} %fc1_me.7), channel_id=1, source_target_pairs={{0,1},{1,0},{2,3},{3,2},{4,5},{5,4},{6,7},{7,6},{8,9},{9,8},{10,11... | collective-permute-start | bytes 7962632 | tf_op jit(solution)/shard_map/ppermute | solution.py:654
  0.5 22.3 %collective-permute-start = (bf16[3,288,1152]{2,1,0:T(8,128)(2,1)}, bf16[3,288,1152]{2,1,0:T(8,128)(2,1)}, u32[]{:S(2)}, u32[]{:S(2)}) collective-permute-start(bf16[3,288,1152]{2,1,0:T(8,128)(2,1)} %bitcast.12), channel_id=1, source_target_pairs={{0,1},{1,0},{2,3},{3,2},{4,5},{5,4},{6,7},{7,6},{8,9},{9,8},{10,11... | collective-permute-start | bytes 5971976 | tf_op jit(solution)/shard_map/ppermute | solution.py:604
  1.0 18.4 %collective-permute-start.2 = (bf16[288,1152]{1,0:T(8,128)(2,1)}, bf16[288,1152]{1,0:T(8,128)(2,1)}, u32[]{:S(2)}, u32[]{:S(2)}) collective-permute-start(bf16[288,1152]{1,0:T(8,128)(2,1)} %refs_3_.1), channel_id=1, source_target_pairs={{0,2},{2,0},{1,3},{3,1},{4,6},{6,4},{5,7},{7,5},{8,10},{10,8},{9,1... | collective-permute-start | bytes 1990664 | tf_op jit(solution)/shard_map/ppermute | solution.py:605
  3.6 19.3 %collective-permute-start.1 = (bf16[288,1152]{1,0:T(8,128)(2,1)}, bf16[288,1152]{1,0:T(8,128)(2,1)}, u32[]{:S(2)}, u32[]{:S(2)}) collective-permute-start(bf16[288,1152]{1,0:T(8,128)(2,1)} %refs_3_.1), channel_id=1, source_target_pairs={{0,1},{1,0},{2,3},{3,2},{4,5},{5,4},{6,7},{7,6},{8,9},{9,8},{10,11... | collective-permute-start | bytes 1990664 | tf_op jit(solution)/shard_map/ppermute | solution.py:606
  5.8 17.0 %all-to-all-start = ((bf16[16,2,40,128]{3,2,1,0:T(8,128)(2,1)}), bf16[16,2,40,128]{3,2,1,0:T(8,128)(2,1)S(1)}, u32[]{:S(2)}, u32[]{:S(2)}) async-start(bf16[16,2,40,128]{3,2,1,0:T(8,128)(2,1)} %payload.1), calls=%async_computation | async-start | bytes 655360 | tf_op jit(solution)/shard_map/all_to_all | solution.py:612
  19.4 5.6 %collective-permute-start.4 = (bf16[288,1152]{1,0:T(8,128)(2,1)}, bf16[288,1152]{1,0:T(8,128)(2,1)}, u32[]{:S(2)}, u32[]{:S(2)}) collective-permute-start(bf16[288,1152]{1,0:T(8,128)(2,1)} %collective-permute-done.2.refs_5_.refs_7_), channel_id=1, source_target_pairs={{0,1},{1,0},{2,3},{3,2},{4,5},{5,4},{6,7},{7,6},{8,9},{9,8},{10,11... | collective-permute-start | bytes 1990664 | tf_op jit(solution)/shard_map/ppermute | solution.py:606
  22.9 7.1 %collective-permute-start.11 = (bf16[8,2,40,128]{3,2,1,0:T(8,128)(2,1)S(1)}, bf16[8,2,40,128]{3,2,1,0:T(8,128)(2,1)S(1)}, u32[]{:S(2)}, u32[]{:S(2)}) collective-permute-start(bf16[8,2,40,128]{3,2,1,0:T(8,128)(2,1)S(1)} %get-tuple-element.73.mine_ref), channel_id=1, source_target_pairs={{0,2},{2,0},{1,3},{3,1},{4,6},{6,4},{5,7},{7,5},{8,10},{10,8},{9,1... | collective-permute-start | bytes 491528 | tf_op jit(solution)/shard_map/ppermute | solution.py:626
  23.5 9.9 %collective-permute-start.5 = (bf16[8,2,40,128]{3,2,1,0:T(8,128)(2,1)S(1)}, bf16[8,2,40,128]{3,2,1,0:T(8,128)(2,1)S(1)}, u32[]{:S(2)}, u32[]{:S(2)}) collective-permute-start(bf16[8,2,40,128]{3,2,1,0:T(8,128)(2,1)S(1)} %get-tuple-element.74.received_ref.mine_ref), channel_id=1, source_target_pairs={{0,2},{2,0},{1,3},{3,1},{4,6},{6,4},{5,7},{7,5},{8,10},{10,8},{9,1... | collective-permute-start | bytes 491528 | tf_op jit(solution)/shard_map/ppermute | solution.py:626
  25.0 5.0 %copy-start.2 = (bf16[3,1152,288]{1,2,0:T(8,128)(2,1)S(1)}, bf16[3,1152,288]{1,2,0:T(8,128)(2,1)}, u32[]{:S(2)}) copy-start(bf16[3,1152,288]{1,2,0:T(8,128)(2,1)} %param.18) | copy-start | bytes 5971972
  30.0 8.2 %copy-start.1 = (bf16[1152,1152]{1,0:T(8,128)(2,1)S(1)}, bf16[1152,1152]{1,0:T(8,128)(2,1)}, u32[]{:S(2)}) copy-start(bf16[1152,1152]{1,0:T(8,128)(2,1)} %fc1_me.7) | copy-start | bytes 7962628
  32.9 5.4 %copy-start = (bf16[1152,1152]{1,0:T(8,128)(2,1)S(1)}, bf16[1152,1152]{1,0:T(8,128)(2,1)}, u32[]{:S(2)}) copy-start(bf16[1152,1152]{1,0:T(8,128)(2,1)} %fc2_me.7) | copy-start | bytes 7962628
  32.9 5.4 %collective-permute-start.12 = (bf16[576,128]{1,0:T(8,128)(2,1)S(1)}, bf16[576,128]{1,0:T(8,128)(2,1)S(1)}, u32[]{:S(2)}, u32[]{:S(2)}) collective-permute-start(bf16[576,128]{1,0:T(8,128)(2,1)S(1)} %get-tuple-element.64.mine_ref), channel_id=1, source_target_pairs={{0,2},{2,0},{1,3},{3,1},{4,6},{6,4},{5,7},{7,5},{8,10},{10,8},{9,1... | collective-permute-start | bytes 442376 | tf_op jit(solution)/shard_map/ppermute | solution.py:653
  36.2 5.3 %collective-permute-start.6 = (bf16[576,128]{1,0:T(8,128)(2,1)S(1)}, bf16[576,128]{1,0:T(8,128)(2,1)S(1)}, u32[]{:S(2)}, u32[]{:S(2)}) collective-permute-start(bf16[576,128]{1,0:T(8,128)(2,1)S(1)} %get-tuple-element.51.mine_ref), channel_id=1, source_target_pairs={{0,2},{2,0},{1,3},{3,1},{4,6},{6,4},{5,7},{7,5},{8,10},{10,8},{9,1... | collective-permute-start | bytes 442376 | tf_op jit(solution)/shard_map/ppermute | solution.py:653
  41.2 10.0 %collective-permute-start.13 = (bf16[128,1152]{1,0:T(8,128)(2,1)S(1)}, bf16[128,1152]{1,0:T(8,128)(2,1)S(1)}, u32[]{:S(2)}, u32[]{:S(2)}) collective-permute-start(bf16[128,1152]{1,0:T(8,128)(2,1)S(1)} %get-tuple-element.66.mine_ref), channel_id=1, source_target_pairs={{0,2},{2,0},{1,3},{3,1},{4,6},{6,4},{5,7},{7,5},{8,10},{10,8},{9,1... | collective-permute-start | bytes 884744 | tf_op jit(solution)/shard_map/ppermute | solution.py:658
  44.4 11.8 %collective-permute-start.8 = (bf16[128,1152]{1,0:T(8,128)(2,1)S(1)}, bf16[128,1152]{1,0:T(8,128)(2,1)S(1)}, u32[]{:S(2)}, u32[]{:S(2)}) collective-permute-start(bf16[128,1152]{1,0:T(8,128)(2,1)S(1)} %get-tuple-element.56.mine_ref), channel_id=1, source_target_pairs={{0,2},{2,0},{1,3},{3,1},{4,6},{6,4},{5,7},{7,5},{8,10},{10,8},{9,1... | collective-permute-start | bytes 884744 | tf_op jit(solution)/shard_map/ppermute | solution.py:658
  54.2 6.4 %collective-permute-start.14 = (bf16[576,128]{1,0:T(8,128)(2,1)S(1)}, bf16[576,128]{1,0:T(8,128)(2,1)S(1)}, u32[]{:S(2)}, u32[]{:S(2)}) collective-permute-start(bf16[576,128]{1,0:T(8,128)(2,1)S(1)} %get-tuple-element.69.mine_ref), channel_id=1, source_target_pairs={{0,2},{2,0},{1,3},{3,1},{4,6},{6,4},{5,7},{7,5},{8,10},{10,8},{9,1... | collective-permute-start | bytes 442376 | tf_op jit(solution)/shard_map/ppermute | solution.py:666
  59.1 5.7 %collective-permute-start.9 = (bf16[576,128]{1,0:T(8,128)(2,1)S(1)}, bf16[576,128]{1,0:T(8,128)(2,1)S(1)}, u32[]{:S(2)}, u32[]{:S(2)}) collective-permute-start(bf16[576,128]{1,0:T(8,128)(2,1)S(1)} %get-tuple-element.59.mine_ref), channel_id=1, source_target_pairs={{0,2},{2,0},{1,3},{3,1},{4,6},{6,4},{5,7},{7,5},{8,10},{10,8},{9,1... | collective-permute-start | bytes 442376 | tf_op jit(solution)/shard_map/ppermute | solution.py:666
  63.5 5.6 %collective-permute-start.15 = (bf16[576,128]{1,0:T(8,128)(2,1)S(1)}, bf16[576,128]{1,0:T(8,128)(2,1)S(1)}, u32[]{:S(2)}, u32[]{:S(2)}) collective-permute-start(bf16[576,128]{1,0:T(8,128)(2,1)S(1)} %get-tuple-element.72), channel_id=1, source_target_pairs={{0,2},{2,0},{1,3},{3,1},{4,6},{6,4},{5,7},{7,5},{8,10},{10,8},{9,1... | collective-permute-start | bytes 442376 | tf_op jit(solution)/shard_map/ppermute | solution.py:672
  67.7 5.2 %collective-permute-start.10 = (bf16[576,128]{1,0:T(8,128)(2,1)S(1)}, bf16[576,128]{1,0:T(8,128)(2,1)S(1)}, u32[]{:S(2)}, u32[]{:S(2)}) collective-permute-start(bf16[576,128]{1,0:T(8,128)(2,1)S(1)} %get-tuple-element.62), channel_id=1, source_target_pairs={{0,2},{2,0},{1,3},{3,1},{4,6},{6,4},{5,7},{7,5},{8,10},{10,8},{9,1... | collective-permute-start | bytes 442376 | tf_op jit(solution)/shard_map/ppermute | solution.py:672

commit v6 on v5

--- a/solution.py
+++ b/solution.py
@@ -46,11 +46,11 @@
 
 
 def payload_kernel(
-    frames, frame_far, level_far, window_far, x_far, fresh_far, out_ref,
-    rows_ref, frame_ref, level_ref, window_ref, x_ref, fresh_ref, sems,
+    frames, x_ref, frame_far, level_far, window_far, fresh_far, out_ref,
+    rows_ref, frame_ref, level_ref, window_ref, fresh_ref, sems,
 ):
-    fars = (x_far, window_far, level_far, frame_far, fresh_far)
-    nears = (x_ref, window_ref, level_ref, frame_ref, fresh_ref)
+    fars = (window_far, level_far, frame_far, fresh_far)
+    nears = (window_ref, level_ref, frame_ref, fresh_ref)
     copies = [pltpu.make_async_copy(a, b, sems.at[n]) for n, (a, b) in enumerate(zip(fars, nears))]
     for copy in copies:
         copy.start()
@@ -118,21 +118,20 @@
     return pl.pallas_call(
         functools.partial(payload_kernel, frames),
         out_shape=out,
-        in_specs=[HBM_SPEC] * 5,
+        in_specs=[VMEM_SPEC] + [HBM_SPEC] * 4,
         out_specs=VMEM_SPEC,
         scratch_shapes=[
             pltpu.VMEM(scratch.shape, F32),
             pltpu.SMEM(frame_index.shape, jnp.int32),
             pltpu.SMEM(noise_level.shape, jnp.int32),
             pltpu.VMEM(window_mask.shape, jnp.int32),
-            pltpu.VMEM(x.shape, BF16),
             pltpu.VMEM(fresh.shape, BF16),
-            pltpu.SemaphoreType.DMA((5,)),
+            pltpu.SemaphoreType.DMA((4,)),
         ],
         compiler_params=params(x, fresh, out, scratch),
         cost_estimate=takes(2),
         name="payload",
-    )(*in_hbm(frame_index, noise_level, window_mask, x, fresh))
+    )(x, *in_hbm(frame_index, noise_level, window_mask, fresh))
 
 
 def fresh_piece(block, size, here, share):

time: 90 us -> 89.5 us (level)
  blocking collectives: 15.3 us -> 13.8 us
  local copies, waits for them, and re-layouts: 0.08 us -> 1.08 us
    all_to_all x1, blocking collectives: 15.3 us -> 13.8 us  [on_device(): result = lax.all_to_all(result, ('frame', 'core'), 0, 0, tiled=True)]
    unnamed x10 -> x12, local copies, waits for them, and re-layouts: 0.02 us -> 1.02 us
where the time goes in v6:
time: 89.5 us; the launch traced here: 89.2 us
  Pallas kernels  31.3 us (35%)
  waiting for transfers between devices  24.1 us (27%)
  starting transfers between devices  18.8 us (21%)
  blocking collectives  13.8 us (15%)
  local copies, waits for them, and re-layouts  1.08 us (1%)
    all_to_all x1, blocking collectives, on_device(): result = lax.all_to_all(result, ('frame', 'core'), 0, 0, tiled=True)  13.8 us
    pallas_call x4, Pallas kernels, attention_call(): pl.pallas_call(kernel, out_shape=outs, in_specs=[VMEM_SPEC] * len(arrays)...  11.6 us
    pallas_call x4, Pallas kernels, feed_call(): pl.pallas_call(functools.partial(feed_kernel, halves), out_shape=outs, in...  11.6 us
    ppermute x1, waiting for transfers between devices, on_device(): out_far = swap_y(w_out)  6.77 us
    ppermute x2, waiting for transfers between devices, on_device(): fed.append((current, after, feed, swap_y(feed), later))  6.61 us
    all_to_all x1, starting transfers between devices, on_device(): received = lax.all_to_all(payload, ('frame', 'core'), 0, 0, tiled=True)  5.92 us
    pallas_call x1, Pallas kernels, prepare(): pl.pallas_call(functools.partial(prepare_kernel, here, lane_at, tuple(pla...  4.64 us
    all_to_all x1, waiting for transfers between devices, on_device(): received = lax.all_to_all(payload, ('frame', 'core'), 0, 0, tiled=True)  4.32 us
  transfers between devices with their start and end apart: 17, of which 10 were waited for; matrix products, arithmetic and copies ran while one was open for 0% of the time, Pallas kernels for 33%

profile of v6, /device:TPU:0, one launch (start us, length us, event | category | flops | bytes accessed | tf_op | source)
XLA Modules:
  0.0 89.2 jit_solution(863791060510519274)
XLA Ops:
  1.0 2.6 %collective-permute-start.2 = (bf16[288,1152]{1,0:T(8,128)(2,1)}, bf16[288,1152]{1,0:T(8,128)(2,1)}, u32[]{:S(2)}, u32[]{:S(2)}) collective-permute-start(bf16[288,1152]{1,0:T(8,128)(2,1)} %refs_3_.1), channel_id=1, source_target_pairs={{0,2},{2,0},{1,3},{3,1},{4,6},{6,4},{5,7},{7,5},{8,10},{10,8},{9,1... | collective-permute-start | bytes 1990664 | tf_op jit(solution)/shard_map/ppermute | solution.py:604
  3.7 1.0 %copy-done.3 = bf16[8,64,288]{2,1,0:T(8,128)(2,1)S(1)} copy-done((bf16[8,64,288]{2,1,0:T(8,128)(2,1)S(1)}, bf16[8,64,288]{2,1,0:T(8,128)(2,1)}, u32[]{:S(2)}) %copy-start.3) | copy-done | bytes 294936
  4.7 1.9 %payload.1 = bf16[16,2,40,128]{3,2,1,0:T(8,128)(2,1)} custom-call(bf16[8,64,288]{2,1,0:T(8,128)(2,1)S(1)} %copy-done.3, s32[1]{0:T(128)} %bitcast.1.frame_far, s32[8]{0:T(128)} %level_far.1, s32[8,17]{1,0:T(8,128)} %window_far.1, bf16[2,64,288]{2,1,0:T(8,128)(2,1)} %fresh_far.1), custom_call_target="tpu_custom_call" | custom-call | bytes 6600000 | tf_op jit(solution)/shard_map/payload/pallas_call | solution.py:118
  6.7 5.9 %all-to-all-start = ((bf16[16,2,40,128]{3,2,1,0:T(8,128)(2,1)}), bf16[16,2,40,128]{3,2,1,0:T(8,128)(2,1)S(1)}, u32[]{:S(2)}, u32[]{:S(2)}) async-start(bf16[16,2,40,128]{3,2,1,0:T(8,128)(2,1)} %payload.1), calls=%async_computation | async-start | bytes 655360 | tf_op jit(solution)/shard_map/all_to_all | solution.py:611
  12.6 6.8 %collective-permute-done.2.refs_5_.refs_7_ = bf16[288,1152]{1,0:T(8,128)(2,1)} collective-permute-done((bf16[288,1152]{1,0:T(8,128)(2,1)}, bf16[288,1152]{1,0:T(8,128)(2,1)}, u32[]{:S(2)}, u32[]{:S(2)}) %collective-permute-start.2) | collective-permute-done | bytes 663584 | tf_op jit(solution)/shard_map/ppermute | solution.py:604
  19.4 4.3 %all-to-all-done = bf16[16,2,40,128]{3,2,1,0:T(8,128)(2,1)S(1)} async-done(((bf16[16,2,40,128]{3,2,1,0:T(8,128)(2,1)}), bf16[16,2,40,128]{3,2,1,0:T(8,128)(2,1)S(1)}, u32[]{:S(2)}, u32[]{:S(2)}) %all-to-all-start) | async-done | bytes 327712 | tf_op jit(solution)/shard_map/all_to_all | solution.py:611
  23.8 0.6 collective-permute-start.11
  24.4 1.5 %collective-permute-start.5 = (bf16[8,2,40,128]{3,2,1,0:T(8,128)(2,1)S(1)}, bf16[8,2,40,128]{3,2,1,0:T(8,128)(2,1)S(1)}, u32[]{:S(2)}, u32[]{:S(2)}) collective-permute-start(bf16[8,2,40,128]{3,2,1,0:T(8,128)(2,1)S(1)} %get-tuple-element.74.received_ref.mine_ref), channel_id=1, source_target_pairs={{0,2},{2,0},{1,3},{3,1},{4,6},{6,4},{5,7},{7,5},{8,10},{10,8},{9,1... | collective-permute-start | bytes 491528 | tf_op jit(solution)/shard_map/ppermute | solution.py:625
  25.9 4.6 %prepare.1 = (f32[2,64,1152]{2,1,0:T(8,128)S(1)}, f32[3,64,1152]{2,1,0:T(8,128)S(1)}, f32[1,64,1152]{2,1,0:T(8,128)S(1)}, f32[64,128]{1,0:T(8,128)S(1)}, f32[128...) custom-call(s32[1]{0:T(128)} %bitcast.place_ref, ...), custom_call_target="tpu_custom_call" | custom-call | bytes 16500000 | tf_op jit(solution)/shard_map/prepare/pallas_call | solution.py:220
  30.9 2.8 %attention.6 = (bf16[128,1152]{1,0:T(8,128)(2,1)S(1)}, bf16[576,128]{1,0:T(8,128)(2,1)S(1)}, f32[2,1152]{1,0:T(2,128)S(1)}) custom-call(bf16[8,2,40,128]{3,2,1,0:T(8,128)(2,1)S(1)} %get-tuple-element.73.mine_ref, bf16[8,2,40,128]{3,2,1,0:T(8,128)(2,1)S(1)} %collective-permute-done.11.other_ref, f32[8,128]{1,0:T(8,128)S(1)} %get-tuple-element.44.flag_ref, ...), custom_call_target="tpu_custom_call" | custom-call | bytes 9240000 | tf_op jit(solution)/shard_map/attention/pallas_call | solution.py:366
  33.7 0.6 collective-permute-start.12
  34.3 2.8 %attention.4 = (bf16[128,1152]{1,0:T(8,128)(2,1)S(1)}, bf16[576,128]{1,0:T(8,128)(2,1)S(1)}, f32[2,1152]{1,0:T(2,128)S(1)}) custom-call(bf16[8,2,40,128]{3,2,1,0:T(8,128)(2,1)S(1)} %get-tuple-element.74.received_ref.mine_ref, bf16[8,2,40,128]{3,2,1,0:T(8,128)(2,1)S(1)} %collective-permute-done.5.other_ref, f32[8,128]{1,0:T(8,128)S(1)} %get-tuple-element.44.flag_ref, ...), custom_call_target="tpu_custom_call" | custom-call | bytes 9240000 | tf_op jit(solution)/shard_map/attention/pallas_call | solution.py:366
  37.1 1.6 %collective-permute-start.6 = (bf16[576,128]{1,0:T(8,128)(2,1)S(1)}, bf16[576,128]{1,0:T(8,128)(2,1)S(1)}, u32[]{:S(2)}, u32[]{:S(2)}) collective-permute-start(bf16[576,128]{1,0:T(8,128)(2,1)S(1)} %get-tuple-element.51.mine_ref), channel_id=1, source_target_pairs={{0,2},{2,0},{1,3},{3,1},{4,6},{6,4},{5,7},{7,5},{8,10},{10,8},{9,1... | collective-permute-start | bytes 442376 | tf_op jit(solution)/shard_map/ppermute | solution.py:652
  39.1 2.9 %feed.6 = (bf16[128,1152]{1,0:T(8,128)(2,1)S(1)}, bf16[128,1152]{1,0:T(8,128)(2,1)S(1)}) custom-call(f32[8,128]{1,0:T(8,128)S(1)} %get-tuple-element.44.flag_ref, bf16[128,1152]{1,0:T(8,128)(2,1)S(1)} %get-tuple-element.63.cur_ref.old_ref, bf16[576,128]{1,0:T(8,128)(2,1)S(1)} %get-tuple-element.64.mine_ref, ...), custom_call_target="tpu_custom_call" | custom-call | bytes 9240000 | tf_op jit(solution)/shard_map/feed/pallas_call | solution.py:465
  42.4 2.9 %feed.4 = (bf16[128,1152]{1,0:T(8,128)(2,1)S(1)}, bf16[128,1152]{1,0:T(8,128)(2,1)S(1)}) custom-call(f32[8,128]{1,0:T(8,128)S(1)} %get-tuple-element.44.flag_ref, bf16[128,1152]{1,0:T(8,128)(2,1)S(1)} %get-tuple-element.50.cur_ref.old_ref, bf16[576,128]{1,0:T(8,128)(2,1)S(1)} %get-tuple-element.51.mine_ref, ...), custom_call_target="tpu_custom_call" | custom-call | bytes 9240000 | tf_op jit(solution)/shard_map/feed/pallas_call | solution.py:465
  45.3 1.8 %collective-permute-start.8 = (bf16[128,1152]{1,0:T(8,128)(2,1)S(1)}, bf16[128,1152]{1,0:T(8,128)(2,1)S(1)}, u32[]{:S(2)}, u32[]{:S(2)}) collective-permute-start(bf16[128,1152]{1,0:T(8,128)(2,1)S(1)} %get-tuple-element.56.mine_ref), channel_id=1, source_target_pairs={{0,2},{2,0},{1,3},{3,1},{4,6},{6,4},{5,7},{7,5},{8,10},{10,8},{9,1... | collective-permute-start | bytes 884744 | tf_op jit(solution)/shard_map/ppermute | solution.py:657
  47.1 5.0 %collective-permute-done.13.other_ref = bf16[128,1152]{1,0:T(8,128)(2,1)S(1)} collective-permute-done((bf16[128,1152]{1,0:T(8,128)(2,1)S(1)}, bf16[128,1152]{1,0:T(8,128)(2,1)S(1)}, u32[]{:S(2)}, u32[]{:S(2)}) %collective-permute-start.13) | collective-permute-done | bytes 294944 | tf_op jit(solution)/shard_map/ppermute | solution.py:657
  52.0 3.1 %attention.7 = (bf16[128,1152]{1,0:T(8,128)(2,1)S(1)}, bf16[576,128]{1,0:T(8,128)(2,1)S(1)}) custom-call(bf16[128,1152]{1,0:T(8,128)(2,1)S(1)} %get-tuple-element.63.cur_ref.old_ref, bf16[128,1152]{1,0:T(8,128)(2,1)S(1)} %get-tuple-element.65.after_ref, bf16[128,1152]{1,0:T(8,128)(2,1)S(1)} %get-tuple-element.66.mine_ref, ...), custom_call_target="tpu_custom_call" | custom-call | bytes 9240000 | tf_op jit(solution)/shard_map/attention/pallas_call | solution.py:366
  55.5 1.7 %collective-permute-done.8.other_ref = bf16[128,1152]{1,0:T(8,128)(2,1)S(1)} collective-permute-done((bf16[128,1152]{1,0:T(8,128)(2,1)S(1)}, bf16[128,1152]{1,0:T(8,128)(2,1)S(1)}, u32[]{:S(2)}, u32[]{:S(2)}) %collective-permute-start.8) | collective-permute-done | bytes 294944 | tf_op jit(solution)/shard_map/ppermute | solution.py:657
  57.1 2.9 %attention.5 = (bf16[128,1152]{1,0:T(8,128)(2,1)S(1)}, bf16[576,128]{1,0:T(8,128)(2,1)S(1)}) custom-call(bf16[128,1152]{1,0:T(8,128)(2,1)S(1)} %get-tuple-element.50.cur_ref.old_ref, bf16[128,1152]{1,0:T(8,128)(2,1)S(1)} %get-tuple-element.55.after_ref, bf16[128,1152]{1,0:T(8,128)(2,1)S(1)} %get-tuple-element.56.mine_ref, ...), custom_call_target="tpu_custom_call" | custom-call | bytes 9240000 | tf_op jit(solution)/shard_map/attention/pallas_call | solution.py:366
  60.0 0.9 %collective-permute-start.9 = (bf16[576,128]{1,0:T(8,128)(2,1)S(1)}, bf16[576,128]{1,0:T(8,128)(2,1)S(1)}, u32[]{:S(2)}, u32[]{:S(2)}) collective-permute-start(bf16[576,128]{1,0:T(8,128)(2,1)S(1)} %get-tuple-element.59.mine_ref), channel_id=1, source_target_pairs={{0,2},{2,0},{1,3},{3,1},{4,6},{6,4},{5,7},{7,5},{8,10},{10,8},{9,1... | collective-permute-start | bytes 442376 | tf_op jit(solution)/shard_map/ppermute | solution.py:665
  60.9 0.6 collective-permute-done.14.other_ref
  61.5 2.9 %feed.7 = (bf16[128,1152]{1,0:T(8,128)(2,1)S(1)}, bf16[576,128]{1,0:T(8,128)(2,1)S(1)}, bf16[576,128]{1,0:T(8,128)(2,1)S(1)}) custom-call(f32[8,128]{1,0:T(8,128)S(1)} %get-tuple-element.44.flag_ref, bf16[128,1152]{1,0:T(8,128)(2,1)S(1)} %get-tuple-element.68.cur_ref.refs_4_, bf16[576,128]{1,0:T(8,128)(2,1)S(1)} %get-tuple-element.69.mine_ref, ...), custom_call_target="tpu_custom_call" | custom-call | bytes 9240000 | tf_op jit(solution)/shard_map/feed/pallas_call | solution.py:465
  64.4 0.6 collective-permute-start.15
  65.0 0.6 collective-permute-done.9.other_ref
  65.7 2.9 %feed.5 = (bf16[128,1152]{1,0:T(8,128)(2,1)S(1)}, bf16[576,128]{1,0:T(8,128)(2,1)S(1)}, bf16[576,128]{1,0:T(8,128)(2,1)S(1)}) custom-call(f32[8,128]{1,0:T(8,128)S(1)} %get-tuple-element.44.flag_ref, bf16[128,1152]{1,0:T(8,128)(2,1)S(1)} %get-tuple-element.58.cur_ref.refs_0_, bf16[576,128]{1,0:T(8,128)(2,1)S(1)} %get-tuple-element.59.mine_ref, ...), custom_call_target="tpu_custom_call" | custom-call | bytes 9240000 | tf_op jit(solution)/shard_map/feed/pallas_call | solution.py:465
  68.6 0.9 %collective-permute-start.10 = (bf16[576,128]{1,0:T(8,128)(2,1)S(1)}, bf16[576,128]{1,0:T(8,128)(2,1)S(1)}, u32[]{:S(2)}, u32[]{:S(2)}) collective-permute-start(bf16[576,128]{1,0:T(8,128)(2,1)S(1)} %get-tuple-element.62), channel_id=1, source_target_pairs={{0,2},{2,0},{1,3},{3,1},{4,6},{6,4},{5,7},{7,5},{8,10},{10,8},{9,1... | collective-permute-start | bytes 442376 | tf_op jit(solution)/shard_map/ppermute | solution.py:671
  69.5 0.6 collective-permute-done.15.refs_7_
  70.0 3.7 %collective-permute-done.10.refs_3_ = bf16[576,128]{1,0:T(8,128)(2,1)S(1)} collective-permute-done((bf16[576,128]{1,0:T(8,128)(2,1)S(1)}, bf16[576,128]{1,0:T(8,128)(2,1)S(1)}, u32[]{:S(2)}, u32[]{:S(2)}) %collective-permute-start.10) | collective-permute-done | bytes 147488 | tf_op jit(solution)/shard_map/ppermute | solution.py:671
  73.8 0.7 finish.1
  74.4 13.8 %all_to_all.10.rows_ref = bf16[16,72,128]{2,1,0:T(8,128)(2,1)S(1)} all-to-all(bf16[16,72,128]{2,1,0:T(8,128)(2,1)S(1)} %bitcast.17), channel_id=1, replica_groups=mesh['frame'=8,'y'=2,'core'=2] {'frame','core'}, dimensions={0} | all-to-all | bytes 589824 | tf_op jit(solution)/shard_map/all_to_all | solution.py:675
  88.2 0.9 %unpack.1 = bf16[8,64,288]{2,1,0:T(8,128)(2,1)} custom-call(bf16[16,72,128]{2,1,0:T(8,128)(2,1)S(1)} %all_to_all.10.rows_ref), custom_call_target="tpu_custom_call" | custom-call | bytes 2970000 | tf_op jit(solution)/shard_map/unpack/pallas_call | solution.py:566
  (29 shorter events, 2.8 us)
Async XLA Ops:
  0.0 25.9 %copy-start.4 = (f32[64]{0:T(128)S(1)}, f32[64]{0:T(128)}, u32[]{:S(2)}) copy-start(f32[64]{0:T(128)} %param.16) | copy-start | bytes 772
  0.0 25.9 %copy-start.5 = (f32[64]{0:T(128)S(1)}, f32[64]{0:T(128)}, u32[]{:S(2)}) copy-start(f32[64]{0:T(128)} %param.17) | copy-start | bytes 772
  0.0 23.8 %collective-permute-start.3 = (bf16[1152,1152]{1,0:T(8,128)(2,1)}, bf16[1152,1152]{1,0:T(8,128)(2,1)}, u32[]{:S(2)}, u32[]{:S(2)}) collective-permute-start(bf16[1152,1152]{1,0:T(8,128)(2,1)} %fc2_me.7), channel_id=1, source_target_pairs={{0,1},{1,0},{2,3},{3,2},{4,5},{5,4},{6,7},{7,6},{8,9},{9,8},{10,11... | collective-permute-start | bytes 7962632 | tf_op jit(solution)/shard_map/ppermute | solution.py:605
  0.5 38.2 %collective-permute-start.7 = (bf16[1152,1152]{1,0:T(8,128)(2,1)}, bf16[1152,1152]{1,0:T(8,128)(2,1)S(1)}, u32[]{:S(2)}, u32[]{:S(2)}) collective-permute-start(bf16[1152,1152]{1,0:T(8,128)(2,1)} %fc1_me.7), channel_id=1, source_target_pairs={{0,1},{1,0},{2,3},{3,2},{4,5},{5,4},{6,7},{7,6},{8,9},{9,8},{10,11... | collective-permute-start | bytes 7962632 | tf_op jit(solution)/shard_map/ppermute | solution.py:653
  0.5 23.2 %collective-permute-start = (bf16[3,288,1152]{2,1,0:T(8,128)(2,1)}, bf16[3,288,1152]{2,1,0:T(8,128)(2,1)}, u32[]{:S(2)}, u32[]{:S(2)}) collective-permute-start(bf16[3,288,1152]{2,1,0:T(8,128)(2,1)} %bitcast.12), channel_id=1, source_target_pairs={{0,1},{1,0},{2,3},{3,2},{4,5},{5,4},{6,7},{7,6},{8,9},{9,8},{10,11... | collective-permute-start | bytes 5971976 | tf_op jit(solution)/shard_map/ppermute | solution.py:603
  1.0 18.4 %collective-permute-start.2 = (bf16[288,1152]{1,0:T(8,128)(2,1)}, bf16[288,1152]{1,0:T(8,128)(2,1)}, u32[]{:S(2)}, u32[]{:S(2)}) collective-permute-start(bf16[288,1152]{1,0:T(8,128)(2,1)} %refs_3_.1), channel_id=1, source_target_pairs={{0,2},{2,0},{1,3},{3,1},{4,6},{6,4},{5,7},{7,5},{8,10},{10,8},{9,1... | collective-permute-start | bytes 1990664 | tf_op jit(solution)/shard_map/ppermute | solution.py:604
  3.6 20.2 %collective-permute-start.1 = (bf16[288,1152]{1,0:T(8,128)(2,1)}, bf16[288,1152]{1,0:T(8,128)(2,1)}, u32[]{:S(2)}, u32[]{:S(2)}) collective-permute-start(bf16[288,1152]{1,0:T(8,128)(2,1)} %refs_3_.1), channel_id=1, source_target_pairs={{0,1},{1,0},{2,3},{3,2},{4,5},{5,4},{6,7},{7,6},{8,9},{9,8},{10,11... | collective-permute-start | bytes 1990664 | tf_op jit(solution)/shard_map/ppermute | solution.py:605
  3.7 1.0 %copy-start.3 = (bf16[8,64,288]{2,1,0:T(8,128)(2,1)S(1)}, bf16[8,64,288]{2,1,0:T(8,128)(2,1)}, u32[]{:S(2)}) copy-start(bf16[8,64,288]{2,1,0:T(8,128)(2,1)} %x_ref.1) | copy-start | bytes 884740
  6.7 17.0 %all-to-all-start = ((bf16[16,2,40,128]{3,2,1,0:T(8,128)(2,1)}), bf16[16,2,40,128]{3,2,1,0:T(8,128)(2,1)S(1)}, u32[]{:S(2)}, u32[]{:S(2)}) async-start(bf16[16,2,40,128]{3,2,1,0:T(8,128)(2,1)} %payload.1), calls=%async_computation | async-start | bytes 655360 | tf_op jit(solution)/shard_map/all_to_all | solution.py:611
  19.4 6.5 %collective-permute-start.4 = (bf16[288,1152]{1,0:T(8,128)(2,1)}, bf16[288,1152]{1,0:T(8,128)(2,1)}, u32[]{:S(2)}, u32[]{:S(2)}) collective-permute-start(bf16[288,1152]{1,0:T(8,128)(2,1)} %collective-permute-done.2.refs_5_.refs_7_), channel_id=1, source_target_pairs={{0,1},{1,0},{2,3},{3,2},{4,5},{5,4},{6,7},{7,6},{8,9},{9,8},{10,11... | collective-permute-start | bytes 1990664 | tf_op jit(solution)/shard_map/ppermute | solution.py:605
  23.8 7.1 %collective-permute-start.11 = (bf16[8,2,40,128]{3,2,1,0:T(8,128)(2,1)S(1)}, bf16[8,2,40,128]{3,2,1,0:T(8,128)(2,1)S(1)}, u32[]{:S(2)}, u32[]{:S(2)}) collective-permute-start(bf16[8,2,40,128]{3,2,1,0:T(8,128)(2,1)S(1)} %get-tuple-element.73.mine_ref), channel_id=1, source_target_pairs={{0,2},{2,0},{1,3},{3,1},{4,6},{6,4},{5,7},{7,5},{8,10},{10,8},{9,1... | collective-permute-start | bytes 491528 | tf_op jit(solution)/shard_map/ppermute | solution.py:625
  24.4 9.9 %collective-permute-start.5 = (bf16[8,2,40,128]{3,2,1,0:T(8,128)(2,1)S(1)}, bf16[8,2,40,128]{3,2,1,0:T(8,128)(2,1)S(1)}, u32[]{:S(2)}, u32[]{:S(2)}) collective-permute-start(bf16[8,2,40,128]{3,2,1,0:T(8,128)(2,1)S(1)} %get-tuple-element.74.received_ref.mine_ref), channel_id=1, source_target_pairs={{0,2},{2,0},{1,3},{3,1},{4,6},{6,4},{5,7},{7,5},{8,10},{10,8},{9,1... | collective-permute-start | bytes 491528 | tf_op jit(solution)/shard_map/ppermute | solution.py:625
  25.9 5.0 %copy-start.2 = (bf16[3,1152,288]{1,2,0:T(8,128)(2,1)S(1)}, bf16[3,1152,288]{1,2,0:T(8,128)(2,1)}, u32[]{:S(2)}) copy-start(bf16[3,1152,288]{1,2,0:T(8,128)(2,1)} %param.18) | copy-start | bytes 5971972
  30.9 8.2 %copy-start.1 = (bf16[1152,1152]{1,0:T(8,128)(2,1)S(1)}, bf16[1152,1152]{1,0:T(8,128)(2,1)}, u32[]{:S(2)}) copy-start(bf16[1152,1152]{1,0:T(8,128)(2,1)} %fc1_me.7) | copy-start | bytes 7962628
  33.7 5.4 %copy-start = (bf16[1152,1152]{1,0:T(8,128)(2,1)S(1)}, bf16[1152,1152]{1,0:T(8,128)(2,1)}, u32[]{:S(2)}) copy-start(bf16[1152,1152]{1,0:T(8,128)(2,1)} %fc2_me.7) | copy-start | bytes 7962628
  33.7 5.4 %collective-permute-start.12 = (bf16[576,128]{1,0:T(8,128)(2,1)S(1)}, bf16[576,128]{1,0:T(8,128)(2,1)S(1)}, u32[]{:S(2)}, u32[]{:S(2)}) collective-permute-start(bf16[576,128]{1,0:T(8,128)(2,1)S(1)} %get-tuple-element.64.mine_ref), channel_id=1, source_target_pairs={{0,2},{2,0},{1,3},{3,1},{4,6},{6,4},{5,7},{7,5},{8,10},{10,8},{9,1... | collective-permute-start | bytes 442376 | tf_op jit(solution)/shard_map/ppermute | solution.py:652
  37.1 5.3 %collective-permute-start.6 = (bf16[576,128]{1,0:T(8,128)(2,1)S(1)}, bf16[576,128]{1,0:T(8,128)(2,1)S(1)}, u32[]{:S(2)}, u32[]{:S(2)}) collective-permute-start(bf16[576,128]{1,0:T(8,128)(2,1)S(1)} %get-tuple-element.51.mine_ref), channel_id=1, source_target_pairs={{0,2},{2,0},{1,3},{3,1},{4,6},{6,4},{5,7},{7,5},{8,10},{10,8},{9,1... | collective-permute-start | bytes 442376 | tf_op jit(solution)/shard_map/ppermute | solution.py:652
  42.0 10.0 %collective-permute-start.13 = (bf16[128,1152]{1,0:T(8,128)(2,1)S(1)}, bf16[128,1152]{1,0:T(8,128)(2,1)S(1)}, u32[]{:S(2)}, u32[]{:S(2)}) collective-permute-start(bf16[128,1152]{1,0:T(8,128)(2,1)S(1)} %get-tuple-element.66.mine_ref), channel_id=1, source_target_pairs={{0,2},{2,0},{1,3},{3,1},{4,6},{6,4},{5,7},{7,5},{8,10},{10,8},{9,1... | collective-permute-start | bytes 884744 | tf_op jit(solution)/shard_map/ppermute | solution.py:657
  45.3 11.8 %collective-permute-start.8 = (bf16[128,1152]{1,0:T(8,128)(2,1)S(1)}, bf16[128,1152]{1,0:T(8,128)(2,1)S(1)}, u32[]{:S(2)}, u32[]{:S(2)}) collective-permute-start(bf16[128,1152]{1,0:T(8,128)(2,1)S(1)} %get-tuple-element.56.mine_ref), channel_id=1, source_target_pairs={{0,2},{2,0},{1,3},{3,1},{4,6},{6,4},{5,7},{7,5},{8,10},{10,8},{9,1... | collective-permute-start | bytes 884744 | tf_op jit(solution)/shard_map/ppermute | solution.py:657
  55.1 6.4 %collective-permute-start.14 = (bf16[576,128]{1,0:T(8,128)(2,1)S(1)}, bf16[576,128]{1,0:T(8,128)(2,1)S(1)}, u32[]{:S(2)}, u32[]{:S(2)}) collective-permute-start(bf16[576,128]{1,0:T(8,128)(2,1)S(1)} %get-tuple-element.69.mine_ref), channel_id=1, source_target_pairs={{0,2},{2,0},{1,3},{3,1},{4,6},{6,4},{5,7},{7,5},{8,10},{10,8},{9,1... | collective-permute-start | bytes 442376 | tf_op jit(solution)/shard_map/ppermute | solution.py:665
  60.0 5.7 %collective-permute-start.9 = (bf16[576,128]{1,0:T(8,128)(2,1)S(1)}, bf16[576,128]{1,0:T(8,128)(2,1)S(1)}, u32[]{:S(2)}, u32[]{:S(2)}) collective-permute-start(bf16[576,128]{1,0:T(8,128)(2,1)S(1)} %get-tuple-element.59.mine_ref), channel_id=1, source_target_pairs={{0,2},{2,0},{1,3},{3,1},{4,6},{6,4},{5,7},{7,5},{8,10},{10,8},{9,1... | collective-permute-start | bytes 442376 | tf_op jit(solution)/shard_map/ppermute | solution.py:665
  64.4 5.6 %collective-permute-start.15 = (bf16[576,128]{1,0:T(8,128)(2,1)S(1)}, bf16[576,128]{1,0:T(8,128)(2,1)S(1)}, u32[]{:S(2)}, u32[]{:S(2)}) collective-permute-start(bf16[576,128]{1,0:T(8,128)(2,1)S(1)} %get-tuple-element.72), channel_id=1, source_target_pairs={{0,2},{2,0},{1,3},{3,1},{4,6},{6,4},{5,7},{7,5},{8,10},{10,8},{9,1... | collective-permute-start | bytes 442376 | tf_op jit(solution)/shard_map/ppermute | solution.py:671
  68.6 5.2 %collective-permute-start.10 = (bf16[576,128]{1,0:T(8,128)(2,1)S(1)}, bf16[576,128]{1,0:T(8,128)(2,1)S(1)}, u32[]{:S(2)}, u32[]{:S(2)}) collective-permute-start(bf16[576,128]{1,0:T(8,128)(2,1)S(1)} %get-tuple-element.62), channel_id=1, source_target_pairs={{0,2},{2,0},{1,3},{3,1},{4,6},{6,4},{5,7},{7,5},{8,10},{10,8},{9,1... | collective-permute-start | bytes 442376 | tf_op jit(solution)/shard_map/ppermute | solution.py:671

commit v7 on v6

--- a/solution.py
+++ b/solution.py
@@ -369,7 +369,6 @@
         in_specs=[VMEM_SPEC] * len(arrays),
         out_specs=(VMEM_SPEC,) * len(outs),
         compiler_params=params(*arrays, *outs),
-        cost_estimate=takes(2.8),
         name="attention",
     )(*arrays)
 
@@ -470,7 +469,6 @@
         scratch_shapes=[pltpu.VMEM((rows, 2 * weights[1].shape[1]), BF16)]
         + ([pltpu.VMEM((rows, features), BF16)] if halves else []),
         compiler_params=params(cur, mine, other, mod, *weights, *outs),
-        cost_estimate=takes(2.8),
         name="feed",
     )(flag, cur, mine, other, mod, *weights)
 

time: 89.5 us -> 89.5 us (level)
  no operation moved by 1% of the time
where the time goes in v7:
time: 89.5 us; the launch traced here: 89.2 us
  Pallas kernels  31.3 us (35%)
  waiting for transfers between devices  24.1 us (27%)
  starting transfers between devices  18.8 us (21%)
  blocking collectives  13.8 us (15%)
  local copies, waits for them, and re-layouts  1.08 us (1%)
    all_to_all x1, blocking collectives, on_device(): result = lax.all_to_all(result, ('frame', 'core'), 0, 0, tiled=True)  13.8 us
    pallas_call x4, Pallas kernels, attention_call(): pl.pallas_call(kernel, out_shape=outs, in_specs=[VMEM_SPEC] * len(arrays)...  11.6 us
    pallas_call x4, Pallas kernels, feed_call(): pl.pallas_call(functools.partial(feed_kernel, halves), out_shape=outs, in...  11.6 us
    ppermute x1, waiting for transfers between devices, on_device(): out_far = swap_y(w_out)  6.77 us
    ppermute x2, waiting for transfers between devices, on_device(): fed.append((current, after, feed, swap_y(feed), later))  6.61 us
    all_to_all x1, starting transfers between devices, on_device(): received = lax.all_to_all(payload, ('frame', 'core'), 0, 0, tiled=True)  5.92 us
    pallas_call x1, Pallas kernels, prepare(): pl.pallas_call(functools.partial(prepare_kernel, here, lane_at, tuple(pla...  4.64 us
    all_to_all x1, waiting for transfers between devices, on_device(): received = lax.all_to_all(payload, ('frame', 'core'), 0, 0, tiled=True)  4.32 us
  transfers between devices with their start and end apart: 17, of which 10 were waited for; matrix products, arithmetic and copies ran while one was open for 0% of the time, Pallas kernels for 33%

profile of v7, /device:TPU:0, one launch (start us, length us, event | category | flops | bytes accessed | tf_op | source)
XLA Modules:
  0.0 89.2 jit_solution(863791060510519274)
XLA Ops:
  1.0 2.6 %collective-permute-start.2 = (bf16[288,1152]{1,0:T(8,128)(2,1)}, bf16[288,1152]{1,0:T(8,128)(2,1)}, u32[]{:S(2)}, u32[]{:S(2)}) collective-permute-start(bf16[288,1152]{1,0:T(8,128)(2,1)} %refs_3_.1), channel_id=1, source_target_pairs={{0,2},{2,0},{1,3},{3,1},{4,6},{6,4},{5,7},{7,5},{8,10},{10,8},{9,1... | collective-permute-start | bytes 1990664 | tf_op jit(solution)/shard_map/ppermute | solution.py:602
  3.7 1.0 %copy-done.3 = bf16[8,64,288]{2,1,0:T(8,128)(2,1)S(1)} copy-done((bf16[8,64,288]{2,1,0:T(8,128)(2,1)S(1)}, bf16[8,64,288]{2,1,0:T(8,128)(2,1)}, u32[]{:S(2)}) %copy-start.3) | copy-done | bytes 294936
  4.7 1.9 %payload.1 = bf16[16,2,40,128]{3,2,1,0:T(8,128)(2,1)} custom-call(bf16[8,64,288]{2,1,0:T(8,128)(2,1)S(1)} %copy-done.3, s32[1]{0:T(128)} %bitcast.1.frame_far, s32[8]{0:T(128)} %level_far.1, s32[8,17]{1,0:T(8,128)} %window_far.1, bf16[2,64,288]{2,1,0:T(8,128)(2,1)} %fresh_far.1), custom_call_target="tpu_custom_call" | custom-call | bytes 6600000 | tf_op jit(solution)/shard_map/payload/pallas_call | solution.py:118
  6.7 5.9 %all-to-all-start = ((bf16[16,2,40,128]{3,2,1,0:T(8,128)(2,1)}), bf16[16,2,40,128]{3,2,1,0:T(8,128)(2,1)S(1)}, u32[]{:S(2)}, u32[]{:S(2)}) async-start(bf16[16,2,40,128]{3,2,1,0:T(8,128)(2,1)} %payload.1), calls=%async_computation | async-start | bytes 655360 | tf_op jit(solution)/shard_map/all_to_all | solution.py:609
  12.6 6.8 %collective-permute-done.2.refs_5_.refs_7_ = bf16[288,1152]{1,0:T(8,128)(2,1)} collective-permute-done((bf16[288,1152]{1,0:T(8,128)(2,1)}, bf16[288,1152]{1,0:T(8,128)(2,1)}, u32[]{:S(2)}, u32[]{:S(2)}) %collective-permute-start.2) | collective-permute-done | bytes 663584 | tf_op jit(solution)/shard_map/ppermute | solution.py:602
  19.4 4.3 %all-to-all-done = bf16[16,2,40,128]{3,2,1,0:T(8,128)(2,1)S(1)} async-done(((bf16[16,2,40,128]{3,2,1,0:T(8,128)(2,1)}), bf16[16,2,40,128]{3,2,1,0:T(8,128)(2,1)S(1)}, u32[]{:S(2)}, u32[]{:S(2)}) %all-to-all-start) | async-done | bytes 327712 | tf_op jit(solution)/shard_map/all_to_all | solution.py:609
  23.8 0.6 collective-permute-start.11
  24.4 1.5 %collective-permute-start.5 = (bf16[8,2,40,128]{3,2,1,0:T(8,128)(2,1)S(1)}, bf16[8,2,40,128]{3,2,1,0:T(8,128)(2,1)S(1)}, u32[]{:S(2)}, u32[]{:S(2)}) collective-permute-start(bf16[8,2,40,128]{3,2,1,0:T(8,128)(2,1)S(1)} %get-tuple-element.74.received_ref.mine_ref), channel_id=1, source_target_pairs={{0,2},{2,0},{1,3},{3,1},{4,6},{6,4},{5,7},{7,5},{8,10},{10,8},{9,1... | collective-permute-start | bytes 491528 | tf_op jit(solution)/shard_map/ppermute | solution.py:623
  25.9 4.6 %prepare.1 = (f32[2,64,1152]{2,1,0:T(8,128)S(1)}, f32[3,64,1152]{2,1,0:T(8,128)S(1)}, f32[1,64,1152]{2,1,0:T(8,128)S(1)}, f32[64,128]{1,0:T(8,128)S(1)}, f32[128...) custom-call(s32[1]{0:T(128)} %bitcast.place_ref, ...), custom_call_target="tpu_custom_call" | custom-call | bytes 16500000 | tf_op jit(solution)/shard_map/prepare/pallas_call | solution.py:220
  30.9 2.8 %attention.6 = (bf16[128,1152]{1,0:T(8,128)(2,1)S(1)}, bf16[576,128]{1,0:T(8,128)(2,1)S(1)}, f32[2,1152]{1,0:T(2,128)S(1)}) custom-call(bf16[8,2,40,128]{3,2,1,0:T(8,128)(2,1)S(1)} %get-tuple-element.73.mine_ref, bf16[8,2,40,128]{3,2,1,0:T(8,128)(2,1)S(1)} %collective-permute-done.11.other_ref, f32[8,128]{1,0:T(8,128)S(1)} %get-tuple-element.44.flag_ref, ...), custom_call_target="tpu_custom_call" | custom-call | tf_op jit(solution)/shard_map/attention/pallas_call | solution.py:366
  33.7 0.6 collective-permute-start.12
  34.3 2.8 %attention.4 = (bf16[128,1152]{1,0:T(8,128)(2,1)S(1)}, bf16[576,128]{1,0:T(8,128)(2,1)S(1)}, f32[2,1152]{1,0:T(2,128)S(1)}) custom-call(bf16[8,2,40,128]{3,2,1,0:T(8,128)(2,1)S(1)} %get-tuple-element.74.received_ref.mine_ref, bf16[8,2,40,128]{3,2,1,0:T(8,128)(2,1)S(1)} %collective-permute-done.5.other_ref, f32[8,128]{1,0:T(8,128)S(1)} %get-tuple-element.44.flag_ref, ...), custom_call_target="tpu_custom_call" | custom-call | tf_op jit(solution)/shard_map/attention/pallas_call | solution.py:366
  37.1 1.6 %collective-permute-start.6 = (bf16[576,128]{1,0:T(8,128)(2,1)S(1)}, bf16[576,128]{1,0:T(8,128)(2,1)S(1)}, u32[]{:S(2)}, u32[]{:S(2)}) collective-permute-start(bf16[576,128]{1,0:T(8,128)(2,1)S(1)} %get-tuple-element.51.mine_ref), channel_id=1, source_target_pairs={{0,2},{2,0},{1,3},{3,1},{4,6},{6,4},{5,7},{7,5},{8,10},{10,8},{9,1... | collective-permute-start | bytes 442376 | tf_op jit(solution)/shard_map/ppermute | solution.py:650
  39.1 2.9 %feed.6 = (bf16[128,1152]{1,0:T(8,128)(2,1)S(1)}, bf16[128,1152]{1,0:T(8,128)(2,1)S(1)}) custom-call(f32[8,128]{1,0:T(8,128)S(1)} %get-tuple-element.44.flag_ref, bf16[128,1152]{1,0:T(8,128)(2,1)S(1)} %get-tuple-element.63.cur_ref.old_ref, bf16[576,128]{1,0:T(8,128)(2,1)S(1)} %get-tuple-element.64.mine_ref, ...), custom_call_target="tpu_custom_call" | custom-call | tf_op jit(solution)/shard_map/feed/pallas_call | solution.py:464
  42.4 2.9 %feed.4 = (bf16[128,1152]{1,0:T(8,128)(2,1)S(1)}, bf16[128,1152]{1,0:T(8,128)(2,1)S(1)}) custom-call(f32[8,128]{1,0:T(8,128)S(1)} %get-tuple-element.44.flag_ref, bf16[128,1152]{1,0:T(8,128)(2,1)S(1)} %get-tuple-element.50.cur_ref.old_ref, bf16[576,128]{1,0:T(8,128)(2,1)S(1)} %get-tuple-element.51.mine_ref, ...), custom_call_target="tpu_custom_call" | custom-call | tf_op jit(solution)/shard_map/feed/pallas_call | solution.py:464
  45.3 1.8 %collective-permute-start.8 = (bf16[128,1152]{1,0:T(8,128)(2,1)S(1)}, bf16[128,1152]{1,0:T(8,128)(2,1)S(1)}, u32[]{:S(2)}, u32[]{:S(2)}) collective-permute-start(bf16[128,1152]{1,0:T(8,128)(2,1)S(1)} %get-tuple-element.56.mine_ref), channel_id=1, source_target_pairs={{0,2},{2,0},{1,3},{3,1},{4,6},{6,4},{5,7},{7,5},{8,10},{10,8},{9,1... | collective-permute-start | bytes 884744 | tf_op jit(solution)/shard_map/ppermute | solution.py:655
  47.1 5.0 %collective-permute-done.13.other_ref = bf16[128,1152]{1,0:T(8,128)(2,1)S(1)} collective-permute-done((bf16[128,1152]{1,0:T(8,128)(2,1)S(1)}, bf16[128,1152]{1,0:T(8,128)(2,1)S(1)}, u32[]{:S(2)}, u32[]{:S(2)}) %collective-permute-start.13) | collective-permute-done | bytes 294944 | tf_op jit(solution)/shard_map/ppermute | solution.py:655
  52.0 3.1 %attention.7 = (bf16[128,1152]{1,0:T(8,128)(2,1)S(1)}, bf16[576,128]{1,0:T(8,128)(2,1)S(1)}) custom-call(bf16[128,1152]{1,0:T(8,128)(2,1)S(1)} %get-tuple-element.63.cur_ref.old_ref, bf16[128,1152]{1,0:T(8,128)(2,1)S(1)} %get-tuple-element.65.after_ref, bf16[128,1152]{1,0:T(8,128)(2,1)S(1)} %get-tuple-element.66.mine_ref, ...), custom_call_target="tpu_custom_call" | custom-call | tf_op jit(solution)/shard_map/attention/pallas_call | solution.py:366
  55.5 1.7 %collective-permute-done.8.other_ref = bf16[128,1152]{1,0:T(8,128)(2,1)S(1)} collective-permute-done((bf16[128,1152]{1,0:T(8,128)(2,1)S(1)}, bf16[128,1152]{1,0:T(8,128)(2,1)S(1)}, u32[]{:S(2)}, u32[]{:S(2)}) %collective-permute-start.8) | collective-permute-done | bytes 294944 | tf_op jit(solution)/shard_map/ppermute | solution.py:655
  57.1 2.9 %attention.5 = (bf16[128,1152]{1,0:T(8,128)(2,1)S(1)}, bf16[576,128]{1,0:T(8,128)(2,1)S(1)}) custom-call(bf16[128,1152]{1,0:T(8,128)(2,1)S(1)} %get-tuple-element.50.cur_ref.old_ref, bf16[128,1152]{1,0:T(8,128)(2,1)S(1)} %get-tuple-element.55.after_ref, bf16[128,1152]{1,0:T(8,128)(2,1)S(1)} %get-tuple-element.56.mine_ref, ...), custom_call_target="tpu_custom_call" | custom-call | tf_op jit(solution)/shard_map/attention/pallas_call | solution.py:366
  60.0 0.9 %collective-permute-start.9 = (bf16[576,128]{1,0:T(8,128)(2,1)S(1)}, bf16[576,128]{1,0:T(8,128)(2,1)S(1)}, u32[]{:S(2)}, u32[]{:S(2)}) collective-permute-start(bf16[576,128]{1,0:T(8,128)(2,1)S(1)} %get-tuple-element.59.mine_ref), channel_id=1, source_target_pairs={{0,2},{2,0},{1,3},{3,1},{4,6},{6,4},{5,7},{7,5},{8,10},{10,8},{9,1... | collective-permute-start | bytes 442376 | tf_op jit(solution)/shard_map/ppermute | solution.py:663
  60.9 0.6 collective-permute-done.14.other_ref
  61.5 2.9 %feed.7 = (bf16[128,1152]{1,0:T(8,128)(2,1)S(1)}, bf16[576,128]{1,0:T(8,128)(2,1)S(1)}, bf16[576,128]{1,0:T(8,128)(2,1)S(1)}) custom-call(f32[8,128]{1,0:T(8,128)S(1)} %get-tuple-element.44.flag_ref, bf16[128,1152]{1,0:T(8,128)(2,1)S(1)} %get-tuple-element.68.cur_ref.refs_4_, bf16[576,128]{1,0:T(8,128)(2,1)S(1)} %get-tuple-element.69.mine_ref, ...), custom_call_target="tpu_custom_call" | custom-call | tf_op jit(solution)/shard_map/feed/pallas_call | solution.py:464
  64.4 0.6 collective-permute-start.15
  65.0 0.6 collective-permute-done.9.other_ref
  65.7 2.9 %feed.5 = (bf16[128,1152]{1,0:T(8,128)(2,1)S(1)}, bf16[576,128]{1,0:T(8,128)(2,1)S(1)}, bf16[576,128]{1,0:T(8,128)(2,1)S(1)}) custom-call(f32[8,128]{1,0:T(8,128)S(1)} %get-tuple-element.44.flag_ref, bf16[128,1152]{1,0:T(8,128)(2,1)S(1)} %get-tuple-element.58.cur_ref.refs_0_, bf16[576,128]{1,0:T(8,128)(2,1)S(1)} %get-tuple-element.59.mine_ref, ...), custom_call_target="tpu_custom_call" | custom-call | tf_op jit(solution)/shard_map/feed/pallas_call | solution.py:464
  68.6 0.9 %collective-permute-start.10 = (bf16[576,128]{1,0:T(8,128)(2,1)S(1)}, bf16[576,128]{1,0:T(8,128)(2,1)S(1)}, u32[]{:S(2)}, u32[]{:S(2)}) collective-permute-start(bf16[576,128]{1,0:T(8,128)(2,1)S(1)} %get-tuple-element.62), channel_id=1, source_target_pairs={{0,2},{2,0},{1,3},{3,1},{4,6},{6,4},{5,7},{7,5},{8,10},{10,8},{9,1... | collective-permute-start | bytes 442376 | tf_op jit(solution)/shard_map/ppermute | solution.py:669
  69.5 0.6 collective-permute-done.15.refs_7_
  70.0 3.7 %collective-permute-done.10.refs_3_ = bf16[576,128]{1,0:T(8,128)(2,1)S(1)} collective-permute-done((bf16[576,128]{1,0:T(8,128)(2,1)S(1)}, bf16[576,128]{1,0:T(8,128)(2,1)S(1)}, u32[]{:S(2)}, u32[]{:S(2)}) %collective-permute-start.10) | collective-permute-done | bytes 147488 | tf_op jit(solution)/shard_map/ppermute | solution.py:669
  73.8 0.7 finish.1
  74.4 13.8 %all_to_all.10.rows_ref = bf16[16,72,128]{2,1,0:T(8,128)(2,1)S(1)} all-to-all(bf16[16,72,128]{2,1,0:T(8,128)(2,1)S(1)} %bitcast.17), channel_id=1, replica_groups=mesh['frame'=8,'y'=2,'core'=2] {'frame','core'}, dimensions={0} | all-to-all | bytes 589824 | tf_op jit(solution)/shard_map/all_to_all | solution.py:673
  88.2 0.9 %unpack.1 = bf16[8,64,288]{2,1,0:T(8,128)(2,1)} custom-call(bf16[16,72,128]{2,1,0:T(8,128)(2,1)S(1)} %all_to_all.10.rows_ref), custom_call_target="tpu_custom_call" | custom-call | bytes 2970000 | tf_op jit(solution)/shard_map/unpack/pallas_call | solution.py:564
  (29 shorter events, 2.8 us)
Async XLA Ops:
  0.0 25.9 %copy-start.4 = (f32[64]{0:T(128)S(1)}, f32[64]{0:T(128)}, u32[]{:S(2)}) copy-start(f32[64]{0:T(128)} %param.16) | copy-start | bytes 772
  0.0 25.9 %copy-start.5 = (f32[64]{0:T(128)S(1)}, f32[64]{0:T(128)}, u32[]{:S(2)}) copy-start(f32[64]{0:T(128)} %param.17) | copy-start | bytes 772
  0.0 23.8 %collective-permute-start.3 = (bf16[1152,1152]{1,0:T(8,128)(2,1)}, bf16[1152,1152]{1,0:T(8,128)(2,1)}, u32[]{:S(2)}, u32[]{:S(2)}) collective-permute-start(bf16[1152,1152]{1,0:T(8,128)(2,1)} %fc2_me.7), channel_id=1, source_target_pairs={{0,1},{1,0},{2,3},{3,2},{4,5},{5,4},{6,7},{7,6},{8,9},{9,8},{10,11... | collective-permute-start | bytes 7962632 | tf_op jit(solution)/shard_map/ppermute | solution.py:603
  0.5 38.2 %collective-permute-start.7 = (bf16[1152,1152]{1,0:T(8,128)(2,1)}, bf16[1152,1152]{1,0:T(8,128)(2,1)S(1)}, u32[]{:S(2)}, u32[]{:S(2)}) collective-permute-start(bf16[1152,1152]{1,0:T(8,128)(2,1)} %fc1_me.7), channel_id=1, source_target_pairs={{0,1},{1,0},{2,3},{3,2},{4,5},{5,4},{6,7},{7,6},{8,9},{9,8},{10,11... | collective-permute-start | bytes 7962632 | tf_op jit(solution)/shard_map/ppermute | solution.py:651
  0.5 23.2 %collective-permute-start = (bf16[3,288,1152]{2,1,0:T(8,128)(2,1)}, bf16[3,288,1152]{2,1,0:T(8,128)(2,1)}, u32[]{:S(2)}, u32[]{:S(2)}) collective-permute-start(bf16[3,288,1152]{2,1,0:T(8,128)(2,1)} %bitcast.12), channel_id=1, source_target_pairs={{0,1},{1,0},{2,3},{3,2},{4,5},{5,4},{6,7},{7,6},{8,9},{9,8},{10,11... | collective-permute-start | bytes 5971976 | tf_op jit(solution)/shard_map/ppermute | solution.py:601
  1.0 18.4 %collective-permute-start.2 = (bf16[288,1152]{1,0:T(8,128)(2,1)}, bf16[288,1152]{1,0:T(8,128)(2,1)}, u32[]{:S(2)}, u32[]{:S(2)}) collective-permute-start(bf16[288,1152]{1,0:T(8,128)(2,1)} %refs_3_.1), channel_id=1, source_target_pairs={{0,2},{2,0},{1,3},{3,1},{4,6},{6,4},{5,7},{7,5},{8,10},{10,8},{9,1... | collective-permute-start | bytes 1990664 | tf_op jit(solution)/shard_map/ppermute | solution.py:602
  3.6 20.2 %collective-permute-start.1 = (bf16[288,1152]{1,0:T(8,128)(2,1)}, bf16[288,1152]{1,0:T(8,128)(2,1)}, u32[]{:S(2)}, u32[]{:S(2)}) collective-permute-start(bf16[288,1152]{1,0:T(8,128)(2,1)} %refs_3_.1), channel_id=1, source_target_pairs={{0,1},{1,0},{2,3},{3,2},{4,5},{5,4},{6,7},{7,6},{8,9},{9,8},{10,11... | collective-permute-start | bytes 1990664 | tf_op jit(solution)/shard_map/ppermute | solution.py:603
  3.7 1.0 %copy-start.3 = (bf16[8,64,288]{2,1,0:T(8,128)(2,1)S(1)}, bf16[8,64,288]{2,1,0:T(8,128)(2,1)}, u32[]{:S(2)}) copy-start(bf16[8,64,288]{2,1,0:T(8,128)(2,1)} %x_ref.1) | copy-start | bytes 884740
  6.7 17.0 %all-to-all-start = ((bf16[16,2,40,128]{3,2,1,0:T(8,128)(2,1)}), bf16[16,2,40,128]{3,2,1,0:T(8,128)(2,1)S(1)}, u32[]{:S(2)}, u32[]{:S(2)}) async-start(bf16[16,2,40,128]{3,2,1,0:T(8,128)(2,1)} %payload.1), calls=%async_computation | async-start | bytes 655360 | tf_op jit(solution)/shard_map/all_to_all | solution.py:609
  19.4 6.5 %collective-permute-start.4 = (bf16[288,1152]{1,0:T(8,128)(2,1)}, bf16[288,1152]{1,0:T(8,128)(2,1)}, u32[]{:S(2)}, u32[]{:S(2)}) collective-permute-start(bf16[288,1152]{1,0:T(8,128)(2,1)} %collective-permute-done.2.refs_5_.refs_7_), channel_id=1, source_target_pairs={{0,1},{1,0},{2,3},{3,2},{4,5},{5,4},{6,7},{7,6},{8,9},{9,8},{10,11... | collective-permute-start | bytes 1990664 | tf_op jit(solution)/shard_map/ppermute | solution.py:603
  23.8 7.1 %collective-permute-start.11 = (bf16[8,2,40,128]{3,2,1,0:T(8,128)(2,1)S(1)}, bf16[8,2,40,128]{3,2,1,0:T(8,128)(2,1)S(1)}, u32[]{:S(2)}, u32[]{:S(2)}) collective-permute-start(bf16[8,2,40,128]{3,2,1,0:T(8,128)(2,1)S(1)} %get-tuple-element.73.mine_ref), channel_id=1, source_target_pairs={{0,2},{2,0},{1,3},{3,1},{4,6},{6,4},{5,7},{7,5},{8,10},{10,8},{9,1... | collective-permute-start | bytes 491528 | tf_op jit(solution)/shard_map/ppermute | solution.py:623
  24.4 9.9 %collective-permute-start.5 = (bf16[8,2,40,128]{3,2,1,0:T(8,128)(2,1)S(1)}, bf16[8,2,40,128]{3,2,1,0:T(8,128)(2,1)S(1)}, u32[]{:S(2)}, u32[]{:S(2)}) collective-permute-start(bf16[8,2,40,128]{3,2,1,0:T(8,128)(2,1)S(1)} %get-tuple-element.74.received_ref.mine_ref), channel_id=1, source_target_pairs={{0,2},{2,0},{1,3},{3,1},{4,6},{6,4},{5,7},{7,5},{8,10},{10,8},{9,1... | collective-permute-start | bytes 491528 | tf_op jit(solution)/shard_map/ppermute | solution.py:623
  25.9 5.0 %copy-start.2 = (bf16[3,1152,288]{1,2,0:T(8,128)(2,1)S(1)}, bf16[3,1152,288]{1,2,0:T(8,128)(2,1)}, u32[]{:S(2)}) copy-start(bf16[3,1152,288]{1,2,0:T(8,128)(2,1)} %param.18) | copy-start | bytes 5971972
  30.9 8.2 %copy-start.1 = (bf16[1152,1152]{1,0:T(8,128)(2,1)S(1)}, bf16[1152,1152]{1,0:T(8,128)(2,1)}, u32[]{:S(2)}) copy-start(bf16[1152,1152]{1,0:T(8,128)(2,1)} %fc1_me.7) | copy-start | bytes 7962628
  33.7 5.4 %copy-start = (bf16[1152,1152]{1,0:T(8,128)(2,1)S(1)}, bf16[1152,1152]{1,0:T(8,128)(2,1)}, u32[]{:S(2)}) copy-start(bf16[1152,1152]{1,0:T(8,128)(2,1)} %fc2_me.7) | copy-start | bytes 7962628
  33.7 5.4 %collective-permute-start.12 = (bf16[576,128]{1,0:T(8,128)(2,1)S(1)}, bf16[576,128]{1,0:T(8,128)(2,1)S(1)}, u32[]{:S(2)}, u32[]{:S(2)}) collective-permute-start(bf16[576,128]{1,0:T(8,128)(2,1)S(1)} %get-tuple-element.64.mine_ref), channel_id=1, source_target_pairs={{0,2},{2,0},{1,3},{3,1},{4,6},{6,4},{5,7},{7,5},{8,10},{10,8},{9,1... | collective-permute-start | bytes 442376 | tf_op jit(solution)/shard_map/ppermute | solution.py:650
  37.1 5.3 %collective-permute-start.6 = (bf16[576,128]{1,0:T(8,128)(2,1)S(1)}, bf16[576,128]{1,0:T(8,128)(2,1)S(1)}, u32[]{:S(2)}, u32[]{:S(2)}) collective-permute-start(bf16[576,128]{1,0:T(8,128)(2,1)S(1)} %get-tuple-element.51.mine_ref), channel_id=1, source_target_pairs={{0,2},{2,0},{1,3},{3,1},{4,6},{6,4},{5,7},{7,5},{8,10},{10,8},{9,1... | collective-permute-start | bytes 442376 | tf_op jit(solution)/shard_map/ppermute | solution.py:650
  42.0 10.0 %collective-permute-start.13 = (bf16[128,1152]{1,0:T(8,128)(2,1)S(1)}, bf16[128,1152]{1,0:T(8,128)(2,1)S(1)}, u32[]{:S(2)}, u32[]{:S(2)}) collective-permute-start(bf16[128,1152]{1,0:T(8,128)(2,1)S(1)} %get-tuple-element.66.mine_ref), channel_id=1, source_target_pairs={{0,2},{2,0},{1,3},{3,1},{4,6},{6,4},{5,7},{7,5},{8,10},{10,8},{9,1... | collective-permute-start | bytes 884744 | tf_op jit(solution)/shard_map/ppermute | solution.py:655
  45.3 11.8 %collective-permute-start.8 = (bf16[128,1152]{1,0:T(8,128)(2,1)S(1)}, bf16[128,1152]{1,0:T(8,128)(2,1)S(1)}, u32[]{:S(2)}, u32[]{:S(2)}) collective-permute-start(bf16[128,1152]{1,0:T(8,128)(2,1)S(1)} %get-tuple-element.56.mine_ref), channel_id=1, source_target_pairs={{0,2},{2,0},{1,3},{3,1},{4,6},{6,4},{5,7},{7,5},{8,10},{10,8},{9,1... | collective-permute-start | bytes 884744 | tf_op jit(solution)/shard_map/ppermute | solution.py:655
  55.1 6.4 %collective-permute-start.14 = (bf16[576,128]{1,0:T(8,128)(2,1)S(1)}, bf16[576,128]{1,0:T(8,128)(2,1)S(1)}, u32[]{:S(2)}, u32[]{:S(2)}) collective-permute-start(bf16[576,128]{1,0:T(8,128)(2,1)S(1)} %get-tuple-element.69.mine_ref), channel_id=1, source_target_pairs={{0,2},{2,0},{1,3},{3,1},{4,6},{6,4},{5,7},{7,5},{8,10},{10,8},{9,1... | collective-permute-start | bytes 442376 | tf_op jit(solution)/shard_map/ppermute | solution.py:663
  60.0 5.7 %collective-permute-start.9 = (bf16[576,128]{1,0:T(8,128)(2,1)S(1)}, bf16[576,128]{1,0:T(8,128)(2,1)S(1)}, u32[]{:S(2)}, u32[]{:S(2)}) collective-permute-start(bf16[576,128]{1,0:T(8,128)(2,1)S(1)} %get-tuple-element.59.mine_ref), channel_id=1, source_target_pairs={{0,2},{2,0},{1,3},{3,1},{4,6},{6,4},{5,7},{7,5},{8,10},{10,8},{9,1... | collective-permute-start | bytes 442376 | tf_op jit(solution)/shard_map/ppermute | solution.py:663
  64.4 5.6 %collective-permute-start.15 = (bf16[576,128]{1,0:T(8,128)(2,1)S(1)}, bf16[576,128]{1,0:T(8,128)(2,1)S(1)}, u32[]{:S(2)}, u32[]{:S(2)}) collective-permute-start(bf16[576,128]{1,0:T(8,128)(2,1)S(1)} %get-tuple-element.72), channel_id=1, source_target_pairs={{0,2},{2,0},{1,3},{3,1},{4,6},{6,4},{5,7},{7,5},{8,10},{10,8},{9,1... | collective-permute-start | bytes 442376 | tf_op jit(solution)/shard_map/ppermute | solution.py:669
  68.6 5.2 %collective-permute-start.10 = (bf16[576,128]{1,0:T(8,128)(2,1)S(1)}, bf16[576,128]{1,0:T(8,128)(2,1)S(1)}, u32[]{:S(2)}, u32[]{:S(2)}) collective-permute-start(bf16[576,128]{1,0:T(8,128)(2,1)S(1)} %get-tuple-element.62), channel_id=1, source_target_pairs={{0,2},{2,0},{1,3},{3,1},{4,6},{6,4},{5,7},{7,5},{8,10},{10,8},{9,1... | collective-permute-start | bytes 442376 | tf_op jit(solution)/shard_map/ppermute | solution.py:669

commit v8 on v7

--- a/solution.py
+++ b/solution.py
@@ -418,14 +418,13 @@
     frames = mod_ref.shape[1]
     tokens = cur_ref.shape[0] // frames
     normed = []
-    rows, half = cur_ref.shape[0], out_all.shape[0] // 2
-    attention_total = None
-    for n, ref in enumerate((mine_ref, other_ref)):
-        main, tail = unpack_half(ref, rows)
-        middle = n * half + main.shape[1]
-        part = jnp.dot(main, out_all[n * half : middle], preferred_element_type=F32)
-        part += jnp.dot(tail, out_all[middle : (n + 1) * half], preferred_element_type=F32)
-        attention_total = part if n == 0 else attention_total + part
+    rows = cur_ref.shape[0]
+    both = [unpack_half(ref, rows) for ref in (mine_ref, other_ref)]
+    main = jnp.concatenate([tiles for tiles, _ in both], axis=1)
+    tail = jnp.concatenate([rest_of for _, rest_of in both], axis=1)
+    attention_total = jnp.dot(
+        main, out_all[: main.shape[1]], preferred_element_type=F32
+    ) + jnp.dot(tail, out_all[main.shape[1] :], preferred_element_type=F32)
     for p in range(tokens):
         at = slice(p * frames, (p + 1) * frames)
         after = (cur_ref[at, :].astype(F32) + mod_ref[0] * attention_total[at]).astype(BF16)
@@ -626,9 +625,9 @@
     for n in range(2):
         first, second = ((w_out, out_core), (out_far, out_corner))[n]
         weights += [first, second, first, second]
-        to = 2 * n * share
+        to = 2 * n * full * LANES
         places += [(1, to, 0, full * LANES), (1, to + full * LANES, 0, full * LANES)]
-        to += 2 * full * LANES
+        to = 4 * full * LANES + 2 * n * rest
         places += [(1, to, full * LANES, rest), (1, to + rest, full * LANES, rest)]
     weights.append(fc2_other)
     places.append((2, 0, 0, w_fc2.shape[0]))

time: 89.5 us -> 89.4 us (level)
  no operation moved by 1% of the time
where the time goes in v8:
time: 89.4 us; the launch traced here: 89.1 us
  Pallas kernels  31.2 us (35%)
  waiting for transfers between devices  24.1 us (27%)
  starting transfers between devices  18.8 us (21%)
  blocking collectives  13.8 us (15%)
  local copies, waits for them, and re-layouts  1.08 us (1%)
    all_to_all x1, blocking collectives, on_device(): result = lax.all_to_all(result, ('frame', 'core'), 0, 0, tiled=True)  13.8 us
    pallas_call x4, Pallas kernels, attention_call(): pl.pallas_call(kernel, out_shape=outs, in_specs=[VMEM_SPEC] * len(arrays)...  11.6 us
    pallas_call x4, Pallas kernels, feed_call(): pl.pallas_call(functools.partial(feed_kernel, halves), out_shape=outs, in...  11.5 us
    ppermute x1, waiting for transfers between devices, on_device(): out_far = swap_y(w_out)  6.77 us
    ppermute x2, waiting for transfers between devices, on_device(): fed.append((current, after, feed, swap_y(feed), later))  6.58 us
    all_to_all x1, starting transfers between devices, on_device(): received = lax.all_to_all(payload, ('frame', 'core'), 0, 0, tiled=True)  5.92 us
    pallas_call x1, Pallas kernels, prepare(): pl.pallas_call(functools.partial(prepare_kernel, here, lane_at, tuple(pla...  4.64 us
    ppermute x2, waiting for transfers between devices, on_device(): parts.append((current, after, feed_here, swap_y(feed_there)))  4.37 us
  transfers between devices with their start and end apart: 17, of which 10 were waited for; matrix products, arithmetic and copies ran while one was open for 0% of the time, Pallas kernels for 33%

profile of v8, /device:TPU:0, one launch (start us, length us, event | category | flops | bytes accessed | tf_op | source)
XLA Modules:
  0.0 89.1 jit_solution(7738236058140790574)
XLA Ops:
  1.0 2.6 %collective-permute-start.2 = (bf16[288,1152]{1,0:T(8,128)(2,1)}, bf16[288,1152]{1,0:T(8,128)(2,1)}, u32[]{:S(2)}, u32[]{:S(2)}) collective-permute-start(bf16[288,1152]{1,0:T(8,128)(2,1)} %refs_3_.1), channel_id=1, source_target_pairs={{0,2},{2,0},{1,3},{3,1},{4,6},{6,4},{5,7},{7,5},{8,10},{10,8},{9,1... | collective-permute-start | bytes 1990664 | tf_op jit(solution)/shard_map/ppermute | solution.py:601
  3.7 1.0 %copy-done.3 = bf16[8,64,288]{2,1,0:T(8,128)(2,1)S(1)} copy-done((bf16[8,64,288]{2,1,0:T(8,128)(2,1)S(1)}, bf16[8,64,288]{2,1,0:T(8,128)(2,1)}, u32[]{:S(2)}) %copy-start.3) | copy-done | bytes 294936
  4.7 1.9 %payload.1 = bf16[16,2,40,128]{3,2,1,0:T(8,128)(2,1)} custom-call(bf16[8,64,288]{2,1,0:T(8,128)(2,1)S(1)} %copy-done.3, s32[1]{0:T(128)} %bitcast.1.frame_far, s32[8]{0:T(128)} %level_far.1, s32[8,17]{1,0:T(8,128)} %window_far.1, bf16[2,64,288]{2,1,0:T(8,128)(2,1)} %fresh_far.1), custom_call_target="tpu_custom_call" | custom-call | bytes 6600000 | tf_op jit(solution)/shard_map/payload/pallas_call | solution.py:118
  6.7 5.9 %all-to-all-start = ((bf16[16,2,40,128]{3,2,1,0:T(8,128)(2,1)}), bf16[16,2,40,128]{3,2,1,0:T(8,128)(2,1)S(1)}, u32[]{:S(2)}, u32[]{:S(2)}) async-start(bf16[16,2,40,128]{3,2,1,0:T(8,128)(2,1)} %payload.1), calls=%async_computation | async-start | bytes 655360 | tf_op jit(solution)/shard_map/all_to_all | solution.py:608
  12.6 6.8 %collective-permute-done.2.refs_5_.refs_7_ = bf16[288,1152]{1,0:T(8,128)(2,1)} collective-permute-done((bf16[288,1152]{1,0:T(8,128)(2,1)}, bf16[288,1152]{1,0:T(8,128)(2,1)}, u32[]{:S(2)}, u32[]{:S(2)}) %collective-permute-start.2) | collective-permute-done | bytes 663584 | tf_op jit(solution)/shard_map/ppermute | solution.py:601
  19.4 4.3 %all-to-all-done = bf16[16,2,40,128]{3,2,1,0:T(8,128)(2,1)S(1)} async-done(((bf16[16,2,40,128]{3,2,1,0:T(8,128)(2,1)}), bf16[16,2,40,128]{3,2,1,0:T(8,128)(2,1)S(1)}, u32[]{:S(2)}, u32[]{:S(2)}) %all-to-all-start) | async-done | bytes 327712 | tf_op jit(solution)/shard_map/all_to_all | solution.py:608
  23.8 0.6 collective-permute-start.11
  24.4 1.5 %collective-permute-start.5 = (bf16[8,2,40,128]{3,2,1,0:T(8,128)(2,1)S(1)}, bf16[8,2,40,128]{3,2,1,0:T(8,128)(2,1)S(1)}, u32[]{:S(2)}, u32[]{:S(2)}) collective-permute-start(bf16[8,2,40,128]{3,2,1,0:T(8,128)(2,1)S(1)} %get-tuple-element.74.received_ref.mine_ref), channel_id=1, source_target_pairs={{0,2},{2,0},{1,3},{3,1},{4,6},{6,4},{5,7},{7,5},{8,10},{10,8},{9,1... | collective-permute-start | bytes 491528 | tf_op jit(solution)/shard_map/ppermute | solution.py:622
  25.9 4.6 %prepare.1 = (f32[2,64,1152]{2,1,0:T(8,128)S(1)}, f32[3,64,1152]{2,1,0:T(8,128)S(1)}, f32[1,64,1152]{2,1,0:T(8,128)S(1)}, f32[64,128]{1,0:T(8,128)S(1)}, f32[128...) custom-call(s32[1]{0:T(128)} %bitcast.place_ref, ...), custom_call_target="tpu_custom_call" | custom-call | bytes 16500000 | tf_op jit(solution)/shard_map/prepare/pallas_call | solution.py:220
  30.9 2.8 %attention.6 = (bf16[128,1152]{1,0:T(8,128)(2,1)S(1)}, bf16[576,128]{1,0:T(8,128)(2,1)S(1)}, f32[2,1152]{1,0:T(2,128)S(1)}) custom-call(bf16[8,2,40,128]{3,2,1,0:T(8,128)(2,1)S(1)} %get-tuple-element.73.mine_ref, bf16[8,2,40,128]{3,2,1,0:T(8,128)(2,1)S(1)} %collective-permute-done.11.other_ref, f32[8,128]{1,0:T(8,128)S(1)} %get-tuple-element.44.flag_ref, ...), custom_call_target="tpu_custom_call" | custom-call | tf_op jit(solution)/shard_map/attention/pallas_call | solution.py:366
  33.7 0.6 collective-permute-start.12
  34.3 2.8 %attention.4 = (bf16[128,1152]{1,0:T(8,128)(2,1)S(1)}, bf16[576,128]{1,0:T(8,128)(2,1)S(1)}, f32[2,1152]{1,0:T(2,128)S(1)}) custom-call(bf16[8,2,40,128]{3,2,1,0:T(8,128)(2,1)S(1)} %get-tuple-element.74.received_ref.mine_ref, bf16[8,2,40,128]{3,2,1,0:T(8,128)(2,1)S(1)} %collective-permute-done.5.other_ref, f32[8,128]{1,0:T(8,128)S(1)} %get-tuple-element.44.flag_ref, ...), custom_call_target="tpu_custom_call" | custom-call | tf_op jit(solution)/shard_map/attention/pallas_call | solution.py:366
  37.1 1.6 %collective-permute-start.6 = (bf16[576,128]{1,0:T(8,128)(2,1)S(1)}, bf16[576,128]{1,0:T(8,128)(2,1)S(1)}, u32[]{:S(2)}, u32[]{:S(2)}) collective-permute-start(bf16[576,128]{1,0:T(8,128)(2,1)S(1)} %get-tuple-element.51.mine_ref), channel_id=1, source_target_pairs={{0,2},{2,0},{1,3},{3,1},{4,6},{6,4},{5,7},{7,5},{8,10},{10,8},{9,1... | collective-permute-start | bytes 442376 | tf_op jit(solution)/shard_map/ppermute | solution.py:649
  39.1 2.9 %feed.6 = (bf16[128,1152]{1,0:T(8,128)(2,1)S(1)}, bf16[128,1152]{1,0:T(8,128)(2,1)S(1)}) custom-call(f32[8,128]{1,0:T(8,128)S(1)} %get-tuple-element.44.flag_ref, bf16[128,1152]{1,0:T(8,128)(2,1)S(1)} %get-tuple-element.63.cur_ref.old_ref, bf16[576,128]{1,0:T(8,128)(2,1)S(1)} %get-tuple-element.64.mine_ref, ...), custom_call_target="tpu_custom_call" | custom-call | tf_op jit(solution)/shard_map/feed/pallas_call | solution.py:463
  42.4 2.9 %feed.4 = (bf16[128,1152]{1,0:T(8,128)(2,1)S(1)}, bf16[128,1152]{1,0:T(8,128)(2,1)S(1)}) custom-call(f32[8,128]{1,0:T(8,128)S(1)} %get-tuple-element.44.flag_ref, bf16[128,1152]{1,0:T(8,128)(2,1)S(1)} %get-tuple-element.50.cur_ref.old_ref, bf16[576,128]{1,0:T(8,128)(2,1)S(1)} %get-tuple-element.51.mine_ref, ...), custom_call_target="tpu_custom_call" | custom-call | tf_op jit(solution)/shard_map/feed/pallas_call | solution.py:463
  45.2 1.9 %collective-permute-start.8 = (bf16[128,1152]{1,0:T(8,128)(2,1)S(1)}, bf16[128,1152]{1,0:T(8,128)(2,1)S(1)}, u32[]{:S(2)}, u32[]{:S(2)}) collective-permute-start(bf16[128,1152]{1,0:T(8,128)(2,1)S(1)} %get-tuple-element.56.mine_ref), channel_id=1, source_target_pairs={{0,2},{2,0},{1,3},{3,1},{4,6},{6,4},{5,7},{7,5},{8,10},{10,8},{9,1... | collective-permute-start | bytes 884744 | tf_op jit(solution)/shard_map/ppermute | solution.py:654
  47.1 4.9 %collective-permute-done.13.other_ref = bf16[128,1152]{1,0:T(8,128)(2,1)S(1)} collective-permute-done((bf16[128,1152]{1,0:T(8,128)(2,1)S(1)}, bf16[128,1152]{1,0:T(8,128)(2,1)S(1)}, u32[]{:S(2)}, u32[]{:S(2)}) %collective-permute-start.13) | collective-permute-done | bytes 294944 | tf_op jit(solution)/shard_map/ppermute | solution.py:654
  52.0 3.1 %attention.7 = (bf16[128,1152]{1,0:T(8,128)(2,1)S(1)}, bf16[576,128]{1,0:T(8,128)(2,1)S(1)}) custom-call(bf16[128,1152]{1,0:T(8,128)(2,1)S(1)} %get-tuple-element.63.cur_ref.old_ref, bf16[128,1152]{1,0:T(8,128)(2,1)S(1)} %get-tuple-element.65.after_ref, bf16[128,1152]{1,0:T(8,128)(2,1)S(1)} %get-tuple-element.66.mine_ref, ...), custom_call_target="tpu_custom_call" | custom-call | tf_op jit(solution)/shard_map/attention/pallas_call | solution.py:366
  55.4 1.7 %collective-permute-done.8.other_ref = bf16[128,1152]{1,0:T(8,128)(2,1)S(1)} collective-permute-done((bf16[128,1152]{1,0:T(8,128)(2,1)S(1)}, bf16[128,1152]{1,0:T(8,128)(2,1)S(1)}, u32[]{:S(2)}, u32[]{:S(2)}) %collective-permute-start.8) | collective-permute-done | bytes 294944 | tf_op jit(solution)/shard_map/ppermute | solution.py:654
  57.1 2.9 %attention.5 = (bf16[128,1152]{1,0:T(8,128)(2,1)S(1)}, bf16[576,128]{1,0:T(8,128)(2,1)S(1)}) custom-call(bf16[128,1152]{1,0:T(8,128)(2,1)S(1)} %get-tuple-element.50.cur_ref.old_ref, bf16[128,1152]{1,0:T(8,128)(2,1)S(1)} %get-tuple-element.55.after_ref, bf16[128,1152]{1,0:T(8,128)(2,1)S(1)} %get-tuple-element.56.mine_ref, ...), custom_call_target="tpu_custom_call" | custom-call | tf_op jit(solution)/shard_map/attention/pallas_call | solution.py:366
  60.0 0.9 %collective-permute-start.9 = (bf16[576,128]{1,0:T(8,128)(2,1)S(1)}, bf16[576,128]{1,0:T(8,128)(2,1)S(1)}, u32[]{:S(2)}, u32[]{:S(2)}) collective-permute-start(bf16[576,128]{1,0:T(8,128)(2,1)S(1)} %get-tuple-element.59.mine_ref), channel_id=1, source_target_pairs={{0,2},{2,0},{1,3},{3,1},{4,6},{6,4},{5,7},{7,5},{8,10},{10,8},{9,1... | collective-permute-start | bytes 442376 | tf_op jit(solution)/shard_map/ppermute | solution.py:662
  60.9 0.5 collective-permute-done.14.other_ref
  61.5 2.9 %feed.7 = (bf16[128,1152]{1,0:T(8,128)(2,1)S(1)}, bf16[576,128]{1,0:T(8,128)(2,1)S(1)}, bf16[576,128]{1,0:T(8,128)(2,1)S(1)}) custom-call(f32[8,128]{1,0:T(8,128)S(1)} %get-tuple-element.44.flag_ref, bf16[128,1152]{1,0:T(8,128)(2,1)S(1)} %get-tuple-element.68.cur_ref.refs_4_, bf16[576,128]{1,0:T(8,128)(2,1)S(1)} %get-tuple-element.69.mine_ref, ...), custom_call_target="tpu_custom_call" | custom-call | tf_op jit(solution)/shard_map/feed/pallas_call | solution.py:463
  64.4 0.6 collective-permute-start.15
  65.0 0.7 collective-permute-done.9.other_ref
  65.7 2.9 %feed.5 = (bf16[128,1152]{1,0:T(8,128)(2,1)S(1)}, bf16[576,128]{1,0:T(8,128)(2,1)S(1)}, bf16[576,128]{1,0:T(8,128)(2,1)S(1)}) custom-call(f32[8,128]{1,0:T(8,128)S(1)} %get-tuple-element.44.flag_ref, bf16[128,1152]{1,0:T(8,128)(2,1)S(1)} %get-tuple-element.58.cur_ref.refs_0_, bf16[576,128]{1,0:T(8,128)(2,1)S(1)} %get-tuple-element.59.mine_ref, ...), custom_call_target="tpu_custom_call" | custom-call | tf_op jit(solution)/shard_map/feed/pallas_call | solution.py:463
  68.6 0.8 collective-permute-start.10
  69.4 0.6 collective-permute-done.15.refs_7_
  70.0 3.7 %collective-permute-done.10.refs_3_ = bf16[576,128]{1,0:T(8,128)(2,1)S(1)} collective-permute-done((bf16[576,128]{1,0:T(8,128)(2,1)S(1)}, bf16[576,128]{1,0:T(8,128)(2,1)S(1)}, u32[]{:S(2)}, u32[]{:S(2)}) %collective-permute-start.10) | collective-permute-done | bytes 147488 | tf_op jit(solution)/shard_map/ppermute | solution.py:668
  73.8 0.7 finish.1
  74.4 13.8 %all_to_all.10.rows_ref = bf16[16,72,128]{2,1,0:T(8,128)(2,1)S(1)} all-to-all(bf16[16,72,128]{2,1,0:T(8,128)(2,1)S(1)} %bitcast.17), channel_id=1, replica_groups=mesh['frame'=8,'y'=2,'core'=2] {'frame','core'}, dimensions={0} | all-to-all | bytes 589824 | tf_op jit(solution)/shard_map/all_to_all | solution.py:672
  88.2 0.9 %unpack.1 = bf16[8,64,288]{2,1,0:T(8,128)(2,1)} custom-call(bf16[16,72,128]{2,1,0:T(8,128)(2,1)S(1)} %all_to_all.10.rows_ref), custom_call_target="tpu_custom_call" | custom-call | bytes 2970000 | tf_op jit(solution)/shard_map/unpack/pallas_call | solution.py:563
  (29 shorter events, 2.8 us)
Async XLA Ops:
  0.0 25.9 %copy-start.4 = (f32[64]{0:T(128)S(1)}, f32[64]{0:T(128)}, u32[]{:S(2)}) copy-start(f32[64]{0:T(128)} %param.16) | copy-start | bytes 772
  0.0 25.9 %copy-start.5 = (f32[64]{0:T(128)S(1)}, f32[64]{0:T(128)}, u32[]{:S(2)}) copy-start(f32[64]{0:T(128)} %param.17) | copy-start | bytes 772
  0.0 23.8 %collective-permute-start.3 = (bf16[1152,1152]{1,0:T(8,128)(2,1)}, bf16[1152,1152]{1,0:T(8,128)(2,1)}, u32[]{:S(2)}, u32[]{:S(2)}) collective-permute-start(bf16[1152,1152]{1,0:T(8,128)(2,1)} %fc2_me.7), channel_id=1, source_target_pairs={{0,1},{1,0},{2,3},{3,2},{4,5},{5,4},{6,7},{7,6},{8,9},{9,8},{10,11... | collective-permute-start | bytes 7962632 | tf_op jit(solution)/shard_map/ppermute | solution.py:602
  0.5 38.2 %collective-permute-start.7 = (bf16[1152,1152]{1,0:T(8,128)(2,1)}, bf16[1152,1152]{1,0:T(8,128)(2,1)S(1)}, u32[]{:S(2)}, u32[]{:S(2)}) collective-permute-start(bf16[1152,1152]{1,0:T(8,128)(2,1)} %fc1_me.7), channel_id=1, source_target_pairs={{0,1},{1,0},{2,3},{3,2},{4,5},{5,4},{6,7},{7,6},{8,9},{9,8},{10,11... | collective-permute-start | bytes 7962632 | tf_op jit(solution)/shard_map/ppermute | solution.py:650
  0.5 23.2 %collective-permute-start = (bf16[3,288,1152]{2,1,0:T(8,128)(2,1)}, bf16[3,288,1152]{2,1,0:T(8,128)(2,1)}, u32[]{:S(2)}, u32[]{:S(2)}) collective-permute-start(bf16[3,288,1152]{2,1,0:T(8,128)(2,1)} %bitcast.12), channel_id=1, source_target_pairs={{0,1},{1,0},{2,3},{3,2},{4,5},{5,4},{6,7},{7,6},{8,9},{9,8},{10,11... | collective-permute-start | bytes 5971976 | tf_op jit(solution)/shard_map/ppermute | solution.py:600
  1.0 18.4 %collective-permute-start.2 = (bf16[288,1152]{1,0:T(8,128)(2,1)}, bf16[288,1152]{1,0:T(8,128)(2,1)}, u32[]{:S(2)}, u32[]{:S(2)}) collective-permute-start(bf16[288,1152]{1,0:T(8,128)(2,1)} %refs_3_.1), channel_id=1, source_target_pairs={{0,2},{2,0},{1,3},{3,1},{4,6},{6,4},{5,7},{7,5},{8,10},{10,8},{9,1... | collective-permute-start | bytes 1990664 | tf_op jit(solution)/shard_map/ppermute | solution.py:601
  3.6 20.2 %collective-permute-start.1 = (bf16[288,1152]{1,0:T(8,128)(2,1)}, bf16[288,1152]{1,0:T(8,128)(2,1)}, u32[]{:S(2)}, u32[]{:S(2)}) collective-permute-start(bf16[288,1152]{1,0:T(8,128)(2,1)} %refs_3_.1), channel_id=1, source_target_pairs={{0,1},{1,0},{2,3},{3,2},{4,5},{5,4},{6,7},{7,6},{8,9},{9,8},{10,11... | collective-permute-start | bytes 1990664 | tf_op jit(solution)/shard_map/ppermute | solution.py:602
  3.7 1.0 %copy-start.3 = (bf16[8,64,288]{2,1,0:T(8,128)(2,1)S(1)}, bf16[8,64,288]{2,1,0:T(8,128)(2,1)}, u32[]{:S(2)}) copy-start(bf16[8,64,288]{2,1,0:T(8,128)(2,1)} %x_ref.1) | copy-start | bytes 884740
  6.7 17.0 %all-to-all-start = ((bf16[16,2,40,128]{3,2,1,0:T(8,128)(2,1)}), bf16[16,2,40,128]{3,2,1,0:T(8,128)(2,1)S(1)}, u32[]{:S(2)}, u32[]{:S(2)}) async-start(bf16[16,2,40,128]{3,2,1,0:T(8,128)(2,1)} %payload.1), calls=%async_computation | async-start | bytes 655360 | tf_op jit(solution)/shard_map/all_to_all | solution.py:608
  19.4 6.5 %collective-permute-start.4 = (bf16[288,1152]{1,0:T(8,128)(2,1)}, bf16[288,1152]{1,0:T(8,128)(2,1)}, u32[]{:S(2)}, u32[]{:S(2)}) collective-permute-start(bf16[288,1152]{1,0:T(8,128)(2,1)} %collective-permute-done.2.refs_5_.refs_7_), channel_id=1, source_target_pairs={{0,1},{1,0},{2,3},{3,2},{4,5},{5,4},{6,7},{7,6},{8,9},{9,8},{10,11... | collective-permute-start | bytes 1990664 | tf_op jit(solution)/shard_map/ppermute | solution.py:602
  23.8 7.1 %collective-permute-start.11 = (bf16[8,2,40,128]{3,2,1,0:T(8,128)(2,1)S(1)}, bf16[8,2,40,128]{3,2,1,0:T(8,128)(2,1)S(1)}, u32[]{:S(2)}, u32[]{:S(2)}) collective-permute-start(bf16[8,2,40,128]{3,2,1,0:T(8,128)(2,1)S(1)} %get-tuple-element.73.mine_ref), channel_id=1, source_target_pairs={{0,2},{2,0},{1,3},{3,1},{4,6},{6,4},{5,7},{7,5},{8,10},{10,8},{9,1... | collective-permute-start | bytes 491528 | tf_op jit(solution)/shard_map/ppermute | solution.py:622
  24.4 9.9 %collective-permute-start.5 = (bf16[8,2,40,128]{3,2,1,0:T(8,128)(2,1)S(1)}, bf16[8,2,40,128]{3,2,1,0:T(8,128)(2,1)S(1)}, u32[]{:S(2)}, u32[]{:S(2)}) collective-permute-start(bf16[8,2,40,128]{3,2,1,0:T(8,128)(2,1)S(1)} %get-tuple-element.74.received_ref.mine_ref), channel_id=1, source_target_pairs={{0,2},{2,0},{1,3},{3,1},{4,6},{6,4},{5,7},{7,5},{8,10},{10,8},{9,1... | collective-permute-start | bytes 491528 | tf_op jit(solution)/shard_map/ppermute | solution.py:622
  25.9 5.0 %copy-start.2 = (bf16[3,1152,288]{1,2,0:T(8,128)(2,1)S(1)}, bf16[3,1152,288]{1,2,0:T(8,128)(2,1)}, u32[]{:S(2)}) copy-start(bf16[3,1152,288]{1,2,0:T(8,128)(2,1)} %param.18) | copy-start | bytes 5971972
  30.9 8.2 %copy-start.1 = (bf16[1152,1152]{1,0:T(8,128)(2,1)S(1)}, bf16[1152,1152]{1,0:T(8,128)(2,1)}, u32[]{:S(2)}) copy-start(bf16[1152,1152]{1,0:T(8,128)(2,1)} %fc1_me.7) | copy-start | bytes 7962628
  33.7 5.4 %copy-start = (bf16[1152,1152]{1,0:T(8,128)(2,1)S(1)}, bf16[1152,1152]{1,0:T(8,128)(2,1)}, u32[]{:S(2)}) copy-start(bf16[1152,1152]{1,0:T(8,128)(2,1)} %fc2_me.7) | copy-start | bytes 7962628
  33.7 5.4 %collective-permute-start.12 = (bf16[576,128]{1,0:T(8,128)(2,1)S(1)}, bf16[576,128]{1,0:T(8,128)(2,1)S(1)}, u32[]{:S(2)}, u32[]{:S(2)}) collective-permute-start(bf16[576,128]{1,0:T(8,128)(2,1)S(1)} %get-tuple-element.64.mine_ref), channel_id=1, source_target_pairs={{0,2},{2,0},{1,3},{3,1},{4,6},{6,4},{5,7},{7,5},{8,10},{10,8},{9,1... | collective-permute-start | bytes 442376 | tf_op jit(solution)/shard_map/ppermute | solution.py:649
  37.1 5.3 %collective-permute-start.6 = (bf16[576,128]{1,0:T(8,128)(2,1)S(1)}, bf16[576,128]{1,0:T(8,128)(2,1)S(1)}, u32[]{:S(2)}, u32[]{:S(2)}) collective-permute-start(bf16[576,128]{1,0:T(8,128)(2,1)S(1)} %get-tuple-element.51.mine_ref), channel_id=1, source_target_pairs={{0,2},{2,0},{1,3},{3,1},{4,6},{6,4},{5,7},{7,5},{8,10},{10,8},{9,1... | collective-permute-start | bytes 442376 | tf_op jit(solution)/shard_map/ppermute | solution.py:649
  42.0 10.0 %collective-permute-start.13 = (bf16[128,1152]{1,0:T(8,128)(2,1)S(1)}, bf16[128,1152]{1,0:T(8,128)(2,1)S(1)}, u32[]{:S(2)}, u32[]{:S(2)}) collective-permute-start(bf16[128,1152]{1,0:T(8,128)(2,1)S(1)} %get-tuple-element.66.mine_ref), channel_id=1, source_target_pairs={{0,2},{2,0},{1,3},{3,1},{4,6},{6,4},{5,7},{7,5},{8,10},{10,8},{9,1... | collective-permute-start | bytes 884744 | tf_op jit(solution)/shard_map/ppermute | solution.py:654
  45.2 11.8 %collective-permute-start.8 = (bf16[128,1152]{1,0:T(8,128)(2,1)S(1)}, bf16[128,1152]{1,0:T(8,128)(2,1)S(1)}, u32[]{:S(2)}, u32[]{:S(2)}) collective-permute-start(bf16[128,1152]{1,0:T(8,128)(2,1)S(1)} %get-tuple-element.56.mine_ref), channel_id=1, source_target_pairs={{0,2},{2,0},{1,3},{3,1},{4,6},{6,4},{5,7},{7,5},{8,10},{10,8},{9,1... | collective-permute-start | bytes 884744 | tf_op jit(solution)/shard_map/ppermute | solution.py:654
  55.1 6.4 %collective-permute-start.14 = (bf16[576,128]{1,0:T(8,128)(2,1)S(1)}, bf16[576,128]{1,0:T(8,128)(2,1)S(1)}, u32[]{:S(2)}, u32[]{:S(2)}) collective-permute-start(bf16[576,128]{1,0:T(8,128)(2,1)S(1)} %get-tuple-element.69.mine_ref), channel_id=1, source_target_pairs={{0,2},{2,0},{1,3},{3,1},{4,6},{6,4},{5,7},{7,5},{8,10},{10,8},{9,1... | collective-permute-start | bytes 442376 | tf_op jit(solution)/shard_map/ppermute | solution.py:662
  60.0 5.7 %collective-permute-start.9 = (bf16[576,128]{1,0:T(8,128)(2,1)S(1)}, bf16[576,128]{1,0:T(8,128)(2,1)S(1)}, u32[]{:S(2)}, u32[]{:S(2)}) collective-permute-start(bf16[576,128]{1,0:T(8,128)(2,1)S(1)} %get-tuple-element.59.mine_ref), channel_id=1, source_target_pairs={{0,2},{2,0},{1,3},{3,1},{4,6},{6,4},{5,7},{7,5},{8,10},{10,8},{9,1... | collective-permute-start | bytes 442376 | tf_op jit(solution)/shard_map/ppermute | solution.py:662
  64.4 5.7 %collective-permute-start.15 = (bf16[576,128]{1,0:T(8,128)(2,1)S(1)}, bf16[576,128]{1,0:T(8,128)(2,1)S(1)}, u32[]{:S(2)}, u32[]{:S(2)}) collective-permute-start(bf16[576,128]{1,0:T(8,128)(2,1)S(1)} %get-tuple-element.72), channel_id=1, source_target_pairs={{0,2},{2,0},{1,3},{3,1},{4,6},{6,4},{5,7},{7,5},{8,10},{10,8},{9,1... | collective-permute-start | bytes 442376 | tf_op jit(solution)/shard_map/ppermute | solution.py:668
  68.6 5.2 %collective-permute-start.10 = (bf16[576,128]{1,0:T(8,128)(2,1)S(1)}, bf16[576,128]{1,0:T(8,128)(2,1)S(1)}, u32[]{:S(2)}, u32[]{:S(2)}) collective-permute-start(bf16[576,128]{1,0:T(8,128)(2,1)S(1)} %get-tuple-element.62), channel_id=1, source_target_pairs={{0,2},{2,0},{1,3},{3,1},{4,6},{6,4},{5,7},{7,5},{8,10},{10,8},{9,1... | collective-permute-start | bytes 442376 | tf_op jit(solution)/shard_map/ppermute | solution.py:668
